TPU v7x, 32 devices: a whole 2x2x4 slice. The times are simulated.
32 devices in a mesh: fsdp: 8 (over z, core), seq: 4 (over y, x).
Axes of the slice: x: 2, y: 2, z: 4, core: 2. Of those that a mesh axis runs over, the one named last changes fastest.
Arguments:
- inputs: bfloat16 [16, 1024, 1152], P('fsdp', 'seq'), may hold values from -24 to 24
- key_mask: int32 [16, 1024], P('fsdp'), may hold values from 0 to 1, as said below
- w_qkv: bfloat16 [1152, 3456], P('fsdp'), may hold values from -1 to 1
- w_out: bfloat16 [1152, 1152], P('fsdp'), may hold values from -2 to 2
- w_up: bfloat16 [1152, 4304], P('fsdp'), may hold values from -0.1875 to 0.1875
- w_down: bfloat16 [4304, 1152], P(None, 'fsdp'), may hold values from -0.09375 to 0.09375
- norm_gains: bfloat16 [2, 1152], P(None, 'fsdp'), may hold values from 0.099609375 to 1.8984375
- biases: bfloat16 [6, 1152], P(None, 'fsdp'), may hold values from -3 to 3
- up_bias: bfloat16 [4304], P('fsdp'), may hold values from -3 to 3
- cotangent: bfloat16 [16, 1024, 1152], P('fsdp', 'seq'), may hold values from -6 to 6
Outputs:
- layer_out: bfloat16 [16, 1024, 1152], P('fsdp', 'seq')
- grad_in: bfloat16 [16, 1024, 1152], P('fsdp', 'seq')
- grad_qkv: float32 [1152, 3456], P('fsdp')
- grad_proj: float32 [1152, 1152], P('fsdp')
- grad_up: float32 [1152, 4304], P('fsdp')
- grad_down: float32 [4304, 1152], P(None, 'fsdp')
- grad_gains: float32 [2, 1152], P(None, 'fsdp')
- grad_biases: float32 [6, 1152], P(None, 'fsdp')
- grad_upbias: float32 [4304], P('fsdp')
Inputs may be any that keep to these rules, and one draw needn't show every extreme that they name: `key_mask`: in each image the live keys are its first L tokens, with L between 512 and 1024; image 0 has L = 512.
All inputs are finite; a program needn't handle non-finite values.
Results may differ from a plain program's by a relative error of at most 0.012.
Values may be sent and summed in bfloat16 or wider, within the bound.
No kernel may reach another device: no remote copies, remote signals or barrier semaphores. Data moves between devices by JAX's collectives and lax.ppermute only.
A program may use at most 256 MiB of HBM per device.

v0:
```python
import math

import jax
import jax.numpy as jnp
from jax import lax
from jax.sharding import PartitionSpec as P

HEAD_DIM = 72
QBLOCK = 512


EPSILON = 1e-06
NEG_FILL = -1e30
GELU_CUBE = 0.044715
GELU_SCALE = math.sqrt(2.0 / math.pi)


def for_sending(array):
    return jax.tree.map(lambda a: a.astype(jnp.bfloat16) if a.dtype == jnp.float32 else a, array)


def layer_norm(values, gain_row, shift_row):
    row_mean = jnp.mean(values, axis=-1, keepdims=True)
    centred = values - row_mean
    variance = jnp.mean(centred * centred, axis=-1, keepdims=True)
    inv_std = lax.rsqrt(variance + EPSILON)
    normed = centred * inv_std
    return (normed * gain_row + shift_row, normed, inv_std)


def norm_back(upstream, normed, inv_std, gain_row):
    scaled = upstream * gain_row
    first_mean = jnp.mean(scaled, axis=-1, keepdims=True)
    second_mean = jnp.mean(scaled * normed, axis=-1, keepdims=True)
    return inv_std * (scaled - first_mean - normed * second_mean)


def gelu_tanh(values):
    return (
        0.5
        * values
        * (1.0 + jnp.tanh(GELU_SCALE * (values + GELU_CUBE * values * values * values)))
    )


def gelu_slope(values):
    tangent = jnp.tanh(GELU_SCALE * (values + GELU_CUBE * values * values * values))
    return 0.5 * (1.0 + tangent) + 0.5 * values * (1.0 - tangent * tangent) * GELU_SCALE * (
        1.0 + 3.0 * GELU_CUBE * values * values
    )


def block_scores(q_block, keys_full, live, score_scale):
    scores = (
        jnp.einsum("qhd,khd->hqk", q_block, keys_full, preferred_element_type=jnp.float32)
        * score_scale
    )
    return jnp.where(live[None, None, :] > 0, scores, NEG_FILL)


def forward_image(pieces, block_rows, score_scale):
    query, keys_full, values_full, live = pieces
    out_parts = []
    total_parts = []
    for start in range(0, query.shape[0], block_rows):
        masked = block_scores(query[start : start + block_rows], keys_full, live, score_scale)
        top_score = jnp.max(masked, axis=-1, keepdims=True)
        log_total = top_score + jnp.log(
            jnp.sum(jnp.exp(masked - top_score), axis=-1, keepdims=True)
        )
        probs_low = jnp.exp(masked - log_total).astype(jnp.bfloat16)
        out_parts.append(
            jnp.einsum(
                "hqk,khd->qhd", probs_low, values_full, preferred_element_type=jnp.float32
            ).astype(jnp.bfloat16)
        )
        total_parts.append(log_total)
    return (jnp.concatenate(out_parts, axis=0), jnp.concatenate(total_parts, axis=1))


def backward_image(pieces, block_rows, score_scale):
    query, keys_full, values_full, live, log_totals, d_heads = pieces
    dq_parts = []
    dk_total = jnp.zeros(keys_full.shape, jnp.float32)
    dv_total = jnp.zeros(values_full.shape, jnp.float32)
    for start in range(0, query.shape[0], block_rows):
        q_block = query[start : start + block_rows]
        d_block = d_heads[start : start + block_rows]
        masked = block_scores(q_block, keys_full, live, score_scale)
        probs = jnp.exp(masked - log_totals[:, start : start + block_rows])
        probs_low = probs.astype(jnp.bfloat16)
        d_probs = jnp.einsum(
            "qhd,khd->hqk", d_block, values_full, preferred_element_type=jnp.float32
        )
        row_dot = jnp.sum(probs * d_probs, axis=-1, keepdims=True)
        d_scores = (probs * (d_probs - row_dot)).astype(jnp.bfloat16)
        dq_block = (
            jnp.einsum("hqk,khd->qhd", d_scores, keys_full, preferred_element_type=jnp.float32)
            * score_scale
        )
        dq_parts.append(dq_block.astype(jnp.bfloat16))
        dk_total = dk_total + jnp.einsum(
            "hqk,qhd->khd", d_scores, q_block, preferred_element_type=jnp.float32
        )
        dv_total = dv_total + jnp.einsum(
            "hqk,qhd->khd", probs_low, d_block, preferred_element_type=jnp.float32
        )
    return (
        jnp.concatenate(dq_parts, axis=0),
        (dk_total * score_scale).astype(jnp.bfloat16),
        dv_total.astype(jnp.bfloat16),
    )


def on_device(inputs, key_mask, w_qkv, w_out, w_up, w_down, norm_gains, biases, up_bias, cotangent):
    img_count, tok_count, width = inputs.shape
    seq_len = key_mask.shape[1]
    row_count = img_count * tok_count
    head_cols = width // lax.axis_size("seq")
    local_heads = head_cols // HEAD_DIM
    block_rows = min(QBLOCK, seq_len)
    score_scale = 1.0 / math.sqrt(HEAD_DIM)
    gathered = (
        lax.all_gather(w_qkv, "fsdp", axis=0, tiled=True),
        lax.all_gather(w_out, "fsdp", axis=0, tiled=True),
        lax.all_gather(w_up, "fsdp", axis=0, tiled=True),
        lax.all_gather(w_down, "fsdp", axis=1, tiled=True),
        lax.all_gather(norm_gains, "fsdp", axis=1, tiled=True),
        lax.all_gather(biases, "fsdp", axis=1, tiled=True),
        lax.all_gather(up_bias, "fsdp", axis=0, tiled=True),
    )
    full_qkv, full_out, full_up, full_down, full_gains, full_biases, full_upbias = gathered
    gain_rows = full_gains.astype(jnp.float32)
    bias_rows = full_biases.astype(jnp.float32)
    up_shift = full_upbias.astype(jnp.float32)
    qkv_shift = jnp.concatenate([bias_rows[2], jnp.zeros((width,), jnp.float32), bias_rows[3]])
    tok_wide = inputs.reshape(row_count, width).astype(jnp.float32)
    first_out, first_normed, first_inv = layer_norm(tok_wide, gain_rows[0], bias_rows[0])
    first_low = first_out.astype(jnp.bfloat16)
    packed = (jnp.dot(first_low, full_qkv, preferred_element_type=jnp.float32) + qkv_shift).astype(
        jnp.bfloat16
    )
    by_heads = lax.all_to_all(
        packed.reshape(img_count, tok_count, 3, width),
        "seq",
        split_axis=3,
        concat_axis=1,
        tiled=True,
    )
    query = by_heads[:, :, 0].reshape(img_count, seq_len, local_heads, HEAD_DIM)
    keys_full = by_heads[:, :, 1].reshape(img_count, seq_len, local_heads, HEAD_DIM)
    values_full = by_heads[:, :, 2].reshape(img_count, seq_len, local_heads, HEAD_DIM)

    def run_forward(pieces):
        return forward_image(pieces, block_rows, score_scale)

    attended_heads, log_totals = lax.map(run_forward, (query, keys_full, values_full, key_mask))
    attended = lax.all_to_all(
        for_sending(attended_heads.reshape(img_count, seq_len, head_cols)),
        "seq",
        split_axis=1,
        concat_axis=2,
        tiled=True,
    ).reshape(row_count, width)
    residual = (
        tok_wide + jnp.dot(attended, full_out, preferred_element_type=jnp.float32) + bias_rows[4]
    )
    second_out, second_normed, second_inv = layer_norm(residual, gain_rows[1], bias_rows[1])
    second_low = second_out.astype(jnp.bfloat16)
    upper = jnp.dot(second_low, full_up, preferred_element_type=jnp.float32) + up_shift
    active = gelu_tanh(upper).astype(jnp.bfloat16)
    layer_out = (
        residual + jnp.dot(active, full_down, preferred_element_type=jnp.float32) + bias_rows[5]
    ).astype(jnp.bfloat16)
    back_qkv, back_out, back_up, back_down, back_gains, back_biases, back_upbias = gathered
    back_gain_rows = back_gains.astype(jnp.float32)
    upstream = cotangent.reshape(row_count, width)
    grad_wide = upstream.astype(jnp.float32)
    d_active = jnp.dot(upstream, back_down.T, preferred_element_type=jnp.float32)
    dw_down = jnp.dot(active.T, upstream, preferred_element_type=jnp.float32)
    d_upper = (d_active * gelu_slope(upper)).astype(jnp.bfloat16)
    dw_up = jnp.dot(second_low.T, d_upper, preferred_element_type=jnp.float32)
    d_second = jnp.dot(d_upper, back_up.T, preferred_element_type=jnp.float32)
    d_resid = grad_wide + norm_back(d_second, second_normed, second_inv, back_gain_rows[1])
    d_resid_low = d_resid.astype(jnp.bfloat16)
    dw_out = jnp.dot(attended.T, d_resid_low, preferred_element_type=jnp.float32)
    d_attended = jnp.dot(d_resid_low, back_out.T, preferred_element_type=jnp.float32).astype(
        jnp.bfloat16
    )
    d_heads = lax.all_to_all(
        d_attended.reshape(img_count, tok_count, width),
        "seq",
        split_axis=2,
        concat_axis=1,
        tiled=True,
    ).reshape(img_count, seq_len, local_heads, HEAD_DIM)

    def run_backward(pieces):
        return backward_image(pieces, block_rows, score_scale)

    dq_heads, dk_heads, dv_heads = lax.map(
        run_backward, (query, keys_full, values_full, key_mask, log_totals, d_heads)
    )
    stacked = jnp.stack(
        [
            dq_heads.reshape(img_count, seq_len, head_cols),
            dk_heads.reshape(img_count, seq_len, head_cols),
            dv_heads.reshape(img_count, seq_len, head_cols),
        ],
        axis=2,
    )
    d_packed = (
        lax.all_to_all(for_sending(stacked), "seq", split_axis=1, concat_axis=3, tiled=True)
        .astype(stacked.dtype)
        .reshape(row_count, 3 * width)
    )
    d_pack_wide = d_packed.astype(jnp.float32)
    dw_qkv = jnp.dot(first_low.T, d_packed, preferred_element_type=jnp.float32)
    d_first = jnp.dot(d_packed, back_qkv.T, preferred_element_type=jnp.float32)
    grad_in = (d_resid + norm_back(d_first, first_normed, first_inv, back_gain_rows[0])).astype(
        jnp.bfloat16
    )
    d_gains = jnp.stack(
        [jnp.sum(d_first * first_normed, axis=0), jnp.sum(d_second * second_normed, axis=0)]
    )
    d_biases = jnp.stack(
        [
            jnp.sum(d_first, axis=0),
            jnp.sum(d_second, axis=0),
            jnp.sum(d_pack_wide[:, :width], axis=0),
            jnp.sum(d_pack_wide[:, 2 * width :], axis=0),
            jnp.sum(d_resid, axis=0),
            jnp.sum(grad_wide, axis=0),
        ]
    )
    d_upbias = jnp.sum(d_upper.astype(jnp.float32), axis=0)
    owned = (
        lax.psum_scatter(dw_qkv, "fsdp", scatter_dimension=0, tiled=True),
        lax.psum_scatter(dw_out, "fsdp", scatter_dimension=0, tiled=True),
        lax.psum_scatter(dw_up, "fsdp", scatter_dimension=0, tiled=True),
        lax.psum_scatter(dw_down, "fsdp", scatter_dimension=1, tiled=True),
        lax.psum_scatter(d_gains, "fsdp", scatter_dimension=1, tiled=True),
        lax.psum_scatter(d_biases, "fsdp", scatter_dimension=1, tiled=True),
        lax.psum_scatter(d_upbias, "fsdp", scatter_dimension=0, tiled=True),
    )
    summed = lax.psum((owned[0], owned[1], owned[2], owned[3], owned[4], owned[5], owned[6]), "seq")
    grad_qkv, grad_proj, grad_up, grad_down, grad_gains, grad_biases, grad_upbias = summed
    return (
        layer_out.reshape(img_count, tok_count, width),
        grad_in.reshape(img_count, tok_count, width),
        grad_qkv,
        grad_proj,
        grad_up,
        grad_down,
        grad_gains,
        grad_biases,
        grad_upbias,
    )


def solution(mesh):
    return jax.shard_map(
        on_device,
        mesh=mesh,
        in_specs=(
            P("fsdp", "seq", None),
            P("fsdp", None),
            P("fsdp", None),
            P("fsdp", None),
            P("fsdp", None),
            P(None, "fsdp"),
            P(None, "fsdp"),
            P(None, "fsdp"),
            P("fsdp"),
            P("fsdp", "seq", None),
        ),
        out_specs=(
            P("fsdp", "seq", None),
            P("fsdp", "seq", None),
            P("fsdp", None),
            P("fsdp", None),
            P("fsdp", None),
            P(None, "fsdp"),
            P(None, "fsdp"),
            P(None, "fsdp"),
            P("fsdp"),
        ),
        check_vma=False,
    )
```

profile of v0, /device:TPU:0, one launch (start us, length us, event | category | flops | bytes accessed | tf_op | source)
XLA Modules:
  0.0 1370.6 jit_solution(5586630229671598762)
XLA Ops:
  10.0 15.7 %all-gather.1 = bf16[8,144,6]{1,2,0:T(8,128)(2,1)S(1)} all-gather(bf16[1,144,6]{1,2,0:T(8,128)(2,1)S(1)} %bitcast.312), channel_id=1, replica_groups=mesh['fsdp'=8,'seq'=4] {'fsdp'}, dimensions={0}, use_global_device_ids=true | all-gather | bytes 15552 | tf_op jit(solution)/shard_map/all_gather | solution.py:129
  25.8 11.9 all-gather
  41.9 49.1 %all-gather.7.cloned.1.call-done = bf16[1152,3456]{1,0:T(8,128)(2,1)} async-done(((bf16[144,3456]{1,0:T(8,128)(2,1)}), bf16[1152,3456]{1,0:T(8,128)(2,1)}) %all-gather.7.cloned.1.call-update) | async-done | bytes 7962640 | tf_op jit(solution)/shard_map/all_gather | solution.py:124
  91.0 8.4 add_convert_fusion
  99.4 4.0 reshape.221
  103.5 12.9 copy.88
  116.4 4.0 all-to-all-start
  120.4 41.0 %all-to-all-done = bf16[2,256,3,1152]{1,0,2,3:T(2,128)(2,1)S(1)} async-done(((bf16[2,256,3,1152]{1,0,2,3:T(2,128)(2,1)}), bf16[2,256,3,1152]{1,0,2,3:T(2,128)(2,1)S(1)}, u32[]{:S(2)}, u32[]{:S(2)}) %all-to-all-start) | async-done | bytes 3538976 | tf_op jit(solution)/shard_map/all_to_all | solution.py:143
  164.9 36.7 %while.26 = (s32[]{:T(128)}, bf16[2,1024,4,72]{1,3,2,0:T(8,128)(2,1)}, f32[2,4,1024,1]{2,1,3,0:T(4,128)S(1)}, bf16[2,1024,4,72]{1,3,2,0:T(8,128)(2,1)}, s32[2,10...) while((s32[]{:T(128)}, ...), condition=%wide.region_7.8_spmd, body=%wide.region_2.7_spmd.sunk | while | flops 1255572480 | bytes 94532360 | solution.py:157
  165.0 4.8 fusion.165
  169.7 5.9 exponential_reduce_fusion.4
  175.6 2.1 exponential_reduce_fusion.5
  177.8 2.1 fusion.166
  183.3 4.8 fusion.165
  188.0 6.0 exponential_reduce_fusion.4
  196.2 2.1 fusion.166
  201.7 4.8 copy.91
  206.4 4.4 all-to-all-start.1
  212.4 26.9 %all-reduce = bf16[4304]{0:T(1024)(128)(2,1)S(1)} all-reduce(bf16[4304]{0:T(1024)(128)(2,1)S(1)} %dynamic-update-slice), channel_id=1, replica_groups=mesh['fsdp'=8,'seq'=4] {'fsdp'}, use_global_device_ids=true, to_apply=%add | all-reduce | flops 4304 | bytes 17216
  239.4 5.1 copy.102
  244.5 2.5 copy.93
  248.3 4.6 fusion.111
  254.7 12.4 convolution_add_fusion.1
  267.1 50.2 %all-gather.13.cloned.1.call-done = bf16[4304,1152]{0,1:T(8,128)(2,1)} async-done(((bf16[4304,144]{0,1:T(8,128)(2,1)}), bf16[4304,1152]{0,1:T(8,128)(2,1)}) %all-gather.13.cloned.1.call-update) | async-done | bytes 9916432 | tf_op jit(solution)/shard_map/all_gather | solution.py:127
  317.3 16.8 %convert_reduce_fusion = (f32[4304]{0:T(1024)}, bf16[512,4304]{0,1:T(8,128)(2,1)S(1)}) fusion(f32[512,4304]{0,1:T(8,128)} %convolution_add_fusion.1, bf16[512,1152]{1,0:T(8,128)(2,1)} %bitcast.286, bf16[4304,1152]{0,1:T(8,128)(2,1)} %all-gather.13.cloned.1.call-done), kind=kOutput, calls=%fused_computation.120 | convolution fusion | flops 5123477504 | bytes 24335168 | tf_op jit(solution)/shard_map/dot_general | solution.py:179
  334.1 12.7 multiply_reduce_fusion.2
  348.5 2.9 convolution_convert_fusion
  351.4 4.2 copy.94
  355.6 4.3 all-to-all-start.2
  359.9 6.0 fusion.101
  366.0 9.7 all-to-all-done.2
  379.0 3.4 reshape.206
  386.0 84.1 %while.27 = (s32[]{:T(128)}, bf16[2,1024,4,72]{1,3,2,0:T(8,128)(2,1)}, bf16[2,1024,4,72]{1,3,2,0:T(8,128)(2,1)}, bf16[2,1024,4,72]{1,3,2,0:T(8,128)(2,1)}, bf16[...) while((s32[]{:T(128)}, ...), condition=%wide.region_15.16_spmd, body=%wide.region_12.15_spmd.sunk | while | flops 3086054400 | bytes 206144400 | solution.py:201
  386.2 4.5 fusion.181
  390.7 5.8 fusion.182
  398.8 9.6 multiply_reduce_fusion.11
  408.4 8.6 multiply_convert_fusion.6
  424.9 2.1 fusion.190
  428.0 4.5 fusion.181
  432.6 5.8 fusion.182
  440.6 9.5 multiply_reduce_fusion.11
  450.2 8.5 multiply_convert_fusion.6
  466.5 2.1 fusion.190
  470.1 2.2 pad_maximum_fusion
  472.3 8.7 copy.97
  480.9 5.1 all-to-all-start.3
  486.7 52.3 %all-to-all-done.3 = bf16[2,1024,3,288]{3,0,2,1:T(2,128)(2,1)} async-done(((bf16[2,1024,3,288]{3,0,2,1:T(2,128)(2,1)}), bf16[2,1024,3,288]{3,0,2,1:T(2,128)(2,1)}, u32[]{:S(2)}, u32[]{:S(2)}) %all-to-all-start.3) | async-done | bytes 3538976 | tf_op jit(solution)/shard_map/all_to_all | solution.py:213
  538.9 13.0 copy.103
  551.9 5.6 copy.99
  560.1 7.9 fusion.112
  569.6 12.4 fusion.106
  582.1 12.9 fusion.107
  599.7 6.1 convert_element_type.137
  605.9 11.0 multiply_reduce_fusion.3
  619.4 2.8 slice_reduce_fusion
  627.3 99.0 %reduce-scatter.11.cloned.1.call-done = f32[144,3456]{1,0:T(8,128)} async-done(((f32[1152,3456]{1,0:T(8,128)}), f32[144,3456]{1,0:T(8,128)}) %reduce-scatter.11.cloned.1.call-update) | async-done | bytes 1990672 | tf_op jit(solution)/shard_map/reduce_scatter | solution.py:238
  726.3 200.0 %reduce-scatter.15.cloned.1.call-done = f32[144,4304]{1,0:T(8,128)} async-done(((f32[1152,4304]{1,0:T(8,128)}), f32[144,4304]{1,0:T(8,128)}) %reduce-scatter.15.cloned.1.call-update) | async-done | bytes 2479120 | tf_op jit(solution)/shard_map/reduce_scatter | solution.py:240
  926.3 199.9 %reduce-scatter.17.cloned.1.call-done = f32[4304,144]{0,1:T(8,128)} async-done(((f32[4304,1152]{0,1:T(8,128)}), f32[4304,144]{0,1:T(8,128)}) %reduce-scatter.17.cloned.1.call-update) | async-done | bytes 2479120 | tf_op jit(solution)/shard_map/reduce_scatter | solution.py:241
  1126.9 27.5 %all-reduce.1 = f32[4304]{0:T(1024)} all-reduce(f32[4304]{0:T(1024)} %get-tuple-element.194), channel_id=8, replica_groups=mesh['fsdp'=8,'seq'=4] {'fsdp'}, use_global_device_ids=true, to_apply=%region_39.40.clone | all-reduce | flops 4304 | bytes 34432
  1155.7 12.9 fusion.99
  1171.5 19.4 %reduce-scatter.21.cloned.1.call-done = f32[144,6]{1,0:T(8,128)} async-done(((f32[1152,6]{1,0:T(8,128)}), f32[144,6]{1,0:T(8,128)}) %reduce-scatter.21.cloned.1.call-update) | async-done | bytes 3472
  1191.8 17.0 %all-reduce.2 = (f32[2,144]{1,0:T(2,128)}, f32[6,144]{1,0:T(8,128)}, f32[538]{0:T(1024)}) all-reduce(f32[2,144]{1,0:T(2,128)S(1)} %copy.105, f32[6,144]{1,0:T(8,128)S(1)} %copy.107, f32[538]{0:T(1024)S(1)} %copy-done.41), channel_id=1, replica_groups=mesh['fsdp'=8,'seq'=4] {'seq'}, use_global_device_ids=true, to_apply=%region_29.30 | all-reduce | flops 1690 | bytes 13520 | tf_op jit(solution)/shard_map/psum | solution.py:246
  1208.9 146.9 %all-reduce.6.cloned.1.call-done = (f32[144,3456]{1,0:T(8,128)}, f32[144,1152]{1,0:T(8,128)}, f32[144,4304]{1,0:T(8,128)}, f32[4304,144]{0,1:T(8,128)}) async-done(((f32[144,3456]{1,0:T(8,128)}, f32[144,1152]{1,0:T(8,128)}, f32[144,4304]{1,0:T(8,128)}, f32[4304,144]{0,1:T(8,128)}), (f32[144,3456]{1,0:T(8,128)}, f32[144,1152]{1,0:T(8,128)}, f32[144,4304]{1,0:T(8,128)}, ...) | async-done | bytes 7612432 | tf_op jit(solution)/shard_map/psum | solution.py:246
  1355.8 3.1 copy.146
  (263 shorter events, 81.4 us)
Async XLA Ops:
  7.2 2.8 copy-start.46
  7.2 18.6 %copy-start.51 = (bf16[2,144]{1,0:T(2,128)(2,1)S(1)}, bf16[2,144]{1,0:T(2,128)(2,1)}, u32[]{:S(2)}) copy-start(bf16[2,144]{1,0:T(2,128)(2,1)} %param.20) | copy-start | bytes 1732
  7.2 30.6 %copy-start = (bf16[2,256,1152]{2,1,0:T(8,128)(2,1)S(1)}, bf16[2,256,1152]{2,1,0:T(8,128)(2,1)}, u32[]{:S(2)}) copy-start(bf16[2,256,1152]{2,1,0:T(8,128)(2,1)} %param.14) | copy-start | bytes 3538948
  7.2 83.8 %all-gather.7.cloned.1.call-start = ((), (), s32[]{:S(2)}) async-start(), calls=%async_computation.10 | async-start | bytes 8957952 | tf_op jit(solution)/shard_map/all_gather | solution.py:124
  7.9 240.3 %all-gather.9.cloned.1.call-start = ((), (), s32[]{:S(2)}) async-start(), calls=%async_computation.11 | async-start | bytes 2985984 | tf_op jit(solution)/shard_map/all_gather | solution.py:125
  8.7 246.0 %all-gather.11.cloned.1.call-start = ((), (), s32[]{:S(2)}) async-start(), calls=%async_computation.12 | async-start | bytes 11280384 | tf_op jit(solution)/shard_map/all_gather | solution.py:126
  9.4 307.9 %all-gather.13.cloned.1.call-start = ((), (), s32[]{:S(2)}) async-start(), calls=%async_computation.13 | async-start | bytes 11280384 | tf_op jit(solution)/shard_map/all_gather | solution.py:127
  39.1 2.8 copy-start.36
  39.1 2.8 copy-start.38
  39.7 2.2 copy-start.29
  40.4 306.4 %copy-start.31 = (f32[1152]{0:T(1024)}, f32[1152]{0:T(1024)S(1)}, u32[]{:S(2)}) copy-start(f32[1152]{0:T(1024)S(1)} %get-tuple-element.126) | copy-start | bytes 13828
  116.4 45.0 %all-to-all-start = ((bf16[2,256,3,1152]{1,0,2,3:T(2,128)(2,1)}), bf16[2,256,3,1152]{1,0,2,3:T(2,128)(2,1)S(1)}, u32[]{:S(2)}, u32[]{:S(2)}) async-start(bf16[2,256,3,1152]{1,0,2,3:T(2,128)(2,1)} %copy.88), calls=%async_computation | async-start | bytes 7077888 | tf_op jit(solution)/shard_map/all_to_all | solution.py:143
  162.4 2.6 copy-start.25
  162.4 2.5 copy-start.26
  175.6 2.1 copy-start.2
  175.6 4.2 slice-start.2
  177.7 2.3 slice-start.3
  180.1 2.1 copy-start.18
  194.0 2.1 copy-start.2
  194.0 4.2 slice-start.2
  196.1 2.3 slice-start.3
  198.5 2.1 copy-start.18
  201.6 9.2 copy-start.47
  201.6 10.5 copy-start.48
  206.4 32.9 %all-to-all-start.1 = ((bf16[2,1024,288]{2,0,1:T(2,128)(2,1)}), bf16[2,1024,288]{2,0,1:T(2,128)(2,1)}, u32[]{:S(2)}, u32[]{:S(2)}) async-start(bf16[2,1024,288]{2,0,1:T(2,128)(2,1)} %copy.91), calls=%async_computation.1 | async-start | bytes 3145728 | tf_op jit(solution)/shard_map/all_to_all | solution.py:158
  252.9 93.9 %copy-start.40 = (f32[512]{0:T(512)}, f32[512]{0:T(512)S(1)}, u32[]{:S(2)}) copy-start(f32[512]{0:T(512)S(1)} %broadcast_multiply_fusion.4) | copy-start | bytes 6148
  254.7 92.1 %copy-start.43 = (f32[512]{0:T(512)}, f32[512]{0:T(512)S(1)}, u32[]{:S(2)}) copy-start(f32[512]{0:T(512)S(1)} %add_rsqrt_fusion) | copy-start | bytes 6148
  317.3 16.8 %copy-start.6 = (f32[512,1152]{1,0:T(8,128)S(1)}, f32[512,1152]{1,0:T(8,128)}, u32[]{:S(2)}) copy-start(f32[512,1152]{1,0:T(8,128)} %copy-done.5) | copy-start | bytes 7077892
  334.1 12.7 copy-start.52
  334.1 12.7 copy-start.11
  348.3 3.1 copy-start.3
  355.6 20.1 %all-to-all-start.2 = ((bf16[2,256,1152]{1,0,2:T(2,128)(2,1)}), bf16[2,256,1152]{1,0,2:T(2,128)(2,1)}, u32[]{:S(2)}, u32[]{:S(2)}) async-start(bf16[2,256,1152]{1,0,2:T(2,128)(2,1)} %copy.94), calls=%async_computation.2 | async-start | bytes 2359296 | tf_op jit(solution)/shard_map/all_to_all | solution.py:190
  359.9 267.4 %reduce-scatter.13.cloned.1.call-start = ((), (), s32[]{:S(2)}) async-start(), calls=%async_computation.15 | async-start | bytes 5971968 | tf_op jit(solution)/shard_map/reduce_scatter | solution.py:239
  390.7 7.2 slice-start
  396.6 2.2 slice-start.1
  422.5 2.4 copy-start.15
  432.6 7.1 slice-start
  438.4 2.2 slice-start.1
  464.2 2.3 copy-start.15
  480.9 5.2 copy-start.1
  480.9 5.2 copy-start.28
  480.9 5.2 copy-start.30
  480.9 5.2 copy-start.35
  480.9 5.2 copy-start.42
  480.9 58.0 %all-to-all-start.3 = ((bf16[2,1024,3,288]{3,0,2,1:T(2,128)(2,1)}), bf16[2,1024,3,288]{3,0,2,1:T(2,128)(2,1)}, u32[]{:S(2)}, u32[]{:S(2)}) async-start(bf16[2,1024,3,288]{3,0,2,1:T(2,128)(2,1)} %copy.97), calls=%async_computation.3 | async-start | bytes 9437184 | tf_op jit(solution)/shard_map/all_to_all | solution.py:213
  486.0 240.3 %reduce-scatter.11.cloned.1.call-start = ((), (), s32[]{:S(2)}) async-start(), calls=%async_computation.14 | async-start | bytes 17915904 | tf_op jit(solution)/shard_map/reduce_scatter | solution.py:238
  568.0 358.3 %reduce-scatter.15.cloned.1.call-start = ((), (), s32[]{:S(2)}) async-start(), calls=%async_computation.16 | async-start | bytes 22560768 | tf_op jit(solution)/shard_map/reduce_scatter | solution.py:240
  582.0 544.2 %reduce-scatter.17.cloned.1.call-start = ((), (), s32[]{:S(2)}) async-start(), calls=%async_computation.17 | async-start | bytes 22560768 | tf_op jit(solution)/shard_map/reduce_scatter | solution.py:241
  595.0 4.2 copy-start.33
  595.0 575.5 %reduce-scatter.19.cloned.1.call-start = ((), (), s32[]{:S(2)}) async-start(), calls=%async_computation.18 | async-start | bytes 663552
  599.7 6.2 copy-start.10
  599.7 6.2 copy-start.37
  599.7 6.2 copy-start.39
  619.3 571.6 %reduce-scatter.21.cloned.1.call-start = ((), (), s32[]{:S(2)}) async-start(), calls=%async_computation.19 | async-start | bytes 663552
  619.4 2.8 copy-start.45
  627.2 728.5 %all-reduce.6.cloned.1.call-start = ((), (), s32[]{:S(2)}) async-start(), calls=%async_computation.20 | async-start | bytes 15335424 | tf_op jit(solution)/shard_map/psum | solution.py:246
  1155.7 12.9 copy-start.50
  1155.7 12.9 copy-start.49
  1155.7 12.9 copy-start.4
  1155.7 12.9 copy-start.23
  1168.6 23.2 %copy-start.41 = (f32[538]{0:T(1024)S(1)}, f32[538]{0:T(1024)}, u32[]{:S(2)}) copy-start(f32[538]{0:T(1024)} %dynamic-slice.2) | copy-start | bytes 6460
  1355.8 3.1 copy-start.24
  1355.8 4.0 copy-start.22
  1359.8 2.6 copy-start.21
  (22 other events, 31.7 us)
Sparse Core Ops, SparseCore 0:
  9.7 81.3 all-gather.6
  92.7 32.6 all-gather.8
  127.0 94.7 all-gather.10
  223.3 93.9 all-gather.12
  366.1 59.3 reduce-scatter.12
  568.1 158.2 reduce-scatter.10
  728.8 197.4 reduce-scatter.14
  928.8 197.4 reduce-scatter.16
  1129.2 29.5 reduce-scatter.18
  1161.5 29.2 reduce-scatter.20
  1195.2 160.5 all-reduce.5
where the time goes:
time: 1380 us; the launch traced here: 1370 us
  waiting for transfers between devices  870 us (63%)
  matrix products  210 us (15%)
  local copies, waits for them, and re-layouts  113 us (8%)
  blocking collectives  99 us (7%)
  other arithmetic  42.6 us (3%)
  starting transfers between devices  18.2 us (1%)
  between operations  15.9 us (1%)
    reduce_scatter x1, waiting for transfers between devices, on_device(): lax.psum_scatter(dw_up, 'fsdp', scatter_dimension=0, tiled=True)  200 us
    reduce_scatter x1, waiting for transfers between devices, on_device(): lax.psum_scatter(dw_down, 'fsdp', scatter_dimension=1, tiled=True)  200 us
    psum x1, waiting for transfers between devices, on_device(): lax.psum((owned[0], owned[1], owned[2], owned[3], owned[4], owned[5], own...  147 us
    reduce_scatter x1, waiting for transfers between devices, on_device(): lax.psum_scatter(dw_qkv, 'fsdp', scatter_dimension=0, tiled=True)  99 us
    unnamed x2, blocking collectives  54.4 us
    all_to_all x1, waiting for transfers between devices, on_device(): lax.all_to_all(for_sending(stacked), 'seq', split_axis=1, concat_axis=3,...  52.3 us
    all_gather x1, waiting for transfers between devices, on_device(): lax.all_gather(w_down, 'fsdp', axis=1, tiled=True)  50.2 us
    all_gather x1, waiting for transfers between devices, on_device(): lax.all_gather(w_qkv, 'fsdp', axis=0, tiled=True)  49.1 us
  transfers between devices with their start and end apart: 15, of which 10 were waited for; matrix products, arithmetic and copies ran while one was open for 22% of the time, Pallas kernels for 0%

commit v1 on v0

--- a/solution.py
+++ b/solution.py
@@ -1,22 +1,330 @@
+import functools
 import math
 
 import jax
 import jax.numpy as jnp
 from jax import lax
+from jax.experimental import pallas as pl
+from jax.experimental.pallas import tpu as pltpu
 from jax.sharding import PartitionSpec as P
 
 HEAD_DIM = 72
 QBLOCK = 512
-
-
 EPSILON = 1e-06
 NEG_FILL = -1e30
 GELU_CUBE = 0.044715
 GELU_SCALE = math.sqrt(2.0 / math.pi)
-
-
-def for_sending(array):
-    return jax.tree.map(lambda a: a.astype(jnp.bfloat16) if a.dtype == jnp.float32 else a, array)
+LOG2E = math.log2(math.e)
+LANES = 128
+F32 = jnp.float32
+BF16 = jnp.bfloat16
+MIB = 2**20
+
+
+def attention_forward_kernel(block, heads, qkv_ref, bias_ref, out_ref, probs_ref, inv_ref, by_row, out_rows):
+    head = pl.program_id(0)
+    width = heads * HEAD_DIM
+    seq = qkv_ref.shape[0]
+
+    @pl.when(head == 0)
+    def _():
+        by_row[...] = qkv_ref[...].astype(F32).T
+
+    def rows(which):
+        return pl.ds(pl.multiple_of(which * width + head * HEAD_DIM, 8), HEAD_DIM)
+
+    query = by_row[rows(0), :].astype(BF16)
+    keys = by_row[rows(1), :].T.astype(BF16)
+    values = by_row[rows(2), :].astype(BF16)
+    bias = bias_ref[...]
+    for start in range(0, seq, block):
+        part = slice(start, start + block)
+        scores = jnp.dot(keys, query[:, part], preferred_element_type=F32) * (LOG2E / math.sqrt(HEAD_DIM)) + bias
+        top = jnp.max(scores, axis=0, keepdims=True)
+        raised = jnp.exp2(scores - top)
+        inv = 1.0 / jnp.sum(raised, axis=0, keepdims=True)
+        raised_low = raised.astype(BF16)
+        probs_ref[0, :, part] = raised_low
+        inv_ref[0, :, part] = inv
+        out_rows[rows(0), part] = jnp.dot(values, raised_low, preferred_element_type=F32) * inv
+
+    @pl.when(head == heads - 1)
+    def _():
+        out_ref[...] = out_rows[...].T.astype(BF16)
+
+
+def attention_forward(qkv, bias, block=QBLOCK):
+    seq, triple = qkv.shape
+    width = triple // 3
+    heads = width // HEAD_DIM
+    return pl.pallas_call(
+        functools.partial(attention_forward_kernel, block, heads),
+        grid=(heads,),
+        in_specs=[pl.BlockSpec((seq, triple), lambda h: (0, 0)), pl.BlockSpec((seq, 1), lambda h: (0, 0))],
+        out_specs=[
+            pl.BlockSpec((seq, width), lambda h: (0, 0)),
+            pl.BlockSpec((1, seq, seq), lambda h: (h, 0, 0)),
+            pl.BlockSpec((1, 1, seq), lambda h: (h, 0, 0)),
+        ],
+        out_shape=[
+            jax.ShapeDtypeStruct((seq, width), BF16),
+            jax.ShapeDtypeStruct((heads, seq, seq), BF16),
+            jax.ShapeDtypeStruct((heads, 1, seq), F32),
+        ],
+        scratch_shapes=[pltpu.VMEM((triple, seq), F32), pltpu.VMEM((width, seq), F32)],
+        compiler_params=pltpu.CompilerParams(vmem_limit_bytes=48 * MIB),
+        cost_estimate=pl.CostEstimate(
+            flops=10 * heads * seq * seq * 256, bytes_accessed=2 * heads * seq * seq, transcendentals=heads * seq * seq
+        ),
+    )(qkv, bias)
+
+
+def attention_backward_kernel(
+    block, heads, qkv_ref, d_out_ref, out_ref, probs_ref, inv_ref, grad_ref, by_row, d_rows, o_rows, grad_rows
+):
+    head = pl.program_id(0)
+    width = heads * HEAD_DIM
+    seq = qkv_ref.shape[0]
+    scale = 1.0 / math.sqrt(HEAD_DIM)
+
+    @pl.when(head == 0)
+    def _():
+        by_row[...] = qkv_ref[...].astype(F32).T
+        d_rows[...] = d_out_ref[...].astype(F32).T
+        o_rows[...] = out_ref[...].astype(F32).T
+
+    def rows(which):
+        return pl.ds(pl.multiple_of(which * width + head * HEAD_DIM, 8), HEAD_DIM)
+
+    query = by_row[rows(0), :].T.astype(BF16)
+    keys = by_row[rows(1), :].astype(BF16)
+    values = by_row[rows(2), :].T.astype(BF16)
+    d_out = d_rows[rows(0), :]
+    inv = inv_ref[0]
+    row_dot = jnp.sum(d_out * o_rows[rows(0), :], axis=0, keepdims=True) * inv
+    d_scaled = d_out * inv
+    d_tokens = d_scaled.T.astype(BF16)
+    d_scaled = d_scaled.astype(BF16)
+    d_keys = jnp.zeros((seq, HEAD_DIM), F32)
+    d_values = jnp.zeros((seq, HEAD_DIM), F32)
+    for start in range(0, seq, block):
+        part = slice(start, start + block)
+        raised = probs_ref[0, :, part]
+        d_probs = jnp.dot(values, d_scaled[:, part], preferred_element_type=F32)
+        d_scores = (raised.astype(F32) * (d_probs - row_dot[:, part])).astype(BF16)
+        d_values += jnp.dot(raised, d_tokens[part, :], preferred_element_type=F32)
+        d_keys += jnp.dot(d_scores, query[part, :], preferred_element_type=F32)
+        grad_rows[rows(0), part] = jnp.dot(keys, d_scores, preferred_element_type=F32) * scale
+    grad_rows[rows(1), :] = d_keys.T * scale
+    grad_rows[rows(2), :] = d_values.T
+
+    @pl.when(head == heads - 1)
+    def _():
+        grad_ref[...] = grad_rows[...].T.astype(BF16)
+
+
+def attention_backward(qkv, d_out, out, probs, inv, block=QBLOCK):
+    seq, triple = qkv.shape
+    width = triple // 3
+    heads = width // HEAD_DIM
+    whole = lambda h: (0, 0)
+    return pl.pallas_call(
+        functools.partial(attention_backward_kernel, block, heads),
+        grid=(heads,),
+        in_specs=[
+            pl.BlockSpec((seq, triple), whole),
+            pl.BlockSpec((seq, width), whole),
+            pl.BlockSpec((seq, width), whole),
+            pl.BlockSpec((1, seq, seq), lambda h: (h, 0, 0)),
+            pl.BlockSpec((1, 1, seq), lambda h: (h, 0, 0)),
+        ],
+        out_specs=pl.BlockSpec((seq, triple), whole),
+        out_shape=jax.ShapeDtypeStruct((seq, triple), BF16),
+        scratch_shapes=[
+            pltpu.VMEM((triple, seq), F32),
+            pltpu.VMEM((width, seq), F32),
+            pltpu.VMEM((width, seq), F32),
+            pltpu.VMEM((triple, seq), F32),
+        ],
+        compiler_params=pltpu.CompilerParams(vmem_limit_bytes=56 * MIB),
+        cost_estimate=pl.CostEstimate(
+            flops=12 * heads * seq * seq * 256, bytes_accessed=2 * heads * seq * seq, transcendentals=0
+        ),
+    )(qkv, d_out, out, probs, inv)
+
+
+class Place:
+    def __init__(self):
+        self.planes = lax.axis_size("fsdp") // 2
+        f = lax.axis_index("fsdp")
+        k = lax.axis_index("seq")
+        self.z, self.c = f // 2, f % 2
+        self.k, self.y, self.x = k, k // 2, k % 2
+
+    def send(self, value, to):
+        pairs = []
+        for z in range(self.planes):
+            for c in range(2):
+                for y in range(2):
+                    for x in range(2):
+                        tz, tc, ty, tx = to(z, c, y, x)
+                        pairs.append((((z * 2 + c) * 2 + y) * 2 + x, ((tz * 2 + tc) * 2 + ty) * 2 + tx))
+        return lax.ppermute(value, ("fsdp", "seq"), pairs)
+
+    def core(self, value):
+        return self.send(value, lambda z, c, y, x: (z, 1 - c, y, x))
+
+    def along_x(self, value):
+        return self.send(value, lambda z, c, y, x: (z, c, y, 1 - x))
+
+    def along_y(self, value):
+        return self.send(value, lambda z, c, y, x: (z, c, 1 - y, x))
+
+    def across(self, value):
+        return self.send(value, lambda z, c, y, x: (z, c, 1 - y, 1 - x))
+
+    def along_z(self, value, step):
+        return self.send(value, lambda z, c, y, x: (z ^ step, c, y, x))
+
+    def turn(self, value, step):
+        return self.send(value, lambda z, c, y, x: (z, y, c, x ^ step))
+
+
+def after(value, *others):
+    return lax.optimization_barrier((value, *others))[0]
+
+
+def pick(stack, index):
+    return lax.dynamic_index_in_dim(stack, index, 0, keepdims=False)
+
+
+def in_order(flag, mine, other):
+    return jnp.where(flag == 0, jnp.concatenate([mine, other]), jnp.concatenate([other, mine]))
+
+
+def to_image(place, parts):
+    near = place.turn(pick(parts, place.x), 0)
+    far = place.turn(pick(parts, 1 - place.x), 1)
+    return in_order(place.x, near, far)
+
+
+def from_image(place, half):
+    parts = half.reshape(2, half.shape[0] // 2, half.shape[1])
+    near = place.turn(pick(parts, place.x), 0)
+    far = place.turn(pick(parts, 1 - place.x), 1)
+    return in_order(place.x, near[None], far[None])
+
+
+def both_halves(place, half):
+    return in_order(place.c, half, place.core(half))
+
+
+def lane_cut(columns):
+    return columns // 2 // LANES * LANES
+
+
+def spread(place, give, keep):
+    block = in_order(place.c, keep, place.core(give))
+    rows, columns = block.shape[0] // 4, block.shape[1]
+    quarters = block.reshape(4, rows, columns)
+    mine = pick(quarters, place.k)
+    own = jnp.stack([place.along_z(mine, step) for step in range(1, place.planes)])
+    cut = lane_cut(columns)
+    x_part = place.along_x(own)
+    y_part = place.along_y(own)
+    far_low = place.along_x(y_part[:, :, :cut])
+    far_high = place.along_y(x_part[:, :, cut:])
+    return assemble(place, quarters, own, x_part, y_part, far_low, far_high), own
+
+
+def assemble_kernel(planes, cut, scalars, block, own, x_part, y_part, far_low, far_high, out, sems):
+    z, k = scalars[0], scalars[1]
+    copies = [(block, out.at[pl.ds(z * 4, 4)])]
+    for step in range(1, planes):
+        at = (z ^ step) * 4
+        copies.append((own.at[step - 1], out.at[at + k]))
+        copies.append((x_part.at[step - 1], out.at[at + (k ^ 1)]))
+        copies.append((y_part.at[step - 1], out.at[at + (k ^ 2)]))
+        copies.append((far_low.at[step - 1], out.at[at + (k ^ 3), :, pl.ds(0, cut)]))
+        copies.append((far_high.at[step - 1], out.at[at + (k ^ 3), :, pl.ds(cut, out.shape[2] - cut)]))
+    started = [pltpu.make_async_copy(source, target, sems.at[i]) for i, (source, target) in enumerate(copies)]
+    for copy in started:
+        copy.start()
+    for copy in started:
+        copy.wait()
+
+
+def assemble(place, block, own, x_part, y_part, far_low, far_high):
+    rows, columns = block.shape[1:]
+    planes = place.planes
+    anywhere = pl.BlockSpec(memory_space=pl.ANY)
+    out = pl.pallas_call(
+        functools.partial(assemble_kernel, planes, lane_cut(columns)),
+        in_specs=[pl.BlockSpec(memory_space=pltpu.SMEM)] + [anywhere] * 6,
+        out_specs=pl.BlockSpec(memory_space=pltpu.VMEM),
+        out_shape=jax.ShapeDtypeStruct((planes * 4, rows, columns), block.dtype),
+        scratch_shapes=[pltpu.SemaphoreType.DMA((1 + 5 * (planes - 1),))],
+        compiler_params=pltpu.CompilerParams(vmem_limit_bytes=32 * MIB),
+        cost_estimate=pl.CostEstimate(
+            flops=0, bytes_accessed=4 * planes * 4 * rows * columns, transcendentals=0
+        ),
+    )(jnp.stack([place.z, place.k]).astype(jnp.int32), block, own, x_part, y_part, far_low, far_high)
+    return out.reshape(planes * 4 * rows, columns)
+
+
+def collect(place, partial):
+    planes = place.planes
+    columns = partial.shape[1]
+    rows = partial.shape[0] // planes // 4
+    cut = lane_cut(columns)
+    parts = partial.reshape(planes, 2, 2, rows, columns)
+    low, high = parts[..., :cut], parts[..., cut:]
+
+    def take(value, axis, index):
+        return lax.dynamic_index_in_dim(value, index, axis, keepdims=False)
+
+    def add(mine, arrived):
+        return (mine.astype(F32) + arrived.astype(F32)).astype(BF16)
+
+    low = add(take(low, 2, place.x), place.along_x(take(low, 2, 1 - place.x)))
+    high = add(take(high, 1, place.y), place.along_y(take(high, 1, 1 - place.y)))
+    low = add(take(low, 1, place.y), place.along_y(take(low, 1, 1 - place.y)))
+    high = add(take(high, 1, place.x), place.along_x(take(high, 1, 1 - place.x)))
+    plane = jnp.concatenate([low, high], axis=-1)
+    total = pick(plane, place.z).astype(F32)
+    for step in range(1, planes):
+        total = total + place.along_z(pick(plane, place.z ^ step), step).astype(F32)
+    mine = total.astype(BF16)
+    x_part = place.along_x(mine)
+    y_part = place.along_y(mine)
+    far = jnp.concatenate([place.along_x(y_part[:, :cut]), place.along_y(x_part[:, cut:])], axis=-1)
+    near_pair = in_order(place.x, mine, x_part)
+    far_pair = in_order(place.x, y_part, far)
+    matches = place.y == place.c
+    keep = jnp.where(matches, near_pair, far_pair)
+    give = jnp.where(matches, far_pair, near_pair)
+    return keep, place.core(give)
+
+
+def sum_chips(place, value):
+    value = value + place.along_x(value) + place.along_y(value) + place.across(value)
+    total = value
+    for step in range(1, place.planes):
+        total = total + place.along_z(value, step)
+    return total
+
+
+def own_columns(place, rows_of_columns):
+    n, width = rows_of_columns.shape
+    size = width // lax.axis_size("fsdp")
+    return lax.dynamic_slice_in_dim(rows_of_columns, lax.axis_index("fsdp") * size, size, axis=1)
+
+
+def norm_stats(values):
+    row_mean = jnp.mean(values, axis=-1, keepdims=True)
+    centred = values - row_mean
+    variance = jnp.mean(centred * centred, axis=-1, keepdims=True)
+    return row_mean, lax.rsqrt(variance + EPSILON)
 
 
 def layer_norm(values, gain_row, shift_row):
@@ -33,6 +341,218 @@
     first_mean = jnp.mean(scaled, axis=-1, keepdims=True)
     second_mean = jnp.mean(scaled * normed, axis=-1, keepdims=True)
     return inv_std * (scaled - first_mean - normed * second_mean)
+
+
+def gelu_and_slope(values):
+    square = values * values
+    tangent = jnp.tanh(GELU_SCALE * values * (1.0 + GELU_CUBE * square))
+    half = 0.5 * (1.0 + tangent)
+    slope = half + 0.5 * values * (1.0 - tangent * tangent) * GELU_SCALE * (1.0 + 3.0 * GELU_CUBE * square)
+    return values * half, slope
+
+
+def dot(a, b):
+    return jnp.dot(a, b, preferred_element_type=F32)
+
+
+def dot_t(a, b):
+    return lax.dot_general(a, b, (((1,), (1,)), ((), ())), preferred_element_type=F32)
+
+
+def t_dot(a, b):
+    return lax.dot_general(a, b, (((0,), (0,)), ((), ())), preferred_element_type=F32)
+
+
+def image_on_chip(inputs, key_mask, w_qkv, w_out, w_up, w_down, norm_gains, biases, up_bias, cotangent):
+    place = Place()
+    img_count, tok_count, width = inputs.shape
+    shard = w_qkv.shape[0]
+    fsdp = lax.axis_size("fsdp")
+    half_width = width // 2
+    hidden = w_up.shape[1]
+    half_hidden = -(-hidden // 2 // LANES) * LANES
+    up_shard = up_bias.shape[0]
+    up_cols = -(-up_shard // shard)
+
+    def halves_qkv(w):
+        return jnp.moveaxis(w.reshape(w.shape[0], 3, 2, half_width), 2, 0).reshape(2, w.shape[0], 3 * half_width)
+
+    def halves_hidden(w):
+        padded = jnp.pad(w, ((0, 0), (0, 2 * half_hidden - hidden)))
+        return jnp.stack([padded[:, :half_hidden], padded[:, half_hidden:]])
+
+    small = jnp.concatenate(
+        [
+            norm_gains,
+            biases,
+            jnp.pad(up_bias, (0, up_cols * shard - up_shard)).reshape(up_cols, shard),
+        ]
+    )
+    n_small = small.shape[0]
+    spare = -(3 * half_width) % LANES
+    extra = jnp.pad(small.T, ((0, 0), (0, spare - n_small)))
+    qkv_halves = halves_qkv(w_qkv)
+    give = jnp.concatenate([pick(qkv_halves, 1 - place.c), extra], axis=1)
+    keep = jnp.concatenate([pick(qkv_halves, place.c), extra], axis=1)
+
+    tokens = both_halves(place, to_image(place, inputs))
+    full_first, own_first = spread(place, give, keep)
+    full_qkv = full_first[:, : 3 * half_width]
+    small_rows = full_first[:, 3 * half_width : 3 * half_width + n_small].astype(F32).T
+    gain_rows, bias_rows = small_rows[:2], small_rows[2:8]
+    up_shift = (
+        small_rows[8:].reshape(up_cols, fsdp, shard).transpose(1, 0, 2).reshape(fsdp, up_cols * shard)[:, :up_shard]
+    ).reshape(hidden)
+    up_shift = pick(jnp.pad(up_shift, (0, 2 * half_hidden - hidden)).reshape(2, half_hidden), place.c)
+
+    out_halves = jnp.moveaxis(w_out.reshape(shard, 2, half_width), 1, 0)
+    up_halves = halves_hidden(w_up)
+    down_halves = halves_hidden(w_down.T)
+    out_up = jnp.concatenate([up_halves, jnp.pad(out_halves, ((0, 0), (0, 0), (0, -half_width % LANES)))], axis=2)
+    out_up = after(out_up, own_first)
+    full_out_up, own_out_up = spread(place, pick(out_up, 1 - place.c), pick(out_up, place.c))
+    full_up = full_out_up[:, :half_hidden]
+    half_out = full_out_up[:, half_hidden : half_hidden + half_width]
+    other_out = place.core(half_out)
+    full_out = jnp.where(
+        place.c == 0,
+        jnp.concatenate([half_out, other_out], axis=1),
+        jnp.concatenate([other_out, half_out], axis=1),
+    )
+    down_halves = after(down_halves, own_out_up)
+    full_down, _ = spread(place, pick(down_halves, 1 - place.c), pick(down_halves, place.c))
+    upstream = both_halves(place, to_image(place, after(cotangent, full_first)))
+
+    other_mask = place.core(key_mask)
+    live = pick(jnp.where(place.c == place.y, key_mask, other_mask), place.x)
+    mask_bias = jnp.where(live > 0, 0.0, NEG_FILL).astype(F32)[:, None]
+
+    shift_halves = bias_rows.reshape(6, 2, half_width)
+    qkv_shift = jnp.concatenate(
+        [pick(shift_halves[2], place.c), jnp.zeros((half_width,), F32), pick(shift_halves[3], place.c)]
+    )
+    tok_wide = tokens.astype(F32)
+    first_out, first_normed, first_inv = layer_norm(tok_wide, gain_rows[0], bias_rows[0])
+    first_low = first_out.astype(BF16)
+    packed = (dot(first_low, full_qkv) + qkv_shift).astype(BF16)
+    attended_half, raised, inv_total = attention_forward(packed, mask_bias)
+    other_half = place.core(attended_half)
+    attended = jnp.where(
+        place.c == 0,
+        jnp.concatenate([attended_half, other_half], axis=1),
+        jnp.concatenate([other_half, attended_half], axis=1),
+    )
+    residual = tok_wide + dot(attended, full_out) + bias_rows[4]
+    second_out, second_normed, second_inv = layer_norm(residual, gain_rows[1], bias_rows[1])
+    second_low = second_out.astype(BF16)
+    upper = dot(second_low, full_up) + up_shift
+    active, slope = gelu_and_slope(upper)
+    active = active.astype(BF16)
+    slope = slope.astype(BF16)
+
+    def own_half(value):
+        return pick(value.reshape(2, value.shape[0] // 2, value.shape[1]), place.c)
+
+    def other_half_of(value):
+        return pick(value.reshape(2, value.shape[0] // 2, value.shape[1]), 1 - place.c)
+
+    down_part = dot_t(active, full_down)
+    down_sum = own_half(down_part) + place.core(other_half_of(down_part).astype(BF16)).astype(F32)
+    layer_half = (own_half(residual) + down_sum + bias_rows[5]).astype(BF16)
+    layer_out = from_image(place, layer_half)
+
+    grad_wide = upstream.astype(F32)
+    d_active = dot(upstream, full_down)
+    d_upper = (d_active * slope.astype(F32)).astype(BF16)
+    dw_down = t_dot(upstream, active).astype(BF16)
+    down_sums = collect(place, dw_down)
+    d_second_part = dot_t(d_upper, full_up)
+    d_second = d_second_part + place.core(d_second_part.astype(BF16)).astype(F32)
+    dw_up = t_dot(second_low, d_upper).astype(BF16)
+    up_sums = collect(place, dw_up)
+    d_resid = grad_wide + norm_back(d_second, second_normed, second_inv, gain_rows[1])
+    d_resid_low = d_resid.astype(BF16)
+    d_attended = dot_t(d_resid_low, pick(full_out.reshape(2, half_width, width), place.c)).astype(BF16)
+    d_packed = attention_backward(packed, d_attended, attended_half, raised, inv_total)
+    dw_out = t_dot(
+        attended, jnp.where(place.c == 0, d_resid_low[:, :half_width], d_resid_low[:, half_width:])
+    ).astype(BF16)
+    by_hidden = jnp.sum(d_upper.astype(F32), axis=0)
+    by_hidden = jnp.where(
+        place.c == 0,
+        jnp.pad(by_hidden, (0, half_hidden)),
+        jnp.pad(by_hidden, (half_hidden, 0)),
+    )[:hidden].reshape(fsdp, up_shard)
+    by_hidden = jnp.pad(by_hidden, ((0, 0), (0, up_cols * shard - up_shard))).reshape(fsdp, up_cols, shard)
+    by_hidden = by_hidden.transpose(1, 0, 2).reshape(up_cols, width)
+    by_width = jnp.stack(
+        [
+            jnp.sum(d_second * second_normed, axis=0),
+            jnp.sum(d_second, axis=0),
+            jnp.sum(d_resid, axis=0),
+            jnp.sum(grad_wide, axis=0),
+        ]
+    )
+    by_width = jnp.where(place.c == 0, by_width, 0.0)
+    riders = jnp.concatenate([by_width, by_hidden])
+    riders = jnp.pad(riders, ((0, -half_width % LANES - riders.shape[0]), (0, 0))).T.astype(BF16)
+    out_sums = collect(place, jnp.concatenate([dw_out, riders], axis=1))
+    rider_sums = (out_sums[0][:, half_width:].astype(F32) + out_sums[1][:, half_width:].astype(F32)).T
+    out_sums = [part[:, :half_width] for part in out_sums]
+    second_sums = rider_sums[:4]
+    grad_upbias = rider_sums[4 : 4 + up_cols].reshape(up_cols * shard)[:up_shard]
+    dw_qkv = t_dot(first_low, d_packed).astype(BF16)
+    qkv_sums = collect(place, dw_qkv)
+    d_first_part = dot_t(d_packed, full_qkv)
+    d_first = own_half(d_first_part) + place.core(other_half_of(d_first_part).astype(BF16)).astype(F32)
+    normed_half = own_half(first_normed)
+    grad_half = (
+        own_half(d_resid) + norm_back(d_first, normed_half, own_half(first_inv), gain_rows[0])
+    ).astype(BF16)
+    grad_in = from_image(place, grad_half)
+
+    pack_wide = d_packed.astype(F32)
+    q_sum = jnp.sum(pack_wide[:, :half_width], axis=0)
+    v_sum = jnp.sum(pack_wide[:, 2 * half_width :], axis=0)
+    late = jnp.concatenate([jnp.sum(d_first * normed_half, axis=0), jnp.sum(d_first, axis=0), q_sum, v_sum])
+    late = sum_chips(place, late.reshape(-1, LANES)).reshape(-1)
+    late_other = place.core(late)
+    first_sums = (late[: 2 * width] + late_other[: 2 * width]).reshape(2, width)
+    qv_mine = late[2 * width :].reshape(2, 1, half_width)
+    qv_other = late_other[2 * width :].reshape(2, 1, half_width)
+    qv_sums = jnp.where(
+        place.c == 0, jnp.concatenate([qv_mine, qv_other], axis=1), jnp.concatenate([qv_other, qv_mine], axis=1)
+    ).reshape(2, width)
+    first_own = own_columns(place, first_sums)
+    qv_own = own_columns(place, qv_sums)
+    grad_gains = jnp.stack([first_own[0], second_sums[0]])
+    grad_biases = jnp.stack([first_own[1], second_sums[1], qv_own[0], qv_own[1], second_sums[2], second_sums[3]])
+
+    def side_by_side(sums):
+        mine, other = (part.astype(F32) for part in sums)
+        return jnp.where(place.c == 0, mine, other), jnp.where(place.c == 0, other, mine)
+
+    lower, higher = side_by_side(qkv_sums)
+    grad_qkv = jnp.stack([lower.reshape(shard, 3, half_width), higher.reshape(shard, 3, half_width)], axis=2)
+    grad_qkv = grad_qkv.reshape(shard, 3 * width)
+    grad_proj = jnp.concatenate(side_by_side(out_sums), axis=1)
+    grad_up = jnp.concatenate(side_by_side(up_sums), axis=1)[:, :hidden]
+    grad_down = jnp.concatenate(side_by_side(down_sums), axis=1)[:, :hidden].T
+    return (
+        layer_out,
+        grad_in,
+        grad_qkv,
+        grad_proj,
+        grad_up,
+        grad_down,
+        grad_gains,
+        grad_biases,
+        grad_upbias,
+    )
+
+
+def for_sending(array):
+    return jax.tree.map(lambda a: a.astype(jnp.bfloat16) if a.dtype == jnp.float32 else a, array)
 
 
 def gelu_tanh(values):
@@ -112,7 +632,7 @@
     )
 
 
-def on_device(inputs, key_mask, w_qkv, w_out, w_up, w_down, norm_gains, biases, up_bias, cotangent):
+def heads_over_seq(inputs, key_mask, w_qkv, w_out, w_up, w_down, norm_gains, biases, up_bias, cotangent):
     img_count, tok_count, width = inputs.shape
     seq_len = key_mask.shape[1]
     row_count = img_count * tok_count
@@ -259,31 +779,35 @@
 
 
 def solution(mesh):
-    return jax.shard_map(
-        on_device,
-        mesh=mesh,
-        in_specs=(
-            P("fsdp", "seq", None),
-            P("fsdp", None),
-            P("fsdp", None),
-            P("fsdp", None),
-            P("fsdp", None),
-            P(None, "fsdp"),
-            P(None, "fsdp"),
-            P(None, "fsdp"),
-            P("fsdp"),
-            P("fsdp", "seq", None),
-        ),
-        out_specs=(
-            P("fsdp", "seq", None),
-            P("fsdp", "seq", None),
-            P("fsdp", None),
-            P("fsdp", None),
-            P("fsdp", None),
-            P(None, "fsdp"),
-            P(None, "fsdp"),
-            P(None, "fsdp"),
-            P("fsdp"),
-        ),
-        check_vma=False,
-    )
+    in_specs = (
+        P("fsdp", "seq", None),
+        P("fsdp", None),
+        P("fsdp", None),
+        P("fsdp", None),
+        P("fsdp", None),
+        P(None, "fsdp"),
+        P(None, "fsdp"),
+        P(None, "fsdp"),
+        P("fsdp"),
+        P("fsdp", "seq", None),
+    )
+    out_specs = (
+        P("fsdp", "seq", None),
+        P("fsdp", "seq", None),
+        P("fsdp", None),
+        P("fsdp", None),
+        P("fsdp", None),
+        P(None, "fsdp"),
+        P(None, "fsdp"),
+        P(None, "fsdp"),
+        P("fsdp"),
+    )
+
+    def layer(*args):
+        images = args[0].shape[0] // mesh.shape["fsdp"]
+        planes = mesh.shape["fsdp"] // 2
+        fits = mesh.shape["seq"] == 4 and images == 2 and planes * 2 == mesh.shape["fsdp"] and planes & (planes - 1) == 0
+        plan = image_on_chip if fits else heads_over_seq
+        return jax.shard_map(plan, mesh=mesh, in_specs=in_specs, out_specs=out_specs, check_vma=False)(*args)
+
+    return layer

time: 1380 us -> 751 us (0.54)
  waiting for transfers between devices: 870 us -> 238 us
  starting transfers between devices: 18.2 us -> 139 us
  matrix products: 210 us -> 101 us
  blocking collectives: 99 us -> 0 us
  Pallas kernels: 0 us -> 57.3 us
  other arithmetic: 42.6 us -> 92.4 us
    reduce_scatter x4 -> x0, waiting for transfers between devices: 499 us -> none  [the longest x1 200 us: on_device(): lax.psum_scatter(dw_up, 'fsdp', scatter_dimension=0, tiled=True)]
    ppermute x0 -> x95, waiting for transfers between devices: none -> 238 us  [send(): return lax.ppermute(value, ('fsdp', 'seq'), pairs)]
    psum x1 -> x0, waiting for transfers between devices: 147 us -> none  [on_device(): lax.psum((owned[0], owned[1], owned[2], owned[3], owned[4], owned[5], own...]
    ppermute x0 -> x95, starting transfers between devices: none -> 139 us  [send(): return lax.ppermute(value, ('fsdp', 'seq'), pairs)]
    dot_general x40 -> x12, matrix products: 210 us -> 101 us  [the longest x4 42.5 us: dot(): return jnp.dot(a, b, preferred_element_type=F32)]
    all_to_all x4 -> x0, waiting for transfers between devices: 103 us -> none  [the longest x1 52.3 us: on_device(): lax.all_to_all(for_sending(stacked), 'seq', split_axis=1, concat_axis=3,...]
    all_gather x4 -> x0, waiting for transfers between devices: 99.4 us -> none  [the longest x1 50.2 us: on_device(): lax.all_gather(w_down, 'fsdp', axis=1, tiled=True)]
    pallas_call x0 -> x5, Pallas kernels: none -> 57.3 us  [the longest x1 26.6 us: attention_backward(): pl.pallas_call(functools.partial(attention_backward_kernel, block, heads)...]
  transfers between devices with their start and end apart: 15 -> 95, of which waited for: 10 -> 40; matrix products, arithmetic and copies ran while one was open for 22% -> 30% of each run, Pallas kernels for 0% -> 8%
where the time goes in v1:
time: 751 us; the launch traced here: 740 us
  waiting for transfers between devices  238 us (32%)
  starting transfers between devices  139 us (19%)
  local copies, waits for them, and re-layouts  109 us (15%)
  matrix products  101 us (13%)
  other arithmetic  92.4 us (12%)
  Pallas kernels  57.3 us (8%)
    ppermute x95, waiting for transfers between devices, send(): return lax.ppermute(value, ('fsdp', 'seq'), pairs)  238 us
    ppermute x95, starting transfers between devices, send(): return lax.ppermute(value, ('fsdp', 'seq'), pairs)  139 us
    dot_general x4, matrix products, dot(): return jnp.dot(a, b, preferred_element_type=F32)  42.5 us
    dot_general x4, matrix products, t_dot(): lax.dot_general(a, b, (((0,), (0,)), ((), ())), preferred_element_type=F32)  30.4 us
    unnamed x172, local copies, waits for them, and re-layouts  28.1 us
    dot_general x4, matrix products, dot_t(): lax.dot_general(a, b, (((1,), (1,)), ((), ())), preferred_element_type=F32)  27.8 us
    pallas_call x1, Pallas kernels, attention_backward(): pl.pallas_call(functools.partial(attention_backward_kernel, block, heads)...  26.6 us
    pallas_call x1, Pallas kernels, attention_forward(): pl.pallas_call(functools.partial(attention_forward_kernel, block, heads),...  19.5 us
  transfers between devices with their start and end apart: 95, of which 40 were waited for; matrix products, arithmetic and copies ran while one was open for 30% of the time, Pallas kernels for 8%

profile of v1, /device:TPU:0, one launch (start us, length us, event | category | flops | bytes accessed | tf_op | source)
XLA Modules:
  0.0 739.9 jit_solution(9174451237873665273)
XLA Ops:
  8.6 6.1 collective-permute-start
  22.1 2.6 collective-permute-start.5
  25.1 4.9 collective-permute-done.4
  30.0 12.5 %collective-permute-done.5 = bf16[72,1792]{1,0:T(8,128)(2,1)S(1)} collective-permute-done((bf16[72,1792]{1,0:T(8,128)(2,1)S(1)}, bf16[72,1792]{1,0:T(8,128)(2,1)S(1)}, u32[]{:S(2)}, u32[]{:S(2)}) %collective-permute-start.5) | collective-permute-done | bytes 258080 | tf_op jit(solution)/shard_map/ppermute | solution.py:172
  45.0 2.9 maximum_select_fusion.7
  50.2 5.1 collective-permute-done.7.x_part
  56.6 5.4 collective-permute-done.8.y_part
  66.9 2.9 collective-permute-start.14
  72.3 3.1 convert_reduce_fusion.2
  75.4 3.4 multiply_reduce_fusion.3
  78.8 8.6 %collective-permute-done.14 = bf16[72,2816]{1,0:T(8,128)(2,1)S(1)} collective-permute-done((bf16[72,2816]{1,0:T(8,128)(2,1)S(1)}, bf16[72,2816]{1,0:T(8,128)(2,1)S(1)}, u32[]{:S(2)}, u32[]{:S(2)}) %collective-permute-start.14) | collective-permute-done | bytes 405536 | tf_op jit(solution)/shard_map/ppermute | solution.py:172
  87.4 13.0 %collective-permute-done.15 = bf16[72,2816]{1,0:T(8,128)(2,1)S(1)} collective-permute-done((bf16[72,2816]{1,0:T(8,128)(2,1)S(1)}, bf16[72,2816]{1,0:T(8,128)(2,1)S(1)}, u32[]{:S(2)}, u32[]{:S(2)}) %collective-permute-start.15) | collective-permute-done | bytes 405536 | tf_op jit(solution)/shard_map/ppermute | solution.py:172
  102.6 4.4 shard_map.169
  114.3 8.2 %collective-permute-start.23 = (bf16[72,2176]{1,0:T(8,128)(2,1)S(1)}, bf16[72,2176]{1,0:T(8,128)(2,1)S(1)}, u32[]{:S(2)}, u32[]{:S(2)}) collective-permute-start(bf16[72,2176]{1,0:T(8,128)(2,1)S(1)} %dynamic-slice_bitcast_fusion.23), channel_id=1, source_target_pairs={{0,8},{1,9},{2,10},{3,11},{4,12},{5,13},{6,14},{7,15},{8,0},{9,1},... | collective-permute-start | bytes 940040 | tf_op jit(solution)/shard_map/ppermute | solution.py:172
  125.0 9.1 %add_convert_fusion.1.qkv_ref = bf16[1024,1728]{1,0:T(8,128)(2,1)S(1)} fusion(f32[1728]{0:T(1024)S(1)} %copy-done.63, bf16[1152,1792]{1,0:T(8,128)(2,1)} %bitcast.304, f32[1152]{0:T(1024)S(1)} %get-tuple-element.73, f32[1152]{0:T(1024)S(1)} %get-tuple-element.74, f32[1024]{0:T(1024)S(1)} %add_rsqrt_fusion.1, f32[1024]{0:T(1024)S(1)} %broadcast_multiply_fusion.3, ...), kind=kOutput, calls=%fused_computation.9 | convolution fusion | flops 4098097152 | bytes 10051329 | tf_op jit(solution)/shard_map/dot_general | solution.py:355
  136.0 11.1 %collective-permute-done.24 = bf16[72,2176]{1,0:T(8,128)(2,1)S(1)} collective-permute-done((bf16[72,2176]{1,0:T(8,128)(2,1)S(1)}, bf16[72,2176]{1,0:T(8,128)(2,1)S(1)}, u32[]{:S(2)}, u32[]{:S(2)}) %collective-permute-start.24) | collective-permute-done | bytes 313376 | tf_op jit(solution)/shard_map/ppermute | solution.py:172
  156.0 19.5 %shard_map.170 = (bf16[1024,576]{1,0:T(8,128)(2,1)S(1)}, bf16[8,1024,1024]{2,1,0:T(8,128)(2,1)}, f32[8,1,1024]{2,1,0:T(1,128)S(1)}) custom-call(bf16[1024,1728]{1,0:T(8,128)(2,1)S(1)} %add_convert_fusion.1.qkv_ref, f32[1024,1]{1,0:T(8,128)S(1)} %copy-done.18), custom_call_target="tpu_custom_call" | custom-call | flops 21474836480 | bytes 16777216 | tf_op jit(solution)/shard_map/pallas_call | solution.py:60
  186.4 3.7 shard_map.171
  190.2 2.7 copy-done
  200.4 5.0 fusion.114
  216.0 3.0 collective-permute-start.35
  223.0 3.2 collective-permute-done.29.far_high
  226.2 3.1 shard_map.172
  229.4 10.7 %fusion.118 = (f32[1024]{0:T(1024)S(1)}, f32[1024,1152]{1,0:T(8,128)S(1)}) fusion(f32[1152]{0:T(1024)S(1)} %get-tuple-element.70, bf16[1152,576]{0,1:T(8,128)(2,1)} %collective-permute-done.21, bf16[1152,576]{0,1:T(8,128)(2,1)} %copy.194, pred[]{:T(512)S(6)} %eq.12, bf16[1024,576]{1,0:T(8,128)(2,1)} %copy.169, bf16[1024,576]{1,0:T(8,128)(2,1)S(1)} %copy-done.16, ...), kind=kOutput, calls=%fused_computation.361 | convolution fusion | flops 2755804160 | bytes 12100097 | tf_op jit(solution)/shard_map/dot_general | solution.py:355
  240.7 9.5 %multiply_convert_fusion.1 = (bf16[1024,2176]{1,0:T(8,128)(2,1)S(1)}, f32[1024,2176]{1,0:T(8,128)}) fusion(f32[2176]{0:T(1024)S(1)} %fusion.105, bf16[1152,2816]{1,0:T(8,128)(2,1)S(1)} %bitcast.291, f32[1024,1152]{1,0:T(8,128)S(1)} %get-tuple-element.132, f32[1152]{0:T(1024)S(1)} %get-tuple-element.68, f32[1152]{0:T(1024)S(1)} %get-tuple-element.69, ...), kind=kOutput, calls=%fused_computation.5 | convolution fusion | flops 5162008576 | bytes 23138304 | tf_op jit(solution)/shard_map/dot_general | solution.py:355
  250.2 10.3 %convolution_convert_fusion = bf16[1152,2176]{1,0:T(8,128)(2,1)S(1)} fusion(bf16[1024,2176]{1,0:T(8,128)(2,1)S(1)} %get-tuple-element.133, bf16[512,1152]{1,0:T(8,128)(2,1)} %collective-permute-done.35, bf16[512,1152]{1,0:T(8,128)(2,1)} %maximum_select_fusion.9, pred[]{:T(512)S(6)} %eq.12), kind=kOutput, calls=%fused_computation | convolution fusion | flops 5146951680 | bytes 11829249 | tf_op jit(solution)/shard_map/dot_general | solution.py:363
  263.9 13.3 %convert_reduce_fusion = (bf16[2176]{0:T(1024)(128)(2,1)S(1)}, bf16[1024,2176]{1,0:T(8,128)(2,1)S(1)}) fusion(f32[1024,2176]{1,0:T(8,128)} %get-tuple-element.134, f32[2176]{0:T(1024)S(1)} %fusion.105, bf16[1152,2176]{1,0:T(8,128)(2,1)S(1)} %bitcast.299, bf16[512,1152]{1,0:T(8,128)(2,1)} %collective-permute-done.35, ...), kind=kOutput, calls=%fused_computation.2 | convolution fusion | flops 5195692032 | bytes 20755200 | tf_op jit(solution)/shard_map/dot_general | solution.py:355
  277.2 8.3 %fusion.119 = (bf16[1024,1152]{1,0:T(8,128)(2,1)}, f32[1024,1152]{1,0:T(8,128)}) fusion(bf16[1024,2176]{1,0:T(8,128)(2,1)S(1)} %get-tuple-element.138, bf16[1152,2816]{1,0:T(8,128)(2,1)S(1)} %bitcast.292), kind=kOutput, calls=%fused_computation.362 | convolution fusion | flops 5135007744 | bytes 16547840 | tf_op jit(solution)/shard_map/dot_general | solution.py:359
  285.5 6.7 convolution_convert_fusion.1
  294.6 3.0 constant_dynamic-slice_fusion.7
  307.0 8.4 %fusion.120 = f32[2,512,1152]{2,1,0:T(8,128)S(1)} fusion(bf16[2,512,2176]{2,1,0:T(8,128)(2,1)} %bitcast.358, bf16[1152,2176,1]{1,0,2:T(8,128)(2,1)S(1)} %bitcast.302), kind=kOutput, calls=%fused_computation.363 | convolution fusion | flops 5133828096 | bytes 14188544 | tf_op jit(solution)/shard_map/dot_general | solution.py:359
  319.6 2.7 copy.175
  322.3 5.5 collective-permute-done.76
  330.2 22.5 %collective-permute-done.64 = bf16[4,2,72,1024]{3,2,0,1:T(8,128)(2,1)} collective-permute-done((bf16[4,2,72,1024]{3,2,0,1:T(8,128)(2,1)}, bf16[4,2,72,1024]{3,2,0,1:T(8,128)(2,1)}, u32[]{:S(2)}, u32[]{:S(2)}) %collective-permute-start.64) | collective-permute-done | bytes 1179680 | tf_op jit(solution)/shard_map/ppermute | solution.py:172
  364.4 17.4 %collective-permute-done.77 = bf16[4,72,1024]{2,1,0:T(8,128)(2,1)S(1)} collective-permute-done((bf16[4,72,1024]{2,1,0:T(8,128)(2,1)S(1)}, bf16[4,72,1024]{2,1,0:T(8,128)(2,1)S(1)}, u32[]{:S(2)}, u32[]{:S(2)}) %collective-permute-start.77) | collective-permute-done | bytes 589856 | tf_op jit(solution)/shard_map/ppermute | solution.py:172
  383.1 10.7 %collective-permute-done.65 = bf16[4,72,1024]{2,1,0:T(8,128)(2,1)S(1)} collective-permute-done((bf16[4,72,1024]{2,1,0:T(8,128)(2,1)S(1)}, bf16[4,72,1024]{2,1,0:T(8,128)(2,1)S(1)}, u32[]{:S(2)}, u32[]{:S(2)}) %collective-permute-start.65) | collective-permute-done | bytes 589856 | tf_op jit(solution)/shard_map/ppermute | solution.py:172
  396.3 2.6 collective-permute-done.79
  399.1 7.3 collective-permute-start.80
  408.8 2.7 collective-permute-done.67
  411.8 7.3 collective-permute-start.68
  420.2 10.5 %collective-permute-start.70 = (bf16[72,2176]{1,0:T(8,128)(2,1)S(1)}, bf16[72,2176]{1,0:T(8,128)(2,1)S(1)}, u32[]{:S(2)}, u32[]{:S(2)}) collective-permute-start(bf16[72,2176]{1,0:T(8,128)(2,1)S(1)} %get-tuple-element.96), channel_id=1, source_target_pairs={{0,24},{1,25},{2,26},{3,27},{4,28},{5,29},{6,30},{7,31},{8,16},{9,... | collective-permute-start | bytes 940040 | tf_op jit(solution)/shard_map/ppermute | solution.py:172
  430.8 4.4 collective-permute-start.84
  436.3 20.3 %collective-permute-done.69 = bf16[72,2176]{1,0:T(8,128)(2,1)S(1)} collective-permute-done((bf16[72,2176]{1,0:T(8,128)(2,1)S(1)}, bf16[72,2176]{1,0:T(8,128)(2,1)S(1)}, u32[]{:S(2)}, u32[]{:S(2)}) %collective-permute-start.69) | collective-permute-done | bytes 313376 | tf_op jit(solution)/shard_map/ppermute | solution.py:172
  459.0 4.4 multiply_reduce_fusion
  463.4 6.0 fusion.115
  476.6 26.6 %shard_map.173 = bf16[1024,1728]{1,0:T(8,128)(2,1)} custom-call(bf16[1024,1728]{1,0:T(8,128)(2,1)} %copy-done.19, bf16[1024,576]{1,0:T(8,128)(2,1)} %copy.176.d_out_ref, bf16[1024,576]{1,0:T(8,128)(2,1)} %copy-done.15, bf16[8,1024,1024]{2,1,0:T(8,128)(2,1)} %get-tuple-element.19.probs_ref, f32[8,1,1024]{2,1,0:T(1,128)} %copy-done.20), custom_call_target="tpu_custom_call" | custom-call | flops 25769803776 | bytes 16777216 | tf_op jit(solution)/shard_map/pallas_call | solution.py:131
  503.2 9.3 %fusion.4 = f32[1024,1152]{1,0:T(8,128)} fusion(bf16[1024,1728]{1,0:T(8,128)(2,1)} %shard_map.173, bf16[1152,1792]{1,0:T(8,128)(2,1)S(1)} %bitcast.305), kind=kOutput, calls=%fused_computation.27 | convolution fusion | flops 4076863488 | bytes 12386304 | tf_op jit(solution)/shard_map/dot_general | solution.py:359
  512.6 4.1 convert_element_type.530
  517.3 2.8 convolution_convert_fusion.3
  523.2 10.6 %convolution_convert_fusion.2 = bf16[1152,1728]{0,1:T(8,128)(2,1)} fusion(bf16[1024,1728]{1,0:T(8,128)(2,1)} %shard_map.173, f32[1152]{0:T(1024)S(1)} %copy-done.61, f32[1152]{0:T(1024)S(1)} %copy-done.52, f32[1024]{0:T(1024)S(1)} %copy-done.56, f32[1024]{0:T(1024)S(1)} %copy-done.54, bf16[512,1152]{1,0:T(8,128)(2,1)} %collective-permute-done.2, ...), kind=kOutput, calls=%fused_computation.8 | convolution fusion | flops 4096548864 | bytes 9896961 | tf_op jit(solution)/shard_map/dot_general | solution.py:363
  533.8 6.8 copy.177
  548.3 2.8 fusion.40
  561.5 20.6 %collective-permute-done.85 = bf16[72,1024]{1,0:T(8,128)(2,1)S(1)} collective-permute-done((bf16[72,1024]{1,0:T(8,128)(2,1)S(1)}, bf16[72,1024]{1,0:T(8,128)(2,1)S(1)}, u32[]{:S(2)}, u32[]{:S(2)}) %collective-permute-start.85) | collective-permute-done | bytes 147488 | tf_op jit(solution)/shard_map/ppermute | solution.py:172
  584.3 4.5 collective-permute-done.86
  590.4 4.6 collective-permute-done.55
  595.1 6.2 collective-permute-start.56
  605.7 3.0 collective-permute-done.57
  610.9 21.0 %collective-permute-done.74 = bf16[72,1152]{1,0:T(8,128)(2,1)S(1)} collective-permute-done((bf16[72,1152]{1,0:T(8,128)(2,1)S(1)}, bf16[72,1152]{1,0:T(8,128)(2,1)S(1)}, u32[]{:S(2)}, u32[]{:S(2)}) %collective-permute-start.74) | collective-permute-done | bytes 165920 | tf_op jit(solution)/shard_map/ppermute | solution.py:172
  660.5 4.4 multiply_reduce_fusion.5
  671.2 4.8 collective-permute-done.88
  682.0 3.2 fusion.22
  698.7 4.3 collective-permute-done.44
  703.0 7.5 %collective-permute-done.45 = bf16[72,1728]{1,0:T(8,128)(2,1)S(1)} collective-permute-done((bf16[72,1728]{1,0:T(8,128)(2,1)S(1)}, bf16[72,1728]{1,0:T(8,128)(2,1)S(1)}, u32[]{:S(2)}, u32[]{:S(2)}) %collective-permute-start.45) | collective-permute-done | bytes 248864 | tf_op jit(solution)/shard_map/ppermute | solution.py:172
  713.2 5.1 collective-permute-done.48
  (532 shorter events, 247.2 us)
Async XLA Ops:
  8.6 35.9 %collective-permute-start = (bf16[256,1152]{1,0:T(8,128)(2,1)}, bf16[256,1152]{1,0:T(8,128)(2,1)}, u32[]{:S(2)}, u32[]{:S(2)}) collective-permute-start(bf16[256,1152]{1,0:T(8,128)(2,1)} %get-tuple-element.109), channel_id=1, source_target_pairs={{0,0},{1,1},{2,4},{3,5},{4,2},{5,3},{6,6},{7,7},{8,8},{9,9},{10,12... | collective-permute-start | bytes 1769480 | tf_op jit(solution)/shard_map/ppermute | solution.py:172
  14.7 30.3 %collective-permute-start.1 = (bf16[256,1152]{1,0:T(8,128)(2,1)}, bf16[256,1152]{1,0:T(8,128)(2,1)}, u32[]{:S(2)}, u32[]{:S(2)}) collective-permute-start(bf16[256,1152]{1,0:T(8,128)(2,1)} %get-tuple-element.110), channel_id=1, source_target_pairs={{0,1},{1,0},{2,5},{3,4},{4,3},{5,2},{6,7},{7,6},{8,9},{9,8},{10,13... | collective-permute-start | bytes 1769480 | tf_op jit(solution)/shard_map/ppermute | solution.py:172
  22.1 20.3 %collective-permute-start.5 = (bf16[72,1792]{1,0:T(8,128)(2,1)S(1)}, bf16[72,1792]{1,0:T(8,128)(2,1)S(1)}, u32[]{:S(2)}, u32[]{:S(2)}) collective-permute-start(bf16[72,1792]{1,0:T(8,128)(2,1)S(1)} %dynamic-slice_bitcast_fusion.24), channel_id=1, source_target_pairs={{0,16},{1,17},{2,18},{3,19},{4,20},{5,21},{6,22},{7,23},{8,24},{9,... | collective-permute-start | bytes 774152 | tf_op jit(solution)/shard_map/ppermute | solution.py:172
  24.7 17.7 %collective-permute-start.6 = (bf16[72,1792]{1,0:T(8,128)(2,1)S(1)}, bf16[72,1792]{1,0:T(8,128)(2,1)S(1)}, u32[]{:S(2)}, u32[]{:S(2)}) collective-permute-start(bf16[72,1792]{1,0:T(8,128)(2,1)S(1)} %dynamic-slice_bitcast_fusion.24), channel_id=1, source_target_pairs={{0,24},{1,25},{2,26},{3,27},{4,28},{5,29},{6,30},{7,31},{8,16},{9,... | collective-permute-start | bytes 774152 | tf_op jit(solution)/shard_map/ppermute | solution.py:172
  30.0 19.2 %collective-permute-start.11 = (s32[2,1024]{1,0:T(2,128)S(1)}, s32[2,1024]{1,0:T(2,128)S(1)}, u32[]{:S(2)}, u32[]{:S(2)}) collective-permute-start(s32[2,1024]{1,0:T(2,128)S(1)} %copy-done.65), channel_id=1, source_target_pairs={{0,4},{1,5},{2,6},{3,7},{4,0},{5,1},{6,2},{7,3},{8,12},{9,13},{10,... | collective-permute-start | bytes 24584 | tf_op jit(solution)/shard_map/ppermute | solution.py:172
  43.2 18.8 %collective-permute-start.8 = (bf16[3,72,1792]{2,1,0:T(8,128)(2,1)S(1)}, bf16[3,72,1792]{2,1,0:T(8,128)(2,1)S(1)}, u32[]{:S(2)}, u32[]{:S(2)}) collective-permute-start(bf16[3,72,1792]{2,1,0:T(8,128)(2,1)S(1)} %pad_maximum_fusion.7.own), channel_id=1, source_target_pairs={{0,2},{1,3},{2,0},{3,1},{4,6},{5,7},{6,4},{7,5},{8,10},{9,11},{10,... | collective-permute-start | bytes 2322440 | tf_op jit(solution)/shard_map/ppermute | solution.py:172
  44.4 20.1 %collective-permute-start.13 = (bf16[144,2816]{1,0:T(8,128)(2,1)}, bf16[144,2816]{1,0:T(8,128)(2,1)}, u32[]{:S(2)}, u32[]{:S(2)}) collective-permute-start(bf16[144,2816]{1,0:T(8,128)(2,1)} %get-tuple-element.90), channel_id=1, source_target_pairs={{0,4},{1,5},{2,6},{3,7},{4,0},{5,1},{6,2},{7,3},{8,12},{9,13},{10,... | collective-permute-start | bytes 2433032 | tf_op jit(solution)/shard_map/ppermute | solution.py:172
  47.9 23.0 %collective-permute-start.2 = (bf16[512,1152]{1,0:T(8,128)(2,1)}, bf16[512,1152]{1,0:T(8,128)(2,1)}, u32[]{:S(2)}, u32[]{:S(2)}) collective-permute-start(bf16[512,1152]{1,0:T(8,128)(2,1)} %maximum_select_fusion.7), channel_id=1, source_target_pairs={{0,4},{1,5},{2,6},{3,7},{4,0},{5,1},{6,2},{7,3},{8,12},{9,13},{10,... | collective-permute-start | bytes 3538952 | tf_op jit(solution)/shard_map/ppermute | solution.py:172
  55.4 47.1 %collective-permute-start.10 = (bf16[3,72,896]{2,1,0:T(8,128)(2,1)S(1)}, bf16[3,72,896]{2,1,0:T(8,128)(2,1)S(1)}, u32[]{:S(2)}, u32[]{:S(2)}) collective-permute-start(bf16[3,72,896]{2,1,0:T(8,128)(2,1)S(1)} %slice.300), channel_id=1, source_target_pairs={{0,2},{1,3},{2,0},{3,1},{4,6},{5,7},{6,4},{7,5},{8,10},{9,11},{10,... | collective-permute-start | bytes 1161224 | tf_op jit(solution)/shard_map/ppermute | solution.py:172
  62.0 40.5 %collective-permute-start.9 = (bf16[3,72,896]{2,1,0:T(8,128)(2,1)S(1)}, bf16[3,72,896]{2,1,0:T(8,128)(2,1)S(1)}, u32[]{:S(2)}, u32[]{:S(2)}) collective-permute-start(bf16[3,72,896]{2,1,0:T(8,128)(2,1)S(1)} %slice.299), channel_id=1, source_target_pairs={{0,1},{1,0},{2,3},{3,2},{4,5},{5,4},{6,7},{7,6},{8,9},{9,8},{10,11... | collective-permute-start | bytes 1161224 | tf_op jit(solution)/shard_map/ppermute | solution.py:172
  66.9 20.5 %collective-permute-start.14 = (bf16[72,2816]{1,0:T(8,128)(2,1)S(1)}, bf16[72,2816]{1,0:T(8,128)(2,1)S(1)}, u32[]{:S(2)}, u32[]{:S(2)}) collective-permute-start(bf16[72,2816]{1,0:T(8,128)(2,1)S(1)} %dynamic-slice_bitcast_fusion.22), channel_id=1, source_target_pairs={{0,8},{1,9},{2,10},{3,11},{4,12},{5,13},{6,14},{7,15},{8,0},{9,1},... | collective-permute-start | bytes 1216520 | tf_op jit(solution)/shard_map/ppermute | solution.py:172
  69.8 30.6 %collective-permute-start.15 = (bf16[72,2816]{1,0:T(8,128)(2,1)S(1)}, bf16[72,2816]{1,0:T(8,128)(2,1)S(1)}, u32[]{:S(2)}, u32[]{:S(2)}) collective-permute-start(bf16[72,2816]{1,0:T(8,128)(2,1)S(1)} %dynamic-slice_bitcast_fusion.22), channel_id=1, source_target_pairs={{0,16},{1,17},{2,18},{3,19},{4,20},{5,21},{6,22},{7,23},{8,24},{9,... | collective-permute-start | bytes 1216520 | tf_op jit(solution)/shard_map/ppermute | solution.py:172
  70.9 29.5 %collective-permute-start.16 = (bf16[72,2816]{1,0:T(8,128)(2,1)S(1)}, bf16[72,2816]{1,0:T(8,128)(2,1)S(1)}, u32[]{:S(2)}, u32[]{:S(2)}) collective-permute-start(bf16[72,2816]{1,0:T(8,128)(2,1)S(1)} %dynamic-slice_bitcast_fusion.22), channel_id=1, source_target_pairs={{0,24},{1,25},{2,26},{3,27},{4,28},{5,29},{6,30},{7,31},{8,16},{9,... | collective-permute-start | bytes 1216520 | tf_op jit(solution)/shard_map/ppermute | solution.py:172
  110.8 39.5 %collective-permute-start.18 = (bf16[3,72,2816]{2,1,0:T(8,128)(2,1)}, bf16[3,72,2816]{2,1,0:T(8,128)(2,1)S(1)}, u32[]{:S(2)}, u32[]{:S(2)}) collective-permute-start(bf16[3,72,2816]{2,1,0:T(8,128)(2,1)} %pad_maximum_fusion.5.own), channel_id=1, source_target_pairs={{0,2},{1,3},{2,0},{3,1},{4,6},{5,7},{6,4},{7,5},{8,10},{9,11},{10,... | collective-permute-start | bytes 3649544 | tf_op jit(solution)/shard_map/ppermute | solution.py:172
  111.9 41.3 %collective-permute-start.17 = (bf16[3,72,2816]{2,1,0:T(8,128)(2,1)}, bf16[3,72,2816]{2,1,0:T(8,128)(2,1)S(1)}, u32[]{:S(2)}, u32[]{:S(2)}) collective-permute-start(bf16[3,72,2816]{2,1,0:T(8,128)(2,1)} %pad_maximum_fusion.5.own), channel_id=1, source_target_pairs={{0,1},{1,0},{2,3},{3,2},{4,5},{5,4},{6,7},{7,6},{8,9},{9,8},{10,11... | collective-permute-start | bytes 3649544 | tf_op jit(solution)/shard_map/ppermute | solution.py:172
  114.3 21.7 %collective-permute-start.23 = (bf16[72,2176]{1,0:T(8,128)(2,1)S(1)}, bf16[72,2176]{1,0:T(8,128)(2,1)S(1)}, u32[]{:S(2)}, u32[]{:S(2)}) collective-permute-start(bf16[72,2176]{1,0:T(8,128)(2,1)S(1)} %dynamic-slice_bitcast_fusion.23), channel_id=1, source_target_pairs={{0,8},{1,9},{2,10},{3,11},{4,12},{5,13},{6,14},{7,15},{8,0},{9,1},... | collective-permute-start | bytes 940040 | tf_op jit(solution)/shard_map/ppermute | solution.py:172
  122.5 24.6 %collective-permute-start.24 = (bf16[72,2176]{1,0:T(8,128)(2,1)S(1)}, bf16[72,2176]{1,0:T(8,128)(2,1)S(1)}, u32[]{:S(2)}, u32[]{:S(2)}) collective-permute-start(bf16[72,2176]{1,0:T(8,128)(2,1)S(1)} %dynamic-slice_bitcast_fusion.23), channel_id=1, source_target_pairs={{0,16},{1,17},{2,18},{3,19},{4,20},{5,21},{6,22},{7,23},{8,24},{9,... | collective-permute-start | bytes 940040 | tf_op jit(solution)/shard_map/ppermute | solution.py:172
  123.6 23.6 %collective-permute-start.25 = (bf16[72,2176]{1,0:T(8,128)(2,1)S(1)}, bf16[72,2176]{1,0:T(8,128)(2,1)S(1)}, u32[]{:S(2)}, u32[]{:S(2)}) collective-permute-start(bf16[72,2176]{1,0:T(8,128)(2,1)S(1)} %dynamic-slice_bitcast_fusion.23), channel_id=1, source_target_pairs={{0,24},{1,25},{2,26},{3,27},{4,28},{5,29},{6,30},{7,31},{8,16},{9,... | collective-permute-start | bytes 940040 | tf_op jit(solution)/shard_map/ppermute | solution.py:172
  148.2 51.1 %collective-permute-start.26 = (bf16[3,72,2176]{2,1,0:T(8,128)(2,1)}, bf16[3,72,2176]{2,1,0:T(8,128)(2,1)}, u32[]{:S(2)}, u32[]{:S(2)}) collective-permute-start(bf16[3,72,2176]{2,1,0:T(8,128)(2,1)} %pad_maximum_fusion.6.own), channel_id=1, source_target_pairs={{0,1},{1,0},{2,3},{3,2},{4,5},{5,4},{6,7},{7,6},{8,9},{9,8},{10,11... | collective-permute-start | bytes 2820104 | tf_op jit(solution)/shard_map/ppermute | solution.py:172
  149.2 58.1 %collective-permute-start.27 = (bf16[3,72,2176]{2,1,0:T(8,128)(2,1)}, bf16[3,72,2176]{2,1,0:T(8,128)(2,1)}, u32[]{:S(2)}, u32[]{:S(2)}) collective-permute-start(bf16[3,72,2176]{2,1,0:T(8,128)(2,1)} %pad_maximum_fusion.6.own), channel_id=1, source_target_pairs={{0,2},{1,3},{2,0},{3,1},{4,6},{5,7},{6,4},{7,5},{8,10},{9,11},{10,... | collective-permute-start | bytes 2820104 | tf_op jit(solution)/shard_map/ppermute | solution.py:172
  152.2 29.5 %collective-permute-start.19 = (bf16[3,72,1408]{2,1,0:T(8,128)(2,1)}, bf16[3,72,1408]{2,1,0:T(8,128)(2,1)S(1)}, u32[]{:S(2)}, u32[]{:S(2)}) collective-permute-start(bf16[3,72,1408]{2,1,0:T(8,128)(2,1)} %slice.307), channel_id=1, source_target_pairs={{0,1},{1,0},{2,3},{3,2},{4,5},{5,4},{6,7},{7,6},{8,9},{9,8},{10,11... | collective-permute-start | bytes 1824776 | tf_op jit(solution)/shard_map/ppermute | solution.py:172
  155.1 27.4 %collective-permute-start.20 = (bf16[3,72,1408]{2,1,0:T(8,128)(2,1)}, bf16[3,72,1408]{2,1,0:T(8,128)(2,1)}, u32[]{:S(2)}, u32[]{:S(2)}) collective-permute-start(bf16[3,72,1408]{2,1,0:T(8,128)(2,1)} %slice.308), channel_id=1, source_target_pairs={{0,2},{1,3},{2,0},{3,1},{4,6},{5,7},{6,4},{7,5},{8,10},{9,11},{10,... | collective-permute-start | bytes 1824776 | tf_op jit(solution)/shard_map/ppermute | solution.py:172
  181.5 37.5 %collective-permute-start.12 = (bf16[1024,576]{0,1:T(8,128)(2,1)}, bf16[1024,576]{0,1:T(8,128)(2,1)}, u32[]{:S(2)}, u32[]{:S(2)}) collective-permute-start(bf16[1024,576]{0,1:T(8,128)(2,1)} %copy.168), channel_id=1, source_target_pairs={{0,4},{1,5},{2,6},{3,7},{4,0},{5,1},{6,2},{7,3},{8,12},{9,13},{10,... | collective-permute-start | bytes 3538952 | tf_op jit(solution)/shard_map/ppermute | solution.py:172
  194.8 34.6 %collective-permute-start.21 = (bf16[1152,576]{0,1:T(8,128)(2,1)}, bf16[1152,576]{0,1:T(8,128)(2,1)}, u32[]{:S(2)}, u32[]{:S(2)}) collective-permute-start(bf16[1152,576]{0,1:T(8,128)(2,1)} %copy.194), channel_id=1, source_target_pairs={{0,4},{1,5},{2,6},{3,7},{4,0},{5,1},{6,2},{7,3},{8,12},{9,13},{10,... | collective-permute-start | bytes 3981320 | tf_op jit(solution)/shard_map/ppermute | solution.py:172
  197.1 14.5 %collective-permute-start.33 = (bf16[256,1152]{1,0:T(8,128)(2,1)}, bf16[256,1152]{1,0:T(8,128)(2,1)S(1)}, u32[]{:S(2)}, u32[]{:S(2)}) collective-permute-start(bf16[256,1152]{1,0:T(8,128)(2,1)} %get-tuple-element.105), channel_id=1, source_target_pairs={{0,0},{1,1},{2,4},{3,5},{4,2},{5,3},{6,6},{7,7},{8,8},{9,9},{10,12... | collective-permute-start | bytes 1769480 | tf_op jit(solution)/shard_map/ppermute | solution.py:172
  199.3 15.2 %collective-permute-start.34 = (bf16[256,1152]{1,0:T(8,128)(2,1)}, bf16[256,1152]{1,0:T(8,128)(2,1)S(1)}, u32[]{:S(2)}, u32[]{:S(2)}) collective-permute-start(bf16[256,1152]{1,0:T(8,128)(2,1)} %get-tuple-element.106), channel_id=1, source_target_pairs={{0,1},{1,0},{2,5},{3,4},{4,3},{5,2},{6,7},{7,6},{8,9},{9,8},{10,13... | collective-permute-start | bytes 1769480 | tf_op jit(solution)/shard_map/ppermute | solution.py:172
  207.3 18.9 %collective-permute-start.29 = (bf16[3,72,1152]{2,1,0:T(8,128)(2,1)}, bf16[3,72,1152]{2,1,0:T(8,128)(2,1)S(1)}, u32[]{:S(2)}, u32[]{:S(2)}) collective-permute-start(bf16[3,72,1152]{2,1,0:T(8,128)(2,1)} %slice.318), channel_id=1, source_target_pairs={{0,2},{1,3},{2,0},{3,1},{4,6},{5,7},{6,4},{7,5},{8,10},{9,11},{10,... | collective-permute-start | bytes 1493000 | tf_op jit(solution)/shard_map/ppermute | solution.py:172
  216.0 34.2 %collective-permute-start.35 = (bf16[512,1152]{1,0:T(8,128)(2,1)}, bf16[512,1152]{1,0:T(8,128)(2,1)}, u32[]{:S(2)}, u32[]{:S(2)}) collective-permute-start(bf16[512,1152]{1,0:T(8,128)(2,1)} %maximum_select_fusion.9), channel_id=1, source_target_pairs={{0,4},{1,5},{2,6},{3,7},{4,0},{5,1},{6,2},{7,3},{8,12},{9,13},{10,... | collective-permute-start | bytes 3538952 | tf_op jit(solution)/shard_map/ppermute | solution.py:172
  294.2 164.8 %collective-permute-start.36 = (bf16[1024,1152]{1,0:T(8,128)(2,1)}, bf16[1024,1152]{1,0:T(8,128)(2,1)}, u32[]{:S(2)}, u32[]{:S(2)}) collective-permute-start(bf16[1024,1152]{1,0:T(8,128)(2,1)} %get-tuple-element.135), channel_id=1, source_target_pairs={{0,4},{1,5},{2,6},{3,7},{4,0},{5,1},{6,2},{7,3},{8,12},{9,13},{10,... | collective-permute-start | bytes 7077896 | tf_op jit(solution)/shard_map/ppermute | solution.py:172
  298.7 29.1 %collective-permute-start.76 = (bf16[4,2,72,1024]{3,2,0,1:T(8,128)(2,1)}, bf16[4,2,72,1024]{3,2,0,1:T(8,128)(2,1)}, u32[]{:S(2)}, u32[]{:S(2)}) collective-permute-start(bf16[4,2,72,1024]{3,2,0,1:T(8,128)(2,1)} %bitcast.281), channel_id=1, source_target_pairs={{0,1},{1,0},{2,3},{3,2},{4,5},{5,4},{6,7},{7,6},{8,9},{9,8},{10,11... | collective-permute-start | bytes 3538952 | tf_op jit(solution)/shard_map/ppermute | solution.py:172
  302.3 56.3 %collective-permute-start.78 = (bf16[4,2,72,1152]{3,2,0,1:T(8,128)(2,1)}, bf16[4,2,72,1152]{3,2,0,1:T(8,128)(2,1)}, u32[]{:S(2)}, u32[]{:S(2)}) collective-permute-start(bf16[4,2,72,1152]{3,2,0,1:T(8,128)(2,1)} %bitcast.279), channel_id=1, source_target_pairs={{0,2},{1,3},{2,0},{3,1},{4,6},{5,7},{6,4},{7,5},{8,10},{9,11},{10,... | collective-permute-start | bytes 3981320 | tf_op jit(solution)/shard_map/ppermute | solution.py:172
  306.0 46.7 %collective-permute-start.64 = (bf16[4,2,72,1024]{3,2,0,1:T(8,128)(2,1)}, bf16[4,2,72,1024]{3,2,0,1:T(8,128)(2,1)}, u32[]{:S(2)}, u32[]{:S(2)}) collective-permute-start(bf16[4,2,72,1024]{3,2,0,1:T(8,128)(2,1)} %bitcast.282), channel_id=1, source_target_pairs={{0,1},{1,0},{2,3},{3,2},{4,5},{5,4},{6,7},{7,6},{8,9},{9,8},{10,11... | collective-permute-start | bytes 3538952 | tf_op jit(solution)/shard_map/ppermute | solution.py:172
  316.7 38.4 %collective-permute-start.30 = (bf16[512,1152]{1,0:T(8,128)(2,1)}, bf16[512,1152]{1,0:T(8,128)(2,1)}, u32[]{:S(2)}, u32[]{:S(2)}) collective-permute-start(bf16[512,1152]{1,0:T(8,128)(2,1)} %fusion.39), channel_id=1, source_target_pairs={{0,4},{1,5},{2,6},{3,7},{4,0},{5,1},{6,2},{7,3},{8,12},{9,13},{10,... | collective-permute-start | bytes 3538952 | tf_op jit(solution)/shard_map/ppermute | solution.py:172
  327.8 35.1 %collective-permute-start.66 = (bf16[4,2,72,1152]{3,2,0,1:T(8,128)(2,1)}, bf16[4,2,72,1152]{3,2,0,1:T(8,128)(2,1)S(1)}, u32[]{:S(2)}, u32[]{:S(2)}) collective-permute-start(bf16[4,2,72,1152]{3,2,0,1:T(8,128)(2,1)} %bitcast.333), channel_id=1, source_target_pairs={{0,2},{1,3},{2,0},{3,1},{4,6},{5,7},{6,4},{7,5},{8,10},{9,11},{10,... | collective-permute-start | bytes 3981320 | tf_op jit(solution)/shard_map/ppermute | solution.py:172
  352.7 29.2 %collective-permute-start.77 = (bf16[4,72,1024]{2,1,0:T(8,128)(2,1)S(1)}, bf16[4,72,1024]{2,1,0:T(8,128)(2,1)S(1)}, u32[]{:S(2)}, u32[]{:S(2)}) collective-permute-start(bf16[4,72,1024]{2,1,0:T(8,128)(2,1)S(1)} %dynamic-slice_bitcast_fusion.7), channel_id=1, source_target_pairs={{0,2},{1,3},{2,0},{3,1},{4,6},{5,7},{6,4},{7,5},{8,10},{9,11},{10,... | collective-permute-start | bytes 1769480 | tf_op jit(solution)/shard_map/ppermute | solution.py:172
  355.1 38.7 %collective-permute-start.65 = (bf16[4,72,1024]{2,1,0:T(8,128)(2,1)S(1)}, bf16[4,72,1024]{2,1,0:T(8,128)(2,1)S(1)}, u32[]{:S(2)}, u32[]{:S(2)}) collective-permute-start(bf16[4,72,1024]{2,1,0:T(8,128)(2,1)S(1)} %dynamic-slice_bitcast_fusion.8), channel_id=1, source_target_pairs={{0,2},{1,3},{2,0},{3,1},{4,6},{5,7},{6,4},{7,5},{8,10},{9,11},{10,... | collective-permute-start | bytes 1769480 | tf_op jit(solution)/shard_map/ppermute | solution.py:172
  358.6 36.4 %collective-permute-start.31 = (bf16[256,1152]{1,0:T(8,128)(2,1)S(1)}, bf16[256,1152]{1,0:T(8,128)(2,1)S(1)}, u32[]{:S(2)}, u32[]{:S(2)}) collective-permute-start(bf16[256,1152]{1,0:T(8,128)(2,1)S(1)} %get-tuple-element.107), channel_id=1, source_target_pairs={{0,0},{1,1},{2,4},{3,5},{4,2},{5,3},{6,6},{7,7},{8,8},{9,9},{10,12... | collective-permute-start | bytes 1769480 | tf_op jit(solution)/shard_map/ppermute | solution.py:172
  362.9 32.1 %collective-permute-start.32 = (bf16[256,1152]{1,0:T(8,128)(2,1)S(1)}, bf16[256,1152]{1,0:T(8,128)(2,1)S(1)}, u32[]{:S(2)}, u32[]{:S(2)}) collective-permute-start(bf16[256,1152]{1,0:T(8,128)(2,1)S(1)} %get-tuple-element.108), channel_id=1, source_target_pairs={{0,1},{1,0},{2,5},{3,4},{4,3},{5,2},{6,7},{7,6},{8,9},{9,8},{10,13... | collective-permute-start | bytes 1769480 | tf_op jit(solution)/shard_map/ppermute | solution.py:172
  381.9 17.0 %collective-permute-start.79 = (bf16[4,72,1152]{2,1,0:T(8,128)(2,1)S(1)}, bf16[4,72,1152]{2,1,0:T(8,128)(2,1)S(1)}, u32[]{:S(2)}, u32[]{:S(2)}) collective-permute-start(bf16[4,72,1152]{2,1,0:T(8,128)(2,1)S(1)} %dynamic-slice_bitcast_fusion.3), channel_id=1, source_target_pairs={{0,1},{1,0},{2,3},{3,2},{4,5},{5,4},{6,7},{7,6},{8,9},{9,8},{10,11... | collective-permute-start | bytes 1990664 | tf_op jit(solution)/shard_map/ppermute | solution.py:172
  393.8 17.8 %collective-permute-start.67 = (bf16[4,72,1152]{2,1,0:T(8,128)(2,1)S(1)}, bf16[4,72,1152]{2,1,0:T(8,128)(2,1)S(1)}, u32[]{:S(2)}, u32[]{:S(2)}) collective-permute-start(bf16[4,72,1152]{2,1,0:T(8,128)(2,1)S(1)} %dynamic-slice_bitcast_fusion.4), channel_id=1, source_target_pairs={{0,1},{1,0},{2,3},{3,2},{4,5},{5,4},{6,7},{7,6},{8,9},{9,8},{10,11... | collective-permute-start | bytes 1990664 | tf_op jit(solution)/shard_map/ppermute | solution.py:172
  399.1 20.0 %collective-permute-start.80 = (bf16[72,2176]{1,0:T(8,128)(2,1)S(1)}, bf16[72,2176]{1,0:T(8,128)(2,1)S(1)}, u32[]{:S(2)}, u32[]{:S(2)}) collective-permute-start(bf16[72,2176]{1,0:T(8,128)(2,1)S(1)} %get-tuple-element.91), channel_id=1, source_target_pairs={{0,8},{1,9},{2,10},{3,11},{4,12},{5,13},{6,14},{7,15},{8,0},{9,1},... | collective-permute-start | bytes 940040 | tf_op jit(solution)/shard_map/ppermute | solution.py:172
  407.5 23.2 %collective-permute-start.82 = (bf16[72,2176]{1,0:T(8,128)(2,1)S(1)}, bf16[72,2176]{1,0:T(8,128)(2,1)S(1)}, u32[]{:S(2)}, u32[]{:S(2)}) collective-permute-start(bf16[72,2176]{1,0:T(8,128)(2,1)S(1)} %get-tuple-element.93), channel_id=1, source_target_pairs={{0,24},{1,25},{2,26},{3,27},{4,28},{5,29},{6,30},{7,31},{8,16},{9,... | collective-permute-start | bytes 940040 | tf_op jit(solution)/shard_map/ppermute | solution.py:172
  411.8 23.4 %collective-permute-start.68 = (bf16[72,2176]{1,0:T(8,128)(2,1)S(1)}, bf16[72,2176]{1,0:T(8,128)(2,1)S(1)}, u32[]{:S(2)}, u32[]{:S(2)}) collective-permute-start(bf16[72,2176]{1,0:T(8,128)(2,1)S(1)} %get-tuple-element.94), channel_id=1, source_target_pairs={{0,8},{1,9},{2,10},{3,11},{4,12},{5,13},{6,14},{7,15},{8,0},{9,1},... | collective-permute-start | bytes 940040 | tf_op jit(solution)/shard_map/ppermute | solution.py:172
  419.1 37.5 %collective-permute-start.69 = (bf16[72,2176]{1,0:T(8,128)(2,1)S(1)}, bf16[72,2176]{1,0:T(8,128)(2,1)S(1)}, u32[]{:S(2)}, u32[]{:S(2)}) collective-permute-start(bf16[72,2176]{1,0:T(8,128)(2,1)S(1)} %get-tuple-element.95), channel_id=1, source_target_pairs={{0,16},{1,17},{2,18},{3,19},{4,20},{5,21},{6,22},{7,23},{8,24},{9,... | collective-permute-start | bytes 940040 | tf_op jit(solution)/shard_map/ppermute | solution.py:172
  420.2 36.4 %collective-permute-start.70 = (bf16[72,2176]{1,0:T(8,128)(2,1)S(1)}, bf16[72,2176]{1,0:T(8,128)(2,1)S(1)}, u32[]{:S(2)}, u32[]{:S(2)}) collective-permute-start(bf16[72,2176]{1,0:T(8,128)(2,1)S(1)} %get-tuple-element.96), channel_id=1, source_target_pairs={{0,24},{1,25},{2,26},{3,27},{4,28},{5,29},{6,30},{7,31},{8,16},{9,... | collective-permute-start | bytes 940040 | tf_op jit(solution)/shard_map/ppermute | solution.py:172
  430.8 120.3 %collective-permute-start.84 = (bf16[72,2176]{1,0:T(8,128)(2,1)S(1)}, bf16[72,2176]{1,0:T(8,128)(2,1)}, u32[]{:S(2)}, u32[]{:S(2)}) collective-permute-start(bf16[72,2176]{1,0:T(8,128)(2,1)S(1)} %fusion.51), channel_id=1, source_target_pairs={{0,2},{1,3},{2,0},{3,1},{4,6},{5,7},{6,4},{7,5},{8,10},{9,11},{10,... | collective-permute-start | bytes 940040 | tf_op jit(solution)/shard_map/ppermute | solution.py:172
  435.2 118.3 %collective-permute-start.83 = (bf16[72,2176]{1,0:T(8,128)(2,1)S(1)}, bf16[72,2176]{1,0:T(8,128)(2,1)}, u32[]{:S(2)}, u32[]{:S(2)}) collective-permute-start(bf16[72,2176]{1,0:T(8,128)(2,1)S(1)} %fusion.51), channel_id=1, source_target_pairs={{0,1},{1,0},{2,3},{3,2},{4,5},{5,4},{6,7},{7,6},{8,9},{9,8},{10,11... | collective-permute-start | bytes 940040 | tf_op jit(solution)/shard_map/ppermute | solution.py:172
  457.5 98.9 %collective-permute-start.72 = (bf16[72,2176]{1,0:T(8,128)(2,1)}, bf16[72,2176]{1,0:T(8,128)(2,1)}, u32[]{:S(2)}, u32[]{:S(2)}) collective-permute-start(bf16[72,2176]{1,0:T(8,128)(2,1)} %fusion.54), channel_id=1, source_target_pairs={{0,2},{1,3},{2,0},{3,1},{4,6},{5,7},{6,4},{7,5},{8,10},{9,11},{10,... | collective-permute-start | bytes 940040 | tf_op jit(solution)/shard_map/ppermute | solution.py:172
  457.9 100.4 %collective-permute-start.71 = (bf16[72,2176]{1,0:T(8,128)(2,1)}, bf16[72,2176]{1,0:T(8,128)(2,1)}, u32[]{:S(2)}, u32[]{:S(2)}) collective-permute-start(bf16[72,2176]{1,0:T(8,128)(2,1)} %fusion.54), channel_id=1, source_target_pairs={{0,1},{1,0},{2,3},{3,2},{4,5},{5,4},{6,7},{7,6},{8,9},{9,8},{10,11... | collective-permute-start | bytes 940040 | tf_op jit(solution)/shard_map/ppermute | solution.py:172
  545.8 14.5 %collective-permute-start.52 = (bf16[4,2,72,256]{3,2,0,1:T(8,128)(2,1)S(1)}, bf16[4,2,72,256]{3,2,0,1:T(8,128)(2,1)S(1)}, u32[]{:S(2)}, u32[]{:S(2)}) collective-permute-start(bf16[4,2,72,256]{3,2,0,1:T(8,128)(2,1)S(1)} %bitcast.345), channel_id=1, source_target_pairs={{0,1},{1,0},{2,3},{3,2},{4,5},{5,4},{6,7},{7,6},{8,9},{9,8},{10,11... | collective-permute-start | bytes 884744 | tf_op jit(solution)/shard_map/ppermute | solution.py:172
  551.1 109.4 %collective-permute-start.37 = (bf16[512,1152]{1,0:T(8,128)(2,1)}, bf16[512,1152]{1,0:T(8,128)(2,1)}, u32[]{:S(2)}, u32[]{:S(2)}) collective-permute-start(bf16[512,1152]{1,0:T(8,128)(2,1)} %fusion.40), channel_id=1, source_target_pairs={{0,4},{1,5},{2,6},{3,7},{4,0},{5,1},{6,2},{7,3},{8,12},{9,13},{10,... | collective-permute-start | bytes 3538952 | tf_op jit(solution)/shard_map/ppermute | solution.py:172
  553.6 35.2 %collective-permute-start.54 = (bf16[4,2,72,384]{3,2,1,0:T(8,128)(2,1)S(1)}, bf16[4,2,72,384]{3,2,1,0:T(8,128)(2,1)S(1)}, u32[]{:S(2)}, u32[]{:S(2)}) collective-permute-start(bf16[4,2,72,384]{3,2,1,0:T(8,128)(2,1)S(1)} %dynamic-slice_bitcast_fusion.20), channel_id=1, source_target_pairs={{0,2},{1,3},{2,0},{3,1},{4,6},{5,7},{6,4},{7,5},{8,10},{9,11},{10,... | collective-permute-start | bytes 1327112 | tf_op jit(solution)/shard_map/ppermute | solution.py:172
  556.3 80.8 %collective-permute-start.40 = (bf16[4,2,72,768]{3,2,0,1:T(8,128)(2,1)S(1)}, bf16[4,2,72,768]{3,2,0,1:T(8,128)(2,1)S(1)}, u32[]{:S(2)}, u32[]{:S(2)}) collective-permute-start(bf16[4,2,72,768]{3,2,0,1:T(8,128)(2,1)S(1)} %bitcast.334), channel_id=1, source_target_pairs={{0,1},{1,0},{2,3},{3,2},{4,5},{5,4},{6,7},{7,6},{8,9},{9,8},{10,11... | collective-permute-start | bytes 2654216 | tf_op jit(solution)/shard_map/ppermute | solution.py:172
  558.3 23.8 %collective-permute-start.85 = (bf16[72,1024]{1,0:T(8,128)(2,1)S(1)}, bf16[72,1024]{1,0:T(8,128)(2,1)S(1)}, u32[]{:S(2)}, u32[]{:S(2)}) collective-permute-start(bf16[72,1024]{1,0:T(8,128)(2,1)S(1)} %slice.338), channel_id=1, source_target_pairs={{0,1},{1,0},{2,3},{3,2},{4,5},{5,4},{6,7},{7,6},{8,9},{9,8},{10,11... | collective-permute-start | bytes 442376 | tf_op jit(solution)/shard_map/ppermute | solution.py:172
  560.4 23.6 %collective-permute-start.73 = (bf16[72,1024]{1,0:T(8,128)(2,1)S(1)}, bf16[72,1024]{1,0:T(8,128)(2,1)S(1)}, u32[]{:S(2)}, u32[]{:S(2)}) collective-permute-start(bf16[72,1024]{1,0:T(8,128)(2,1)S(1)} %slice.334), channel_id=1, source_target_pairs={{0,1},{1,0},{2,3},{3,2},{4,5},{5,4},{6,7},{7,6},{8,9},{9,8},{10,11... | collective-permute-start | bytes 442376 | tf_op jit(solution)/shard_map/ppermute | solution.py:172
  605.4 51.5 %collective-permute-start.42 = (bf16[4,2,72,960]{3,2,1,0:T(8,128)(2,1)}, bf16[4,2,72,960]{3,2,1,0:T(8,128)(2,1)}, u32[]{:S(2)}, u32[]{:S(2)}) collective-permute-start(bf16[4,2,72,960]{3,2,1,0:T(8,128)(2,1)} %dynamic-slice_bitcast_fusion), channel_id=1, source_target_pairs={{0,2},{1,3},{2,0},{3,1},{4,6},{5,7},{6,4},{7,5},{8,10},{9,11},{10,... | collective-permute-start | bytes 3317768 | tf_op jit(solution)/shard_map/ppermute | solution.py:172
  608.7 23.2 %collective-permute-start.74 = (bf16[72,1152]{1,0:T(8,128)(2,1)S(1)}, bf16[72,1152]{1,0:T(8,128)(2,1)S(1)}, u32[]{:S(2)}, u32[]{:S(2)}) collective-permute-start(bf16[72,1152]{1,0:T(8,128)(2,1)S(1)} %slice.335), channel_id=1, source_target_pairs={{0,2},{1,3},{2,0},{3,1},{4,6},{5,7},{6,4},{7,5},{8,10},{9,11},{10,... | collective-permute-start | bytes 497672 | tf_op jit(solution)/shard_map/ppermute | solution.py:172
  609.1 24.0 %collective-permute-start.60 = (bf16[72,640]{1,0:T(8,128)(2,1)S(1)}, bf16[72,640]{1,0:T(8,128)(2,1)S(1)}, u32[]{:S(2)}, u32[]{:S(2)}) collective-permute-start(bf16[72,640]{1,0:T(8,128)(2,1)S(1)} %fusion.91), channel_id=1, source_target_pairs={{0,2},{1,3},{2,0},{3,1},{4,6},{5,7},{6,4},{7,5},{8,10},{9,11},{10,... | collective-permute-start | bytes 276488 | tf_op jit(solution)/shard_map/ppermute | solution.py:172
  641.3 44.9 %collective-permute-start.41 = (bf16[4,72,768]{2,1,0:T(8,128)(2,1)}, bf16[4,72,768]{2,1,0:T(8,128)(2,1)}, u32[]{:S(2)}, u32[]{:S(2)}) collective-permute-start(bf16[4,72,768]{2,1,0:T(8,128)(2,1)} %dynamic-slice_bitcast_fusion.21), channel_id=1, source_target_pairs={{0,2},{1,3},{2,0},{3,1},{4,6},{5,7},{6,4},{7,5},{8,10},{9,11},{10,... | collective-permute-start | bytes 1327112 | tf_op jit(solution)/shard_map/ppermute | solution.py:172
  659.5 27.9 %collective-permute-start.43 = (bf16[4,72,960]{2,1,0:T(8,128)(2,1)}, bf16[4,72,960]{2,1,0:T(8,128)(2,1)}, u32[]{:S(2)}, u32[]{:S(2)}) collective-permute-start(bf16[4,72,960]{2,1,0:T(8,128)(2,1)} %dynamic-slice_bitcast_fusion.9), channel_id=1, source_target_pairs={{0,1},{1,0},{2,3},{3,2},{4,5},{5,4},{6,7},{7,6},{8,9},{9,8},{10,11... | collective-permute-start | bytes 1658888 | tf_op jit(solution)/shard_map/ppermute | solution.py:172
  689.5 21.0 %collective-permute-start.45 = (bf16[72,1728]{1,0:T(8,128)(2,1)S(1)}, bf16[72,1728]{1,0:T(8,128)(2,1)S(1)}, u32[]{:S(2)}, u32[]{:S(2)}) collective-permute-start(bf16[72,1728]{1,0:T(8,128)(2,1)S(1)} %get-tuple-element.112), channel_id=1, source_target_pairs={{0,16},{1,17},{2,18},{3,19},{4,20},{5,21},{6,22},{7,23},{8,24},{9,... | collective-permute-start | bytes 746504 | tf_op jit(solution)/shard_map/ppermute | solution.py:172
  691.6 18.9 %collective-permute-start.46 = (bf16[72,1728]{1,0:T(8,128)(2,1)S(1)}, bf16[72,1728]{1,0:T(8,128)(2,1)S(1)}, u32[]{:S(2)}, u32[]{:S(2)}) collective-permute-start(bf16[72,1728]{1,0:T(8,128)(2,1)S(1)} %get-tuple-element.113), channel_id=1, source_target_pairs={{0,24},{1,25},{2,26},{3,27},{4,28},{5,29},{6,30},{7,31},{8,16},{9,... | collective-permute-start | bytes 746504 | tf_op jit(solution)/shard_map/ppermute | solution.py:172
  694.9 32.7 %collective-permute-start.38 = (bf16[256,1152]{1,0:T(8,128)(2,1)}, bf16[256,1152]{1,0:T(8,128)(2,1)S(1)}, u32[]{:S(2)}, u32[]{:S(2)}) collective-permute-start(bf16[256,1152]{1,0:T(8,128)(2,1)} %get-tuple-element.103), channel_id=1, source_target_pairs={{0,0},{1,1},{2,4},{3,5},{4,2},{5,3},{6,6},{7,7},{8,8},{9,9},{10,12... | collective-permute-start | bytes 1769480 | tf_op jit(solution)/shard_map/ppermute | solution.py:172
  697.6 30.0 %collective-permute-start.39 = (bf16[256,1152]{1,0:T(8,128)(2,1)}, bf16[256,1152]{1,0:T(8,128)(2,1)S(1)}, u32[]{:S(2)}, u32[]{:S(2)}) collective-permute-start(bf16[256,1152]{1,0:T(8,128)(2,1)} %get-tuple-element.104), channel_id=1, source_target_pairs={{0,1},{1,0},{2,5},{3,4},{4,3},{5,2},{6,7},{7,6},{8,9},{9,8},{10,13... | collective-permute-start | bytes 1769480 | tf_op jit(solution)/shard_map/ppermute | solution.py:172
  (111 other events, 1289.4 us)

commit v2 on v1

--- a/solution.py
+++ b/solution.py
@@ -50,31 +50,32 @@
 
     @pl.when(head == heads - 1)
     def _():
-        out_ref[...] = out_rows[...].T.astype(BF16)
+        out_ref[:, :width] = out_rows[...].T.astype(BF16)
 
 
 def attention_forward(qkv, bias, block=QBLOCK):
     seq, triple = qkv.shape
     width = triple // 3
     heads = width // HEAD_DIM
+    whole_tiles = -(-width // LANES) * LANES
     return pl.pallas_call(
         functools.partial(attention_forward_kernel, block, heads),
         grid=(heads,),
         in_specs=[pl.BlockSpec((seq, triple), lambda h: (0, 0)), pl.BlockSpec((seq, 1), lambda h: (0, 0))],
         out_specs=[
-            pl.BlockSpec((seq, width), lambda h: (0, 0)),
+            pl.BlockSpec((seq, whole_tiles), lambda h: (0, 0)),
             pl.BlockSpec((1, seq, seq), lambda h: (h, 0, 0)),
             pl.BlockSpec((1, 1, seq), lambda h: (h, 0, 0)),
         ],
         out_shape=[
-            jax.ShapeDtypeStruct((seq, width), BF16),
+            jax.ShapeDtypeStruct((seq, whole_tiles), BF16),
             jax.ShapeDtypeStruct((heads, seq, seq), BF16),
             jax.ShapeDtypeStruct((heads, 1, seq), F32),
         ],
         scratch_shapes=[pltpu.VMEM((triple, seq), F32), pltpu.VMEM((width, seq), F32)],
         compiler_params=pltpu.CompilerParams(vmem_limit_bytes=48 * MIB),
         cost_estimate=pl.CostEstimate(
-            flops=10 * heads * seq * seq * 256, bytes_accessed=2 * heads * seq * seq, transcendentals=heads * seq * seq
+            flops=heads * seq * seq, bytes_accessed=seq * triple, transcendentals=0
         ),
     )(qkv, bias)
 
@@ -91,7 +92,7 @@
     def _():
         by_row[...] = qkv_ref[...].astype(F32).T
         d_rows[...] = d_out_ref[...].astype(F32).T
-        o_rows[...] = out_ref[...].astype(F32).T
+        o_rows[...] = out_ref[:, :width].astype(F32).T
 
     def rows(which):
         return pl.ds(pl.multiple_of(which * width + head * HEAD_DIM, 8), HEAD_DIM)
@@ -134,7 +135,7 @@
         in_specs=[
             pl.BlockSpec((seq, triple), whole),
             pl.BlockSpec((seq, width), whole),
-            pl.BlockSpec((seq, width), whole),
+            pl.BlockSpec(out.shape, whole),
             pl.BlockSpec((1, seq, seq), lambda h: (h, 0, 0)),
             pl.BlockSpec((1, 1, seq), lambda h: (h, 0, 0)),
         ],
@@ -148,7 +149,7 @@
         ],
         compiler_params=pltpu.CompilerParams(vmem_limit_bytes=56 * MIB),
         cost_estimate=pl.CostEstimate(
-            flops=12 * heads * seq * seq * 256, bytes_accessed=2 * heads * seq * seq, transcendentals=0
+            flops=heads * seq * seq, bytes_accessed=seq * triple, transcendentals=0
         ),
     )(qkv, d_out, out, probs, inv)
 
@@ -160,6 +161,8 @@
         k = lax.axis_index("seq")
         self.z, self.c = f // 2, f % 2
         self.k, self.y, self.x = k, k // 2, k % 2
+        self.z_lines = [[2 * z + c for z in range(self.planes)] for c in range(2)]
+        self.spot = jnp.stack([self.c, self.z, self.y, self.x, self.k]).astype(jnp.int32)
 
     def send(self, value, to):
         pairs = []
@@ -186,12 +189,11 @@
     def along_z(self, value, step):
         return self.send(value, lambda z, c, y, x: (z ^ step, c, y, x))
 
+    def over_z(self, value):
+        return lax.all_to_all(value, "fsdp", 0, 0, axis_index_groups=self.z_lines, tiled=True)
+
     def turn(self, value, step):
         return self.send(value, lambda z, c, y, x: (z, y, c, x ^ step))
-
-
-def after(value, *others):
-    return lax.optimization_barrier((value, *others))[0]
 
 
 def pick(stack, index):
@@ -205,48 +207,94 @@
 def to_image(place, parts):
     near = place.turn(pick(parts, place.x), 0)
     far = place.turn(pick(parts, 1 - place.x), 1)
-    return in_order(place.x, near, far)
+    near, far = yield near, far
+    half = jnp.concatenate([near, far])
+    half, other = yield half, place.core(half)
+    return half, other
+
+
+def image_order(place, row):
+    blocks = row.reshape(4, -1)
+    first = 2 * place.c + place.x
+    return jnp.concatenate([pick(blocks, first ^ i) for i in range(4)])
 
 
 def from_image(place, half):
-    parts = half.reshape(2, half.shape[0] // 2, half.shape[1])
-    near = place.turn(pick(parts, place.x), 0)
-    far = place.turn(pick(parts, 1 - place.x), 1)
+    size = half.shape[0] // 2
+    near = place.turn(half[:size], 0)
+    far = place.turn(half[size:], 1)
+    near, far = yield near, far
     return in_order(place.x, near[None], far[None])
 
 
-def both_halves(place, half):
-    return in_order(place.c, half, place.core(half))
+def other_order(value):
+    size = value.shape[0] // 2
+    return jnp.concatenate([value[size:], value[:size]])
 
 
 def lane_cut(columns):
     return columns // 2 // LANES * LANES
 
 
+class Transfer:
+    def __init__(self, steps):
+        self.steps = steps
+        self.arrays = next(steps)
+        self.result = None
+
+
+def close_round(*transfers, hold=()):
+    arrays, held = lax.optimization_barrier(([transfer.arrays for transfer in transfers], list(hold)))
+    for transfer, arrived in zip(transfers, arrays):
+        try:
+            transfer.arrays = transfer.steps.send(arrived)
+        except StopIteration as end:
+            transfer.result = end.value
+    return held
+
+
 def spread(place, give, keep):
-    block = in_order(place.c, keep, place.core(give))
+    arrived = place.core(give)
+    keep, arrived = yield keep, arrived
+    block = in_order(place.c, keep, arrived)
     rows, columns = block.shape[0] // 4, block.shape[1]
     quarters = block.reshape(4, rows, columns)
     mine = pick(quarters, place.k)
-    own = jnp.stack([place.along_z(mine, step) for step in range(1, place.planes)])
+    planes = place.over_z(jnp.broadcast_to(mine[None], (place.planes, rows, columns)))
+    quarters, planes = yield quarters, planes
+    own = jnp.stack([pick(planes, place.z ^ step) for step in range(1, place.planes)])
+    x_part, y_part = place.along_x(own), place.along_y(own)
+    quarters, own, x_part, y_part = yield quarters, own, x_part, y_part
     cut = lane_cut(columns)
-    x_part = place.along_x(own)
-    y_part = place.along_y(own)
     far_low = place.along_x(y_part[:, :, :cut])
     far_high = place.along_y(x_part[:, :, cut:])
-    return assemble(place, quarters, own, x_part, y_part, far_low, far_high), own
-
-
-def assemble_kernel(planes, cut, scalars, block, own, x_part, y_part, far_low, far_high, out, sems):
-    z, k = scalars[0], scalars[1]
-    copies = [(block, out.at[pl.ds(z * 4, 4)])]
-    for step in range(1, planes):
-        at = (z ^ step) * 4
-        copies.append((own.at[step - 1], out.at[at + k]))
-        copies.append((x_part.at[step - 1], out.at[at + (k ^ 1)]))
-        copies.append((y_part.at[step - 1], out.at[at + (k ^ 2)]))
-        copies.append((far_low.at[step - 1], out.at[at + (k ^ 3), :, pl.ds(0, cut)]))
-        copies.append((far_high.at[step - 1], out.at[at + (k ^ 3), :, pl.ds(cut, out.shape[2] - cut)]))
+    pieces = yield quarters, own, x_part, y_part, far_low, far_high
+    return pieces
+
+
+def assemble_kernel(planes, spans, scalars, *refs):
+    out, sems = refs[-2:]
+    z, k = scalars[1], scalars[4]
+    copies = []
+    for i, (start, size, to, cut) in enumerate(spans):
+        block, own, x_part, y_part, far_low, far_high = refs[6 * i : 6 * i + 6]
+        here, there = pl.ds(start, size), pl.ds(to, size)
+        copies.append((block.at[:, :, here], out.at[pl.ds(z * 4, 4), :, there]))
+        for step in range(1, planes):
+            at = (z ^ step) * 4
+            copies.append((own.at[step - 1, :, here], out.at[at + k, :, there]))
+            copies.append((x_part.at[step - 1, :, here], out.at[at + (k ^ 1), :, there]))
+            copies.append((y_part.at[step - 1, :, here], out.at[at + (k ^ 2), :, there]))
+            low, high = max(0, min(start + size, cut) - start), max(0, start + size - max(start, cut))
+            if low:
+                copies.append((far_low.at[step - 1, :, pl.ds(start, low)], out.at[at + (k ^ 3), :, pl.ds(to, low)]))
+            if high:
+                copies.append(
+                    (
+                        far_high.at[step - 1, :, pl.ds(start + size - high - cut, high)],
+                        out.at[at + (k ^ 3), :, pl.ds(to + size - high, high)],
+                    )
+                )
     started = [pltpu.make_async_copy(source, target, sems.at[i]) for i, (source, target) in enumerate(copies)]
     for copy in started:
         copy.start()
@@ -254,77 +302,435 @@
         copy.wait()
 
 
-def assemble(place, block, own, x_part, y_part, far_low, far_high):
-    rows, columns = block.shape[1:]
+def assemble(place, *parts):
     planes = place.planes
+    rows = parts[0][0][0].shape[1]
+    spans, to, operands = [], 0, []
+    for pieces, start, size in parts:
+        spans.append((start, size, to, lane_cut(pieces[0].shape[2])))
+        operands += list(pieces)
+        to += size
     anywhere = pl.BlockSpec(memory_space=pl.ANY)
     out = pl.pallas_call(
-        functools.partial(assemble_kernel, planes, lane_cut(columns)),
-        in_specs=[pl.BlockSpec(memory_space=pltpu.SMEM)] + [anywhere] * 6,
+        functools.partial(assemble_kernel, planes, spans),
+        in_specs=[pl.BlockSpec(memory_space=pltpu.SMEM)] + [anywhere] * len(operands),
         out_specs=pl.BlockSpec(memory_space=pltpu.VMEM),
-        out_shape=jax.ShapeDtypeStruct((planes * 4, rows, columns), block.dtype),
-        scratch_shapes=[pltpu.SemaphoreType.DMA((1 + 5 * (planes - 1),))],
+        out_shape=jax.ShapeDtypeStruct((planes * 4, rows, to), BF16),
+        scratch_shapes=[pltpu.SemaphoreType.DMA((len(parts) * (1 + 5 * (planes - 1)),))],
         compiler_params=pltpu.CompilerParams(vmem_limit_bytes=32 * MIB),
-        cost_estimate=pl.CostEstimate(
-            flops=0, bytes_accessed=4 * planes * 4 * rows * columns, transcendentals=0
-        ),
-    )(jnp.stack([place.z, place.k]).astype(jnp.int32), block, own, x_part, y_part, far_low, far_high)
-    return out.reshape(planes * 4 * rows, columns)
-
-
-def collect(place, partial):
+        cost_estimate=pl.CostEstimate(flops=0, bytes_accessed=4 * planes * 4 * rows * to, transcendentals=0),
+    )(place.spot, *operands)
+    return out.reshape(planes * 4 * rows, to)
+
+
+def whole_spec():
+    return pl.BlockSpec(memory_space=pltpu.VMEM)
+
+
+def scalar_spec():
+    return pl.BlockSpec(memory_space=pltpu.SMEM)
+
+
+def vmem(mib):
+    return pltpu.CompilerParams(vmem_limit_bytes=mib * MIB)
+
+
+def join_kernel(turn, where, mine, other, out):
+    rows, width = out.shape[0], out.shape[1] // 2
+    half = rows // 2
+
+    for core in range(2):
+
+        @pl.when(where[0] == core)
+        def _():
+            out[:, core * width : (core + 1) * width] = mine[:, :width]
+            low, high = (1 - core) * width, (2 - core) * width
+            if turn:
+                out[:half, low:high] = other[half:, :width]
+                out[half:, low:high] = other[:half, :width]
+            else:
+                out[:, low:high] = other[:, :width]
+
+
+def join(place, mine, other, width, turn):
+    return pl.pallas_call(
+        functools.partial(join_kernel, turn),
+        in_specs=[scalar_spec(), whole_spec(), whole_spec()],
+        out_specs=whole_spec(),
+        out_shape=jax.ShapeDtypeStruct((mine.shape[0], 2 * width), BF16),
+        compiler_params=vmem(24),
+    )(place.spot, mine, other)
+
+
+def weight_grad_kernel(cut, group, rows, pair_count, with_riders, with_sums, where, *refs):
+    lefts, rights, refs = refs[:pair_count], refs[pair_count : 2 * pair_count], refs[2 * pair_count :]
+    riders, refs = (refs[0], refs[1:]) if with_riders else (None, refs)
+    low_keep, low_send, high_keep, high_send, *refs = refs
+    sums, refs = (refs[0], refs[1:]) if with_sums else (None, refs)
+    total, *turned = refs
+    step = pl.program_id(0)
+    y, x = where[2], where[3]
+    block = group * 4 * rows
+
+    @pl.when(step == 0)
+    def _():
+        for left, by_row in zip(lefts, turned):
+            by_row[...] = left[...].astype(F32).T.astype(BF16)
+        if with_sums:
+            sums[...] = jnp.broadcast_to(jnp.sum(rights[0][...].astype(F32), axis=0, keepdims=True), sums.shape)
+
+    at = 0
+    for right, by_row in zip(rights, turned):
+        left = by_row[pl.ds(pl.multiple_of(step * block, 16), block), :]
+        columns = right.shape[1]
+        for start in range(0, columns, 4 * LANES):
+            end = min(start + 4 * LANES, columns)
+            total[:, at + start : at + end] = jnp.dot(left, right[:, start:end], preferred_element_type=F32)
+        at += columns
+    if with_riders:
+        total[:, at:] = riders[...]
+    for plane in range(group):
+        for dy in range(2):
+            for dx in range(2):
+                row = (plane * 4 + (y ^ dy) * 2 + (x ^ dx)) * rows
+                part = total[pl.ds(pl.multiple_of(row, 8), rows), :].astype(BF16)
+                (low_send if dx else low_keep)[dy, plane] = part[:, :cut]
+                (high_send if dy else high_keep)[dx, plane] = part[:, cut:]
+
+
+def weight_grad(place, pairs, riders=None, with_sums=False):
     planes = place.planes
-    columns = partial.shape[1]
-    rows = partial.shape[0] // planes // 4
+    tokens, width = pairs[0][0].shape
+    rows = width // planes // 4
+    group = 2
+    columns = sum(right.shape[1] for _, right in pairs) + (0 if riders is None else riders.shape[1])
+    rider_list = [] if riders is None else [riders]
     cut = lane_cut(columns)
-    parts = partial.reshape(planes, 2, 2, rows, columns)
-    low, high = parts[..., :cut], parts[..., cut:]
-
-    def take(value, axis, index):
-        return lax.dynamic_index_in_dim(value, index, axis, keepdims=False)
-
-    def add(mine, arrived):
-        return (mine.astype(F32) + arrived.astype(F32)).astype(BF16)
-
-    low = add(take(low, 2, place.x), place.along_x(take(low, 2, 1 - place.x)))
-    high = add(take(high, 1, place.y), place.along_y(take(high, 1, 1 - place.y)))
-    low = add(take(low, 1, place.y), place.along_y(take(low, 1, 1 - place.y)))
-    high = add(take(high, 1, place.x), place.along_x(take(high, 1, 1 - place.x)))
-    plane = jnp.concatenate([low, high], axis=-1)
-    total = pick(plane, place.z).astype(F32)
-    for step in range(1, planes):
-        total = total + place.along_z(pick(plane, place.z ^ step), step).astype(F32)
-    mine = total.astype(BF16)
-    x_part = place.along_x(mine)
-    y_part = place.along_y(mine)
-    far = jnp.concatenate([place.along_x(y_part[:, :cut]), place.along_y(x_part[:, cut:])], axis=-1)
-    near_pair = in_order(place.x, mine, x_part)
-    far_pair = in_order(place.x, y_part, far)
-    matches = place.y == place.c
-    keep = jnp.where(matches, near_pair, far_pair)
-    give = jnp.where(matches, far_pair, near_pair)
-    return keep, place.core(give)
-
-
-def sum_chips(place, value):
-    value = value + place.along_x(value) + place.along_y(value) + place.across(value)
-    total = value
-    for step in range(1, place.planes):
-        total = total + place.along_z(value, step)
-    return total
-
-
-def own_columns(place, rows_of_columns):
-    n, width = rows_of_columns.shape
-    size = width // lax.axis_size("fsdp")
-    return lax.dynamic_slice_in_dim(rows_of_columns, lax.axis_index("fsdp") * size, size, axis=1)
-
-
-def norm_stats(values):
+    still = lambda shape: pl.BlockSpec(shape, lambda i: (0, 0), pipeline_mode=pl.Buffered(1))
+    low = jax.ShapeDtypeStruct((2, planes, rows, cut), BF16)
+    high = jax.ShapeDtypeStruct((2, planes, rows, columns - cut), BF16)
+    low_spec = pl.BlockSpec((2, group, rows, cut), lambda i: (0, i, 0, 0))
+    high_spec = pl.BlockSpec((2, group, rows, columns - cut), lambda i: (0, i, 0, 0))
+    sum_shapes = [jax.ShapeDtypeStruct((8, pairs[0][1].shape[1]), F32)] if with_sums else []
+    return pl.pallas_call(
+        functools.partial(weight_grad_kernel, cut, group, rows, len(pairs), riders is not None, with_sums),
+        grid=(planes // group,),
+        in_specs=[scalar_spec()]
+        + [still(left.shape) for left, _ in pairs]
+        + [still(right.shape) for _, right in pairs]
+        + [pl.BlockSpec((group * 4 * rows, extra.shape[1]), lambda i: (i, 0)) for extra in rider_list],
+        out_specs=[low_spec, low_spec, high_spec, high_spec] + [pl.BlockSpec(s.shape, lambda i: (0, 0)) for s in sum_shapes],
+        out_shape=[low, low, high, high] + sum_shapes,
+        scratch_shapes=[pltpu.VMEM((group * 4 * rows, columns), F32)] + [pltpu.VMEM((width, tokens), BF16) for _ in pairs],
+        compiler_params=vmem(56),
+        cost_estimate=pl.CostEstimate(flops=tokens * width, bytes_accessed=width * columns, transcendentals=0),
+    )(place.spot, *[left for left, _ in pairs], *[right for _, right in pairs], *rider_list)
+
+
+def add_first_kernel(low, from_x, high, from_y, low_keep, low_send, high_keep, high_send):
+    for kept, arrived, outs in ((low, from_x, (low_keep, low_send)), (high, from_y, (high_keep, high_send))):
+        for i, out in enumerate(outs):
+            out[...] = (kept[i].astype(F32) + arrived[i].astype(F32)).astype(BF16)
+
+
+def add_first(low, from_x, high, from_y):
+    planes = low.shape[1]
+    ins = lambda a: pl.BlockSpec((2, 1, *a.shape[2:]), lambda i: (0, i, 0, 0))
+    out = lambda a: pl.BlockSpec((1, *a.shape[2:]), lambda i: (i, 0, 0))
+    shape = lambda a: jax.ShapeDtypeStruct(a.shape[1:], BF16)
+    return pl.pallas_call(
+        add_first_kernel,
+        grid=(planes,),
+        in_specs=[ins(low), ins(from_x), ins(high), ins(from_y)],
+        out_specs=[out(low), out(low), out(high), out(high)],
+        out_shape=[shape(low), shape(low), shape(high), shape(high)],
+        compiler_params=vmem(24),
+    )(low, from_x, high, from_y)
+
+
+def add_second_kernel(low, from_y, high, from_x, out):
+    cut = low.shape[2]
+    out[:, :, :cut] = (low[...].astype(F32) + from_y[...].astype(F32)).astype(BF16)
+    out[:, :, cut:] = (high[...].astype(F32) + from_x[...].astype(F32)).astype(BF16)
+
+
+def add_second(low, from_y, high, from_x):
+    planes, rows, cut = low.shape
+    spec = lambda columns: pl.BlockSpec((1, rows, columns), lambda i: (i, 0, 0))
+    rest = high.shape[2]
+    return pl.pallas_call(
+        add_second_kernel,
+        grid=(planes,),
+        in_specs=[spec(cut), spec(cut), spec(rest), spec(rest)],
+        out_specs=spec(cut + rest),
+        out_shape=jax.ShapeDtypeStruct((planes, rows, cut + rest), BF16),
+        compiler_params=vmem(24),
+    )(low, from_y, high, from_x)
+
+
+def quarter_of(where, parts, core, side, store):
+    mine, x_part, y_part, far_low, far_high = parts
+    near, same = where[2] == core, where[3] == side
+
+    @pl.when(near & same)
+    def _():
+        store(mine[...])
+
+    @pl.when(near & ~same)
+    def _():
+        store(x_part[...])
+
+    @pl.when(~near & same)
+    def _():
+        store(y_part[...])
+
+    @pl.when(~near & ~same)
+    def _():
+        store(jnp.concatenate([far_low[...], far_high[...]], axis=1))
+
+
+def give_kernel(where, *refs):
+    out = refs[-1]
+    for core in range(2):
+
+        @pl.when(where[0] != core)
+        def _():
+            for side in range(2):
+
+                def store(value):
+                    out[side] = value
+
+                quarter_of(where, refs[:-1], core, side, store)
+
+
+def give_rows(place, parts):
+    rows, columns = parts[0].shape
+    return pl.pallas_call(
+        give_kernel,
+        in_specs=[scalar_spec()] + [whole_spec()] * 5,
+        out_specs=whole_spec(),
+        out_shape=jax.ShapeDtypeStruct((2, rows, columns), BF16),
+        compiler_params=vmem(24),
+    )(place.spot, *parts)
+
+
+def finish_kernel(write, where, *refs):
+    parts, arrived = refs[:5], refs[5]
+    outs, kept = refs[6:-1], refs[-1]
+    for core in range(2):
+
+        @pl.when(where[0] == core)
+        def _():
+            for side in range(2):
+
+                def store(value):
+                    kept[side] = value
+
+                quarter_of(where, parts, core, side, store)
+            halves = [kept[...], arrived[...]]
+            if core:
+                halves = halves[::-1]
+            lower, higher = (half.astype(F32).reshape(-1, half.shape[2]) for half in halves)
+            write(lower, higher, *outs)
+
+
+def lay_kernel(write, where, mine, other, out):
+    for core in range(2):
+
+        @pl.when(where[0] == core)
+        def _():
+            halves = [mine[...].astype(F32), other[...].astype(F32)]
+            if core:
+                halves = halves[::-1]
+            write(*halves, out)
+
+
+def lay(place, mine, other, write, shape):
+    return pl.pallas_call(
+        functools.partial(lay_kernel, write),
+        in_specs=[scalar_spec()] + [whole_spec()] * 2,
+        out_specs=whole_spec(),
+        out_shape=jax.ShapeDtypeStruct(shape, F32),
+        compiler_params=vmem(24),
+    )(place.spot, mine, other)
+
+
+def finish(place, pieces, write, shapes):
+    *parts, arrived = pieces
+    return pl.pallas_call(
+        functools.partial(finish_kernel, write),
+        in_specs=[scalar_spec()] + [whole_spec()] * 6,
+        out_specs=[whole_spec()] * len(shapes),
+        out_shape=[jax.ShapeDtypeStruct(shape, F32) for shape in shapes],
+        scratch_shapes=[pltpu.VMEM(arrived.shape, BF16)],
+        compiler_params=vmem(40),
+    )(place.spot, *parts, arrived)
+
+
+def collect(place, pieces):
+    low, low_send, high, high_send = pieces
+    low, high, from_x, from_y = yield low, high, place.along_x(low_send), place.along_y(high_send)
+    low, low_send, high, high_send = add_first(low, from_x, high, from_y)
+    low, high, from_y, from_x = yield low, high, place.along_y(low_send), place.along_x(high_send)
+    cut = low.shape[2]
+    arrived = yield place.over_z(add_second(low, from_y, high, from_x))
+    mine = jnp.sum(arrived.astype(F32), axis=0).astype(BF16)
+    mine, x_part, y_part = yield mine, place.along_x(mine), place.along_y(mine)
+    far_low, far_high = place.along_x(y_part[:, :cut]), place.along_y(x_part[:, cut:])
+    parts = yield mine, x_part, y_part, far_low, far_high
+    parts, arrived = yield parts, place.core(give_rows(place, parts))
+    return (*parts, arrived)
+
+
+def first_norm_kernel(half, other, tokens, normed, inv_std):
+    size = half.shape[0]
+    for i, part in enumerate((half, other)):
+        rows = slice(i * size, (i + 1) * size)
+        values = part[...]
+        tokens[rows, :] = values
+        normed[rows, :], inv_std[rows, :] = normalize(values.astype(F32))
+
+
+def first_norm(half, other):
+    size, width = half.shape
+    return pl.pallas_call(
+        first_norm_kernel,
+        in_specs=[whole_spec()] * 2,
+        out_specs=[whole_spec()] * 3,
+        out_shape=[
+            jax.ShapeDtypeStruct((2 * size, width), BF16),
+            jax.ShapeDtypeStruct((2 * size, width), F32),
+            jax.ShapeDtypeStruct((2 * size, 1), F32),
+        ],
+        compiler_params=vmem(32),
+    )(half, other)
+
+
+def sum_plane(place, rows):
+    cut = lane_cut(rows.shape[1])
+    low, high = rows[:, :cut], rows[:, cut:]
+    low, high, from_x, from_y = yield low, high, place.along_x(low), place.along_y(high)
+    low, high = add(low, from_x), add(high, from_y)
+    low, high, from_y, from_x = yield low, high, place.along_y(low), place.along_x(high)
+    return jnp.concatenate([add(low, from_y), add(high, from_x)], axis=1)
+
+
+def sum_devices(place, value):
+    value, other = yield value, place.core(value)
+    value = value + other
+    value, others = yield value, [place.along_x(value), place.along_y(value), place.across(value)]
+    value = value + others[0] + others[1] + others[2]
+    value, others = yield value, [place.along_z(value, step) for step in range(1, place.planes)]
+    return functools.reduce(jnp.add, others, value)
+
+
+def add(mine, arrived):
+    return (mine.astype(F32) + arrived.astype(F32)).astype(BF16)
+
+
+def norm_back_kernel(half, where, part, arrived, upstream, normed, inv_std, gain, low, own_columns, own_rows, sums):
+    step = pl.program_id(0)
+    e = part[...] + arrived[...].astype(F32)
+    n = normed[...].astype(F32)
+    scaled = e * gain[...]
+    first_mean = jnp.mean(scaled, axis=-1, keepdims=True)
+    second_mean = jnp.mean(scaled * n, axis=-1, keepdims=True)
+    cot = upstream[...].astype(F32)
+    d = cot + inv_std[...] * (scaled - first_mean - n * second_mean)
+    d_low = d.astype(BF16)
+    low[...] = d_low
+    for core in range(2):
+
+        @pl.when(where[0] == core)
+        def _():
+            own_columns[...] = d_low[:, core * half : (core + 1) * half]
+
+    @pl.when(step < pl.num_programs(0) // 2)
+    def _():
+        own_rows[...] = d
+
+    rows = jnp.concatenate([jnp.sum(v, axis=0, keepdims=True) for v in (e * n, e, d, cot)] + [jnp.zeros((4, e.shape[1]), F32)])
+
+    @pl.when(step == 0)
+    def _():
+        sums[...] = rows
+
+    @pl.when(step > 0)
+    def _():
+        sums[...] += rows
+
+
+def norm_back_second(place, part, arrived, upstream, normed, inv_std, gain):
+    tokens, width = part.shape
+    size = tokens // 8
+    by_row = pl.BlockSpec((size, width), lambda i: (i, 0))
+    turned = pl.BlockSpec((size, width), lambda i: ((i + 4) % 8, 0))
+    return pl.pallas_call(
+        functools.partial(norm_back_kernel, width // 2),
+        grid=(8,),
+        in_specs=[
+            scalar_spec(),
+            by_row,
+            turned,
+            by_row,
+            by_row,
+            pl.BlockSpec((size, 1), lambda i: (i, 0)),
+            pl.BlockSpec((1, width), lambda i: (0, 0)),
+        ],
+        out_specs=[
+            by_row,
+            pl.BlockSpec((size, width // 2), lambda i: (i, 0)),
+            pl.BlockSpec((size, width), lambda i: (jnp.minimum(i, 3), 0)),
+            pl.BlockSpec((8, width), lambda i: (0, 0)),
+        ],
+        out_shape=[
+            jax.ShapeDtypeStruct((tokens, width), BF16),
+            jax.ShapeDtypeStruct((tokens, width // 2), BF16),
+            jax.ShapeDtypeStruct((tokens // 2, width), F32),
+            jax.ShapeDtypeStruct((8, width), F32),
+        ],
+        compiler_params=vmem(24),
+    )(place.spot, part, arrived, upstream, normed, inv_std, gain)
+
+
+def norm_back_first_kernel(part, arrived, d_resid, normed, inv_std, gain, grad, sums):
+    e = part[...] + arrived[...].astype(F32)
+    n = normed[...].astype(F32)
+    scaled = e * gain[...]
+    first_mean = jnp.mean(scaled, axis=-1, keepdims=True)
+    second_mean = jnp.mean(scaled * n, axis=-1, keepdims=True)
+    grad[...] = (d_resid[...] + inv_std[...] * (scaled - first_mean - n * second_mean)).astype(BF16)
+    rows = jnp.concatenate([jnp.sum(v, axis=0, keepdims=True) for v in (e * n, e)] + [jnp.zeros((6, e.shape[1]), F32)])
+
+    @pl.when(pl.program_id(0) == 0)
+    def _():
+        sums[...] = rows
+
+    @pl.when(pl.program_id(0) > 0)
+    def _():
+        sums[...] += rows
+
+
+def norm_back_first(part, arrived, d_resid, normed, inv_std, gain):
+    tokens, width = arrived.shape
+    size = tokens // 4
+    by_row = pl.BlockSpec((size, width), lambda i: (i, 0))
+    return pl.pallas_call(
+        norm_back_first_kernel,
+        grid=(4,),
+        in_specs=[by_row] * 4 + [pl.BlockSpec((size, 1), lambda i: (i, 0)), pl.BlockSpec((1, width), lambda i: (0, 0))],
+        out_specs=[by_row, pl.BlockSpec((8, width), lambda i: (0, 0))],
+        out_shape=[jax.ShapeDtypeStruct((tokens, width), BF16), jax.ShapeDtypeStruct((8, width), F32)],
+        compiler_params=vmem(24),
+    )(part, arrived, d_resid, normed, inv_std, gain)
+
+
+def normalize(values):
     row_mean = jnp.mean(values, axis=-1, keepdims=True)
     centred = values - row_mean
     variance = jnp.mean(centred * centred, axis=-1, keepdims=True)
-    return row_mean, lax.rsqrt(variance + EPSILON)
+    inv_std = lax.rsqrt(variance + EPSILON)
+    return centred * inv_std, inv_std
 
 
 def layer_norm(values, gain_row, shift_row):
@@ -391,164 +797,161 @@
     n_small = small.shape[0]
     spare = -(3 * half_width) % LANES
     extra = jnp.pad(small.T, ((0, 0), (0, spare - n_small)))
+    c = place.c
+
     qkv_halves = halves_qkv(w_qkv)
-    give = jnp.concatenate([pick(qkv_halves, 1 - place.c), extra], axis=1)
-    keep = jnp.concatenate([pick(qkv_halves, place.c), extra], axis=1)
-
-    tokens = both_halves(place, to_image(place, inputs))
-    full_first, own_first = spread(place, give, keep)
+    give = jnp.concatenate([pick(qkv_halves, 1 - c), extra], axis=1)
+    keep = jnp.concatenate([pick(qkv_halves, c), extra], axis=1)
+    qkv = Transfer(spread(place, give, keep))
+    tokens_in = Transfer(to_image(place, inputs))
+    other_mask = place.core(key_mask)
+    w_out, w_up, w_down = close_round(qkv, hold=(w_out, w_up, w_down))
+
+    out_pad = -half_width % LANES
+    out_cols = half_width + out_pad
+    out_halves = jnp.pad(jnp.moveaxis(w_out.reshape(shard, 2, half_width), 1, 0), ((0, 0), (0, 0), (0, out_pad)))
+    down_halves = halves_hidden(w_down.T)
+    down = Transfer(spread(place, pick(down_halves, 1 - c), pick(down_halves, c)))
+    rest = jnp.concatenate([out_halves, halves_hidden(w_up)], axis=2)
+    out_up = Transfer(spread(place, pick(rest, 1 - c), pick(rest, c)))
+    close_round(qkv, tokens_in, out_up)
+    close_round(qkv, tokens_in)
+
+    live_keys = image_order(place, pick(jnp.where(c == place.y, key_mask, other_mask), place.x))
+    mask_bias = jnp.where(live_keys > 0, 0.0, NEG_FILL).astype(F32)[:, None]
+    tokens, first_normed, first_inv = first_norm(*tokens_in.result)
+    (first_normed,) = close_round(qkv, out_up, down, hold=(first_normed,))
+
+    full_first = assemble(place, (qkv.result, 0, 3 * half_width + spare))
     full_qkv = full_first[:, : 3 * half_width]
     small_rows = full_first[:, 3 * half_width : 3 * half_width + n_small].astype(F32).T
     gain_rows, bias_rows = small_rows[:2], small_rows[2:8]
     up_shift = (
         small_rows[8:].reshape(up_cols, fsdp, shard).transpose(1, 0, 2).reshape(fsdp, up_cols * shard)[:, :up_shard]
     ).reshape(hidden)
-    up_shift = pick(jnp.pad(up_shift, (0, 2 * half_hidden - hidden)).reshape(2, half_hidden), place.c)
-
-    out_halves = jnp.moveaxis(w_out.reshape(shard, 2, half_width), 1, 0)
-    up_halves = halves_hidden(w_up)
-    down_halves = halves_hidden(w_down.T)
-    out_up = jnp.concatenate([up_halves, jnp.pad(out_halves, ((0, 0), (0, 0), (0, -half_width % LANES)))], axis=2)
-    out_up = after(out_up, own_first)
-    full_out_up, own_out_up = spread(place, pick(out_up, 1 - place.c), pick(out_up, place.c))
-    full_up = full_out_up[:, :half_hidden]
-    half_out = full_out_up[:, half_hidden : half_hidden + half_width]
-    other_out = place.core(half_out)
-    full_out = jnp.where(
-        place.c == 0,
-        jnp.concatenate([half_out, other_out], axis=1),
-        jnp.concatenate([other_out, half_out], axis=1),
-    )
-    down_halves = after(down_halves, own_out_up)
-    full_down, _ = spread(place, pick(down_halves, 1 - place.c), pick(down_halves, place.c))
-    upstream = both_halves(place, to_image(place, after(cotangent, full_first)))
-
-    other_mask = place.core(key_mask)
-    live = pick(jnp.where(place.c == place.y, key_mask, other_mask), place.x)
-    mask_bias = jnp.where(live > 0, 0.0, NEG_FILL).astype(F32)[:, None]
-
+    up_shift = pick(jnp.pad(up_shift, (0, 2 * half_hidden - hidden)).reshape(2, half_hidden), c)
     shift_halves = bias_rows.reshape(6, 2, half_width)
     qkv_shift = jnp.concatenate(
-        [pick(shift_halves[2], place.c), jnp.zeros((half_width,), F32), pick(shift_halves[3], place.c)]
-    )
-    tok_wide = tokens.astype(F32)
-    first_out, first_normed, first_inv = layer_norm(tok_wide, gain_rows[0], bias_rows[0])
-    first_low = first_out.astype(BF16)
+        [pick(shift_halves[2], c), jnp.zeros((half_width,), F32), pick(shift_halves[3], c)]
+    )
+    first_low = (first_normed * gain_rows[0] + bias_rows[0]).astype(BF16)
     packed = (dot(first_low, full_qkv) + qkv_shift).astype(BF16)
+    packed, cotangent = close_round(out_up, hold=(packed, cotangent))
+
+    upstream_in = Transfer(to_image(place, cotangent))
     attended_half, raised, inv_total = attention_forward(packed, mask_bias)
-    other_half = place.core(attended_half)
-    attended = jnp.where(
-        place.c == 0,
-        jnp.concatenate([attended_half, other_half], axis=1),
-        jnp.concatenate([other_half, attended_half], axis=1),
-    )
-    residual = tok_wide + dot(attended, full_out) + bias_rows[4]
-    second_out, second_normed, second_inv = layer_norm(residual, gain_rows[1], bias_rows[1])
-    second_low = second_out.astype(BF16)
-    upper = dot(second_low, full_up) + up_shift
-    active, slope = gelu_and_slope(upper)
-    active = active.astype(BF16)
-    slope = slope.astype(BF16)
-
-    def own_half(value):
-        return pick(value.reshape(2, value.shape[0] // 2, value.shape[1]), place.c)
-
-    def other_half_of(value):
-        return pick(value.reshape(2, value.shape[0] // 2, value.shape[1]), 1 - place.c)
-
-    down_part = dot_t(active, full_down)
-    down_sum = own_half(down_part) + place.core(other_half_of(down_part).astype(BF16)).astype(F32)
-    layer_half = (own_half(residual) + down_sum + bias_rows[5]).astype(BF16)
-    layer_out = from_image(place, layer_half)
-
-    grad_wide = upstream.astype(F32)
+    (attended_half,) = close_round(out_up, upstream_in, down, hold=(attended_half,))
+
+    half_out = assemble(place, (out_up.result, 0, out_cols))
+    full_out = join(place, half_out, place.core(half_out), half_width, False)
+    attended = join(place, attended_half, place.core(attended_half), half_width, True)
+    residual = tokens.astype(F32) + dot(attended, full_out) + bias_rows[4]
+    second_normed, second_inv = normalize(residual)
+    second_low = (second_normed * gain_rows[1] + bias_rows[1]).astype(BF16)
+    second_normed = second_normed.astype(BF16)
+    half = residual.shape[0] // 2
+    residual_half = residual[:half]
+    (second_low,) = close_round(upstream_in, down, hold=(second_low,))
+
+    full_up = assemble(place, (out_up.result, out_cols, half_hidden))
+    active, slope = gelu_and_slope(dot(second_low, full_up) + up_shift)
+    active, slope = active.astype(BF16), slope.astype(BF16)
+    active, slope = close_round(down, hold=(active, slope))
+
+    upstream = jnp.concatenate(upstream_in.result)
+    dw_down = t_dot(upstream, active).astype(BF16)
+    down_rows = lax.psum_scatter(dw_down, "fsdp", scatter_dimension=0, tiled=True, axis_index_groups=place.z_lines)
+    full_down = assemble(place, (down.result, 0, half_hidden))
     d_active = dot(upstream, full_down)
     d_upper = (d_active * slope.astype(F32)).astype(BF16)
-    dw_down = t_dot(upstream, active).astype(BF16)
-    down_sums = collect(place, dw_down)
     d_second_part = dot_t(d_upper, full_up)
-    d_second = d_second_part + place.core(d_second_part.astype(BF16)).astype(F32)
-    dw_up = t_dot(second_low, d_upper).astype(BF16)
-    up_sums = collect(place, dw_up)
-    d_resid = grad_wide + norm_back(d_second, second_normed, second_inv, gain_rows[1])
-    d_resid_low = d_resid.astype(BF16)
-    d_attended = dot_t(d_resid_low, pick(full_out.reshape(2, half_width, width), place.c)).astype(BF16)
+    (d_second_part,) = close_round(hold=(d_second_part,))
+
+    d_second_other = place.core(d_second_part.astype(BF16))
+    *dw_up, d_upper_sums = weight_grad(place, [(second_low, d_upper)], with_sums=True)
+    down_part = dot_t(active, full_down)
+    down_sum = down_part[:half] + place.core(down_part[half:].astype(BF16)).astype(F32)
+    layer_half = (residual_half + down_sum + bias_rows[5]).astype(BF16)
+    *dw_up, d_second_other, layer_half = close_round(hold=(*dw_up, d_second_other, layer_half))
+
+    up_grad = Transfer(collect(place, dw_up))
+    layer_out = Transfer(from_image(place, layer_half))
+    d_resid_low, d_resid_columns, d_resid_half, by_width = norm_back_second(
+        place, d_second_part, d_second_other, upstream, second_normed, second_inv, gain_rows[1:]
+    )
+    out_rows = lax.dynamic_slice_in_dim(full_out, c * half_width, half_width)
+    d_attended = dot_t(d_resid_low, out_rows).astype(BF16)
     d_packed = attention_backward(packed, d_attended, attended_half, raised, inv_total)
-    dw_out = t_dot(
-        attended, jnp.where(place.c == 0, d_resid_low[:, :half_width], d_resid_low[:, half_width:])
-    ).astype(BF16)
-    by_hidden = jnp.sum(d_upper.astype(F32), axis=0)
-    by_hidden = jnp.where(
-        place.c == 0,
-        jnp.pad(by_hidden, (0, half_hidden)),
-        jnp.pad(by_hidden, (half_hidden, 0)),
-    )[:hidden].reshape(fsdp, up_shard)
+    d_packed, down_rows = close_round(up_grad, layer_out, hold=(d_packed, down_rows))
+
+    down_grad = Transfer(sum_plane(place, down_rows))
+
+    def own_part(row):
+        size = row.shape[0]
+        return jnp.where(c == 0, jnp.pad(row, (0, size)), jnp.pad(row, (size, 0)))
+
+    by_hidden = own_part(d_upper_sums[0])[:hidden].reshape(fsdp, up_shard)
     by_hidden = jnp.pad(by_hidden, ((0, 0), (0, up_cols * shard - up_shard))).reshape(fsdp, up_cols, shard)
     by_hidden = by_hidden.transpose(1, 0, 2).reshape(up_cols, width)
-    by_width = jnp.stack(
+    pack_wide = d_packed.astype(F32)
+    riders = jnp.concatenate(
         [
-            jnp.sum(d_second * second_normed, axis=0),
-            jnp.sum(d_second, axis=0),
-            jnp.sum(d_resid, axis=0),
-            jnp.sum(grad_wide, axis=0),
+            own_part(jnp.sum(pack_wide[:, :half_width], axis=0))[None],
+            own_part(jnp.sum(pack_wide[:, 2 * half_width :], axis=0))[None],
+            jnp.where(c == 0, by_width[:4], 0.0),
+            by_hidden,
         ]
     )
-    by_width = jnp.where(place.c == 0, by_width, 0.0)
-    riders = jnp.concatenate([by_width, by_hidden])
-    riders = jnp.pad(riders, ((0, -half_width % LANES - riders.shape[0]), (0, 0))).T.astype(BF16)
-    out_sums = collect(place, jnp.concatenate([dw_out, riders], axis=1))
-    rider_sums = (out_sums[0][:, half_width:].astype(F32) + out_sums[1][:, half_width:].astype(F32)).T
-    out_sums = [part[:, :half_width] for part in out_sums]
-    second_sums = rider_sums[:4]
-    grad_upbias = rider_sums[4 : 4 + up_cols].reshape(up_cols * shard)[:up_shard]
-    dw_qkv = t_dot(first_low, d_packed).astype(BF16)
-    qkv_sums = collect(place, dw_qkv)
+    riders = jnp.pad(riders, ((0, LANES - riders.shape[0]), (0, 0))).T
+    dw_last = weight_grad(place, [(first_low, d_packed), (attended, d_resid_columns)], riders)
+    *dw_last, d_packed = close_round(up_grad, down_grad, hold=(*dw_last, d_packed))
+
+    last_grad = Transfer(collect(place, dw_last))
     d_first_part = dot_t(d_packed, full_qkv)
-    d_first = own_half(d_first_part) + place.core(other_half_of(d_first_part).astype(BF16)).astype(F32)
-    normed_half = own_half(first_normed)
-    grad_half = (
-        own_half(d_resid) + norm_back(d_first, normed_half, own_half(first_inv), gain_rows[0])
-    ).astype(BF16)
-    grad_in = from_image(place, grad_half)
-
-    pack_wide = d_packed.astype(F32)
-    q_sum = jnp.sum(pack_wide[:, :half_width], axis=0)
-    v_sum = jnp.sum(pack_wide[:, 2 * half_width :], axis=0)
-    late = jnp.concatenate([jnp.sum(d_first * normed_half, axis=0), jnp.sum(d_first, axis=0), q_sum, v_sum])
-    late = sum_chips(place, late.reshape(-1, LANES)).reshape(-1)
-    late_other = place.core(late)
-    first_sums = (late[: 2 * width] + late_other[: 2 * width]).reshape(2, width)
-    qv_mine = late[2 * width :].reshape(2, 1, half_width)
-    qv_other = late_other[2 * width :].reshape(2, 1, half_width)
-    qv_sums = jnp.where(
-        place.c == 0, jnp.concatenate([qv_mine, qv_other], axis=1), jnp.concatenate([qv_other, qv_mine], axis=1)
-    ).reshape(2, width)
-    first_own = own_columns(place, first_sums)
-    qv_own = own_columns(place, qv_sums)
-    grad_gains = jnp.stack([first_own[0], second_sums[0]])
-    grad_biases = jnp.stack([first_own[1], second_sums[1], qv_own[0], qv_own[1], second_sums[2], second_sums[3]])
-
-    def side_by_side(sums):
-        mine, other = (part.astype(F32) for part in sums)
-        return jnp.where(place.c == 0, mine, other), jnp.where(place.c == 0, other, mine)
-
-    lower, higher = side_by_side(qkv_sums)
-    grad_qkv = jnp.stack([lower.reshape(shard, 3, half_width), higher.reshape(shard, 3, half_width)], axis=2)
-    grad_qkv = grad_qkv.reshape(shard, 3 * width)
-    grad_proj = jnp.concatenate(side_by_side(out_sums), axis=1)
-    grad_up = jnp.concatenate(side_by_side(up_sums), axis=1)[:, :hidden]
-    grad_down = jnp.concatenate(side_by_side(down_sums), axis=1)[:, :hidden].T
-    return (
-        layer_out,
-        grad_in,
-        grad_qkv,
-        grad_proj,
-        grad_up,
-        grad_down,
-        grad_gains,
-        grad_biases,
-        grad_upbias,
-    )
+    grad_half, first_sums = norm_back_first(
+        d_first_part,
+        place.core(d_first_part[half:].astype(BF16)),
+        d_resid_half,
+        first_normed,
+        first_inv,
+        gain_rows[:1],
+    )
+    grad_half, first_sums = close_round(up_grad, last_grad, hold=(grad_half, first_sums))
+
+    def write_hidden(lower, higher, out):
+        out[:, :half_hidden] = lower[:, :half_hidden]
+        out[:, half_hidden:] = higher[:, : hidden - half_hidden]
+
+    def write_last(lower, higher, qkv_out, proj, rest):
+        for i in range(3):
+            here = slice(i * half_width, (i + 1) * half_width)
+            qkv_out[:, i * width : i * width + half_width] = lower[:, here]
+            qkv_out[:, i * width + half_width : (i + 1) * width] = higher[:, here]
+        here = slice(3 * half_width, 4 * half_width)
+        proj[:, :half_width] = lower[:, here]
+        proj[:, half_width:] = higher[:, here]
+        rest[...] = lower[:, 4 * half_width :] + higher[:, 4 * half_width :]
+
+    late = Transfer(sum_devices(place, first_sums[:2].reshape(-1, LANES)))
+    close_round(up_grad, last_grad, late, down_grad)
+    grad_in = Transfer(from_image(place, grad_half))
+    down_rows = down_grad.result.reshape(2, shard, half_hidden)
+    down_other = place.core(pick(down_rows, 1 - c))
+    grad_down = lay(place, pick(down_rows, c), down_other, write_hidden, (shard, hidden))
+    (grad_down,) = close_round(up_grad, last_grad, late, grad_in, hold=(grad_down,))
+    grad_in, layer_out = close_round(up_grad, last_grad, late, hold=(grad_in.result, layer_out.result))
+    (grad_up,) = finish(place, up_grad.result, write_hidden, [(shard, hidden)])
+    (grad_up,) = close_round(last_grad, hold=(grad_up,))
+    close_round(last_grad)
+    grad_qkv, grad_proj, rest_sums = finish(
+        place, last_grad.result, write_last, [(shard, 3 * width), (shard, width), (shard, LANES)]
+    )
+    rows = rest_sums[:, : 6 + up_cols].T
+    first_rows = lax.dynamic_slice_in_dim(late.result.reshape(2, width), lax.axis_index("fsdp") * shard, shard, axis=1)
+    grad_upbias = rows[6:].reshape(up_cols * shard)[:up_shard]
+    grad_gains = jnp.stack([first_rows[0], rows[2]])
+    grad_biases = jnp.stack([first_rows[1], rows[3], rows[0], rows[1], rows[4], rows[5]])
+    return (layer_out, grad_in, grad_qkv, grad_proj, grad_up, grad_down.T, grad_gains, grad_biases, grad_upbias)
 
 
 def for_sending(array):

time: 751 us -> 544 us (0.72)
  waiting for transfers between devices: 238 us -> 116 us
  Pallas kernels: 57.3 us -> 122 us
  other arithmetic: 92.4 us -> 35.1 us
  starting transfers between devices: 139 us -> 97.2 us
  matrix products: 101 us -> 64.6 us
  local copies, waits for them, and re-layouts: 109 us -> 83.3 us
  between operations: 2.82 us -> 16 us
    ppermute x95 -> x61, waiting for transfers between devices: 238 us -> 101 us  [send(): return lax.ppermute(value, ('fsdp', 'seq'), pairs)]
    ppermute x95 -> x61, starting transfers between devices: 139 us -> 72.1 us  [send(): return lax.ppermute(value, ('fsdp', 'seq'), pairs)]
    pallas_call x3 -> x20, Pallas kernels: 11.3 us -> 75.8 us  [the longest x2 27.1 us: weight_grad(): pl.pallas_call(functools.partial(weight_grad_kernel, cut, group, rows, le...]
    all_to_all x0 -> x5, starting transfers between devices: none -> 24.8 us  [over_z(): lax.all_to_all(value, 'fsdp', 0, 0, axis_index_groups=self.z_lines, tiled...]
    dot_general x4 -> x1, matrix products: 30.4 us -> 7.46 us  [t_dot(): lax.dot_general(a, b, (((0,), (0,)), ((), ())), preferred_element_type=F32)]
    reduce_sum x7 -> x4, other arithmetic: 22.9 us -> 4.01 us  [the longest x2 3.08 us: collect(): mine = jnp.sum(arrived.astype(F32), axis=0).astype(BF16)]
    unnamed x172 -> x182, local copies, waits for them, and re-layouts: 28.1 us -> 44.5 us
    all_to_all x0 -> x5, waiting for transfers between devices: none -> 14.3 us  [over_z(): lax.all_to_all(value, 'fsdp', 0, 0, axis_index_groups=self.z_lines, tiled...]
  transfers between devices with their start and end apart: 95 -> 67, of which waited for: 40 -> 25; matrix products, arithmetic and copies ran while one was open for 30% -> 21% of each run, Pallas kernels for 8% -> 21%
where the time goes in v2:
time: 544 us; the launch traced here: 534 us
  Pallas kernels  122 us (22%)
  waiting for transfers between devices  116 us (21%)
  starting transfers between devices  97.2 us (18%)
  local copies, waits for them, and re-layouts  83.3 us (15%)
  matrix products  64.6 us (12%)
  other arithmetic  35.1 us (6%)
  between operations  16 us (3%)
    ppermute x61, waiting for transfers between devices, send(): return lax.ppermute(value, ('fsdp', 'seq'), pairs)  101 us
    ppermute x61, starting transfers between devices, send(): return lax.ppermute(value, ('fsdp', 'seq'), pairs)  72.1 us
    unnamed x182, local copies, waits for them, and re-layouts  44.5 us
    dot_general x4, matrix products, dot(): return jnp.dot(a, b, preferred_element_type=F32)  32.7 us
    pallas_call x2, Pallas kernels, weight_grad(): pl.pallas_call(functools.partial(weight_grad_kernel, cut, group, rows, le...  27.1 us
    pallas_call x1, Pallas kernels, attention_backward(): pl.pallas_call(functools.partial(attention_backward_kernel, block, heads)...  26.2 us
    all_to_all x5, starting transfers between devices, over_z(): lax.all_to_all(value, 'fsdp', 0, 0, axis_index_groups=self.z_lines, tiled...  24.8 us
    dot_general x4, matrix products, dot_t(): lax.dot_general(a, b, (((1,), (1,)), ((), ())), preferred_element_type=F32)  24.5 us
  transfers between devices with their start and end apart: 67, of which 25 were waited for; matrix products, arithmetic and copies ran while one was open for 21% of the time, Pallas kernels for 21%

profile of v2, /device:TPU:0, one launch (start us, length us, event | category | flops | bytes accessed | tf_op | source)
XLA Modules:
  0.0 533.8 jit_solution(17340608790530507815)
XLA Ops:
  8.8 2.0 reshape.187
  17.4 6.2 %all-to-all-start = ((bf16[4,72,1792]{2,1,0:T(8,128)(2,1)}), bf16[4,72,1792]{2,1,0:T(8,128)(2,1)S(1)}, u32[]{:S(2)}, u32[]{:S(2)}) async-start(bf16[4,72,1792]{2,1,0:T(8,128)(2,1)} %broadcast_in_dim.63), calls=%async_computation | async-start | bytes 2064384 | tf_op jit(solution)/shard_map/all_to_all | solution.py:193
  27.7 6.0 %collective-permute-start.1 = (bf16[256,1152]{1,0:T(8,128)(2,1)}, bf16[256,1152]{1,0:T(8,128)(2,1)}, u32[]{:S(2)}, u32[]{:S(2)}) collective-permute-start(bf16[256,1152]{1,0:T(8,128)(2,1)} %get-tuple-element.422), channel_id=1, source_target_pairs={{0,0},{1,1},{2,4},{3,5},{4,2},{5,3},{6,6},{7,7},{8,8},{9,9},{10,12... | collective-permute-start | bytes 1769480 | tf_op jit(solution)/shard_map/ppermute | solution.py:175
  33.6 8.8 %collective-permute-done.2 = bf16[256,1152]{1,0:T(8,128)(2,1)} collective-permute-done((bf16[256,1152]{1,0:T(8,128)(2,1)}, bf16[256,1152]{1,0:T(8,128)(2,1)}, u32[]{:S(2)}, u32[]{:S(2)}) %collective-permute-start.2) | collective-permute-done | bytes 589856 | tf_op jit(solution)/shard_map/ppermute | solution.py:175
  42.4 6.8 %all-to-all-done = bf16[4,72,1792]{2,1,0:T(8,128)(2,1)S(1)} async-done(((bf16[4,72,1792]{2,1,0:T(8,128)(2,1)}), bf16[4,72,1792]{2,1,0:T(8,128)(2,1)S(1)}, u32[]{:S(2)}, u32[]{:S(2)}) %all-to-all-start) | async-done | bytes 1032224 | tf_op jit(solution)/shard_map/all_to_all | solution.py:193
  52.4 4.4 all-to-all-start.1
  64.6 10.7 %collective-permute-done.5.refs_3_ = bf16[3,72,1792]{2,1,0:T(8,128)(2,1)S(1)} collective-permute-done((bf16[3,72,1792]{2,1,0:T(8,128)(2,1)S(1)}, bf16[3,72,1792]{2,1,0:T(8,128)(2,1)S(1)}, u32[]{:S(2)}, u32[]{:S(2)}) %collective-permute-start.5) | collective-permute-done | bytes 774176 | tf_op jit(solution)/shard_map/ppermute | solution.py:175
  84.1 2.1 copy-done
  89.6 4.8 all-to-all-done.1
  102.8 4.3 all-to-all-start.2
  112.0 6.9 %shard_map.170 = bf16[16,72,1792]{2,1,0:T(8,128)(2,1)} custom-call(s32[5]{0:T(128)S(1)} %stack.66.scalars.where, bf16[4,72,1792]{2,1,0:T(8,128)(2,1)S(1)} %bitcast.109, bf16[3,72,1792]{2,1,0:T(8,128)(2,1)S(1)} %copy-done.15, bf16[3,72,1792]{2,1,0:T(8,128)(2,1)S(1)} %copy-done.27, bf16[3,72,1792]{2,1,0:T(8,128)(2,1)S(1)} %copy-done.25, ...), custom_call_target="tpu_custom_call" | custom-call | bytes 8257536 | tf_op jit(solution)/shard_map/pallas_call | solution.py:314
  120.9 4.2 add_convert_fusion.3.refs_0_
  125.4 9.7 %add_convert_fusion.1.qkv_ref = bf16[1024,1728]{1,0:T(8,128)(2,1)} fusion(bf16[1024,1152]{1,0:T(8,128)(2,1)} %add_convert_fusion.3.refs_0_, f32[1728]{0:T(1024)S(1)} %concatenate.87, bf16[1152,1792]{1,0:T(8,128)(2,1)} %bitcast.25), kind=kOutput, calls=%fused_computation.6 | convolution fusion | flops 4080402432 | bytes 10033920 | tf_op jit(solution)/shard_map/dot_general | solution.py:761
  135.0 2.0 slice.188
  137.1 1.9 slice.187
  142.7 5.9 %collective-permute-start.14 = (bf16[256,1152]{1,0:T(8,128)(2,1)}, bf16[256,1152]{1,0:T(8,128)(2,1)}, u32[]{:S(2)}, u32[]{:S(2)}) collective-permute-start(bf16[256,1152]{1,0:T(8,128)(2,1)} %get-tuple-element.420), channel_id=1, source_target_pairs={{0,0},{1,1},{2,4},{3,5},{4,2},{5,3},{6,6},{7,7},{8,8},{9,9},{10,12... | collective-permute-start | bytes 1769480 | tf_op jit(solution)/shard_map/ppermute | solution.py:175
  151.7 2.0 copy-done.2
  153.7 20.0 %shard_map.171 = (bf16[1024,640]{1,0:T(8,128)(2,1)}, bf16[8,1024,1024]{2,1,0:T(8,128)(2,1)}, f32[8,1,1024]{2,1,0:T(1,128)S(1)}) custom-call(bf16[1024,1728]{1,0:T(8,128)(2,1)S(1)} %copy-done.2, f32[1024,1]{1,0:T(8,128)S(1)} %broadcast_select_fusion.bias_ref), custom_call_target="tpu_custom_call" | custom-call | flops 8388608 | bytes 1769472 | tf_op jit(solution)/shard_map/pallas_call | solution.py:61
  174.4 3.0 shard_map.173
  181.7 2.5 shard_map.175
  187.3 2.2 shard_map.172.refs_1_
  189.6 3.2 shard_map.174
  193.0 3.7 fusion.32
  199.0 5.0 collective-permute-done.19.refs_3_
  206.5 11.0 %add_convert_fusion = (bf16[1024,2176]{1,0:T(8,128)(2,1)}, bf16[1024,2176]{1,0:T(8,128)(2,1)S(1)}) fusion(f32[2176]{0:T(1024)S(1)} %fusion.19, bf16[1024,1152]{1,0:T(8,128)(2,1)S(1)} %get-tuple-element.236.refs_0_, bf16[1152,2176]{1,0:T(8,128)(2,1)S(1)} %bitcast.112), kind=kOutput, calls=%fused_computation.2 | convolution fusion | flops 5178392576 | bytes 16294400 | tf_op jit(solution)/shard_map/dot_general | solution.py:761
  220.7 7.5 %convolution_convert_fusion = bf16[1152,2176]{1,0:T(8,128)(2,1)} fusion(bf16[1024,1152]{1,0:T(8,128)(2,1)S(1)} %constant_dynamic-update-slice_fusion.4.upstream, bf16[1024,2176]{1,0:T(8,128)(2,1)S(1)} %get-tuple-element.254), kind=kOutput, calls=%fused_computation | convolution fusion | flops 5136334848 | bytes 11829248 | tf_op jit(solution)/shard_map/dot_general | solution.py:769
  235.2 1.9 shard_map.176
  237.1 8.4 %multiply_convert_fusion.refs_1_ = bf16[1024,2176]{1,0:T(8,128)(2,1)S(1)} fusion(bf16[1024,2176]{1,0:T(8,128)(2,1)} %get-tuple-element.249, bf16[1024,1152]{1,0:T(8,128)(2,1)S(1)} %copy-done.7, bf16[1152,2176]{1,0:T(8,128)(2,1)S(1)} %bitcast.110), kind=kOutput, calls=%fused_computation.1 | convolution fusion | flops 5140512768 | bytes 16285696 | tf_op jit(solution)/shard_map/dot_general | solution.py:761
  245.5 6.2 %fusion.33.part = f32[1024,1152]{1,0:T(8,128)S(1)} fusion(bf16[1024,2176]{1,0:T(8,128)(2,1)S(1)} %multiply_convert_fusion.refs_1_, bf16[1152,2176]{1,0:T(8,128)(2,1)S(1)} %bitcast.115), kind=kOutput, calls=%fused_computation.141 | convolution fusion | flops 5133828096 | bytes 14188544 | tf_op jit(solution)/shard_map/dot_general | solution.py:765
  251.8 1.9 convert_element_type.121
  254.7 8.3 %fusion.34 = f32[1024,1152]{1,0:T(8,128)S(1)} fusion(bf16[1024,2176]{1,0:T(8,128)(2,1)} %copy-done.81, bf16[1152,2176]{1,0:T(8,128)(2,1)S(1)} %bitcast.111), kind=kOutput, calls=%fused_computation.142 | convolution fusion | flops 5133828096 | bytes 14188544 | tf_op jit(solution)/shard_map/dot_general | solution.py:765
  263.0 2.1 copy-done.63
  267.0 12.7 %shard_map.177 = (bf16[2,4,72,1024]{3,2,1,0:T(8,128)(2,1)}, bf16[2,4,72,1024]{3,2,1,0:T(8,128)(2,1)}, bf16[2,4,72,1152]{3,2,1,0:T(8,128)(2,1)}, bf16[2,4,72,1152]{3,2,1,0:T(8,128)(2,1)}, f32[8,2176]{1,0:T(8,128)}) custom-call(s32[5]{0:T(128)} %copy-done.51, bf16[1024,1152]{1,0:T(8,128)(2,1)} %copy-done.59, bf16[1024,2176]{1,0:T(8,128)(2,1)} %copy-done.60), custom_call_target="tpu_custom_call" | custom-call | flops 1179648 | bytes 2506752 | tf_op jit(solution)/shard_map/pallas_call | solution.py:415
  280.9 3.3 fusion.6
  288.2 5.9 %collective-permute-start.28 = (bf16[256,1152]{1,0:T(8,128)(2,1)}, bf16[256,1152]{1,0:T(8,128)(2,1)}, u32[]{:S(2)}, u32[]{:S(2)}) collective-permute-start(bf16[256,1152]{1,0:T(8,128)(2,1)} %get-tuple-element.418), channel_id=1, source_target_pairs={{0,0},{1,1},{2,4},{3,5},{4,2},{5,3},{6,6},{7,7},{8,8},{9,9},{10,12... | collective-permute-start | bytes 1769480 | tf_op jit(solution)/shard_map/ppermute | solution.py:175
  294.2 7.4 %shard_map.178 = (bf16[1024,1152]{1,0:T(8,128)(2,1)S(1)}, bf16[1024,576]{1,0:T(8,128)(2,1)S(1)}, f32[512,1152]{1,0:T(8,128)S(1)}, f32[8,1152]{1,0:T(8,128)S(1)}) custom-call(s32[5]{0:T(128)S(1)} %copy-done.52, f32[1024,1152]{1,0:T(8,128)S(1)} %bitcast.102, bf16[1024,1152]{1,0:T(8,128)(2,1)} %collective-permute-done.24.arrived, ...), custom_call_target="tpu_custom_call" | custom-call | tf_op jit(solution)/shard_map/pallas_call | solution.py:668
  307.2 26.2 %shard_map.179.refs_2_ = bf16[1024,1728]{1,0:T(8,128)(2,1)} custom-call(bf16[1024,1728]{1,0:T(8,128)(2,1)} %add_convert_fusion.1.qkv_ref, bf16[1024,576]{1,0:T(8,128)(2,1)} %copy.96.d_out_ref, bf16[1024,640]{1,0:T(8,128)(2,1)} %get-tuple-element.229.mine.out_ref, bf16[8,1024,1024]{2,1,0:T(8,128)(2,1)} %get-tuple-element.262.probs_ref, f32[8,1,1024]{2,1,0:T(1,128)} %copy-done.54), custom_call_target="tpu_custom_call" | custom-call | flops 8388608 | bytes 1769472 | tf_op jit(solution)/shard_map/pallas_call | solution.py:132
  333.6 2.1 slice.202
  335.6 2.0 slice.203
  339.1 3.7 shard_map.180
  343.7 2.0 collective-permute-start.33
  348.7 14.4 %shard_map.181 = (bf16[2,4,72,1152]{3,2,1,0:T(8,128)(2,1)}, bf16[2,4,72,1152]{3,2,1,0:T(8,128)(2,1)}, bf16[2,4,72,1280]{3,2,1,0:T(8,128)(2,1)}, bf16[2,4,72,1280]{3,2,1,0:T(8,128)(2,1)}) custom-call(s32[5]{0:T(128)} %copy-done.51, bf16[1024,1152]{1,0:T(8,128)(2,1)} %add_convert_fusion.3.refs_0_, bf16[1024,1152]{1,0:T(8,128)(2,1)} %copy-done.3, ...), custom_call_target="tpu_custom_call" | custom-call | flops 1179648 | bytes 2801664 | tf_op jit(solution)/shard_map/pallas_call | solution.py:415
  363.2 9.2 %collective-permute-done.33 = bf16[288,1152]{1,0:T(8,128)(2,1)S(1)} collective-permute-done((bf16[288,1152]{1,0:T(8,128)(2,1)}, bf16[288,1152]{1,0:T(8,128)(2,1)S(1)}, u32[]{:S(2)}, u32[]{:S(2)}) %collective-permute-start.33) | collective-permute-done | bytes 663584 | tf_op jit(solution)/shard_map/ppermute | solution.py:175
  372.4 1.9 shard_map.182
  374.3 5.0 all-to-all-start.3
  381.7 8.2 %fusion.part = f32[1024,1152]{1,0:T(8,128)S(1)} fusion(bf16[1024,1728]{1,0:T(8,128)(2,1)} %shard_map.179.refs_2_, bf16[1152,1792]{1,0:T(8,128)(2,1)} %bitcast.25), kind=kOutput, calls=%fused_computation.12 | convolution fusion | flops 4076863488 | bytes 12386304 | tf_op jit(solution)/shard_map/dot_general | solution.py:765
  390.2 2.4 add_convert_fusion.7
  395.8 13.7 %collective-permute-done.34.from_x = bf16[2,4,72,1152]{3,2,1,0:T(8,128)(2,1)S(1)} collective-permute-done((bf16[2,4,72,1152]{3,2,1,0:T(8,128)(2,1)}, bf16[2,4,72,1152]{3,2,1,0:T(8,128)(2,1)S(1)}, u32[]{:S(2)}, u32[]{:S(2)}) %collective-permute-start.34) | collective-permute-done | bytes 1327136 | tf_op jit(solution)/shard_map/ppermute | solution.py:175
  410.5 4.9 collective-permute-done.35.from_y
  418.1 2.2 shard_map.184
  429.5 23.7 %collective-permute-done.43 = bf16[288,1152]{1,0:T(8,128)(2,1)} collective-permute-done((bf16[288,1152]{1,0:T(8,128)(2,1)S(1)}, bf16[288,1152]{1,0:T(8,128)(2,1)}, u32[]{:S(2)}, u32[]{:S(2)}) %collective-permute-start.43) | collective-permute-done | bytes 663584 | tf_op jit(solution)/shard_map/ppermute | solution.py:175
  454.3 2.1 collective-permute-done.37.refs_1_
  460.4 5.0 all-to-all-start.4
  471.6 4.2 collective-permute-start.45
  476.5 8.6 %collective-permute-done.50 = bf16[256,1152]{1,0:T(8,128)(2,1)S(1)} collective-permute-done((bf16[256,1152]{1,0:T(8,128)(2,1)S(1)}, bf16[256,1152]{1,0:T(8,128)(2,1)S(1)}, u32[]{:S(2)}, u32[]{:S(2)}) %collective-permute-start.50) | collective-permute-done | bytes 589856 | tf_op jit(solution)/shard_map/ppermute | solution.py:175
  485.2 3.4 collective-permute-start.48
  488.6 2.0 collective-permute-start.47
  491.5 2.2 shard_map.186
  494.4 2.6 all-to-all-done.4
  504.1 2.8 maximum_select_fusion.3
  512.9 2.3 shard_map.188
  515.2 2.5 collective-permute-done.58.refs_3_
  519.2 2.3 collective-permute-done.60.refs_5_
  521.5 2.4 shard_map.190
  (416 shorter events, 149.1 us)
Async XLA Ops:
  17.4 31.9 %all-to-all-start = ((bf16[4,72,1792]{2,1,0:T(8,128)(2,1)}), bf16[4,72,1792]{2,1,0:T(8,128)(2,1)S(1)}, u32[]{:S(2)}, u32[]{:S(2)}) async-start(bf16[4,72,1792]{2,1,0:T(8,128)(2,1)} %broadcast_in_dim.63), calls=%async_computation | async-start | bytes 2064384 | tf_op jit(solution)/shard_map/all_to_all | solution.py:193
  23.9 18.5 %collective-permute-start.3 = (bf16[144,2816]{1,0:T(8,128)(2,1)S(1)}, bf16[144,2816]{1,0:T(8,128)(2,1)S(1)}, u32[]{:S(2)}, u32[]{:S(2)}) collective-permute-start(bf16[144,2816]{1,0:T(8,128)(2,1)S(1)} %get-tuple-element.402), channel_id=1, source_target_pairs={{0,4},{1,5},{2,6},{3,7},{4,0},{5,1},{6,2},{7,3},{8,12},{9,13},{10,... | collective-permute-start | bytes 2433032 | tf_op jit(solution)/shard_map/ppermute | solution.py:175
  26.2 16.2 %collective-permute-start.2 = (bf16[256,1152]{1,0:T(8,128)(2,1)}, bf16[256,1152]{1,0:T(8,128)(2,1)}, u32[]{:S(2)}, u32[]{:S(2)}) collective-permute-start(bf16[256,1152]{1,0:T(8,128)(2,1)} %get-tuple-element.421), channel_id=1, source_target_pairs={{0,1},{1,0},{2,5},{3,4},{4,3},{5,2},{6,7},{7,6},{8,9},{9,8},{10,13... | collective-permute-start | bytes 1769480 | tf_op jit(solution)/shard_map/ppermute | solution.py:175
  27.7 14.7 %collective-permute-start.1 = (bf16[256,1152]{1,0:T(8,128)(2,1)}, bf16[256,1152]{1,0:T(8,128)(2,1)}, u32[]{:S(2)}, u32[]{:S(2)}) collective-permute-start(bf16[256,1152]{1,0:T(8,128)(2,1)} %get-tuple-element.422), channel_id=1, source_target_pairs={{0,0},{1,1},{2,4},{3,5},{4,2},{5,3},{6,6},{7,7},{8,8},{9,9},{10,12... | collective-permute-start | bytes 1769480 | tf_op jit(solution)/shard_map/ppermute | solution.py:175
  52.4 42.0 %all-to-all-start.1 = ((bf16[4,72,2816]{2,1,0:T(8,128)(2,1)}), bf16[4,72,2816]{2,1,0:T(8,128)(2,1)}, u32[]{:S(2)}, u32[]{:S(2)}) async-start(bf16[4,72,2816]{2,1,0:T(8,128)(2,1)} %broadcast_in_dim.65), calls=%async_computation.1 | async-start | bytes 3244032 | tf_op jit(solution)/shard_map/all_to_all | solution.py:193
  57.0 18.4 %collective-permute-start.5 = (bf16[3,72,1792]{2,1,0:T(8,128)(2,1)S(1)}, bf16[3,72,1792]{2,1,0:T(8,128)(2,1)S(1)}, u32[]{:S(2)}, u32[]{:S(2)}) collective-permute-start(bf16[3,72,1792]{2,1,0:T(8,128)(2,1)S(1)} %pad_maximum_fusion.3.refs_1_), channel_id=1, source_target_pairs={{0,2},{1,3},{2,0},{3,1},{4,6},{5,7},{6,4},{7,5},{8,10},{9,11},{10,... | collective-permute-start | bytes 2322440 | tf_op jit(solution)/shard_map/ppermute | solution.py:175
  58.5 18.0 %collective-permute-start.4 = (bf16[3,72,1792]{2,1,0:T(8,128)(2,1)S(1)}, bf16[3,72,1792]{2,1,0:T(8,128)(2,1)S(1)}, u32[]{:S(2)}, u32[]{:S(2)}) collective-permute-start(bf16[3,72,1792]{2,1,0:T(8,128)(2,1)S(1)} %pad_maximum_fusion.3.refs_1_), channel_id=1, source_target_pairs={{0,1},{1,0},{2,3},{3,2},{4,5},{5,4},{6,7},{7,6},{8,9},{9,8},{10,11... | collective-permute-start | bytes 2322440 | tf_op jit(solution)/shard_map/ppermute | solution.py:175
  62.3 14.3 %collective-permute-start.6 = (bf16[512,1152]{1,0:T(8,128)(2,1)S(1)}, bf16[512,1152]{1,0:T(8,128)(2,1)S(1)}, u32[]{:S(2)}, u32[]{:S(2)}) collective-permute-start(bf16[512,1152]{1,0:T(8,128)(2,1)S(1)} %constant_dynamic-update-slice_fusion.half), channel_id=1, source_target_pairs={{0,4},{1,5},{2,6},{3,7},{4,0},{5,1},{6,2},{7,3},{8,12},{9,13},{10,... | collective-permute-start | bytes 3538952 | tf_op jit(solution)/shard_map/ppermute | solution.py:175
  64.1 24.3 %collective-permute-start.9 = (bf16[144,2176]{1,0:T(8,128)(2,1)}, bf16[144,2176]{1,0:T(8,128)(2,1)}, u32[]{:S(2)}, u32[]{:S(2)}) collective-permute-start(bf16[144,2176]{1,0:T(8,128)(2,1)} %get-tuple-element.409), channel_id=1, source_target_pairs={{0,4},{1,5},{2,6},{3,7},{4,0},{5,1},{6,2},{7,3},{8,12},{9,13},{10,... | collective-permute-start | bytes 1880072 | tf_op jit(solution)/shard_map/ppermute | solution.py:175
  79.2 9.2 %collective-permute-start.7 = (bf16[3,72,896]{2,1,0:T(8,128)(2,1)}, bf16[3,72,896]{2,1,0:T(8,128)(2,1)S(1)}, u32[]{:S(2)}, u32[]{:S(2)}) collective-permute-start(bf16[3,72,896]{2,1,0:T(8,128)(2,1)} %slice.177), channel_id=1, source_target_pairs={{0,1},{1,0},{2,3},{3,2},{4,5},{5,4},{6,7},{7,6},{8,9},{9,8},{10,11... | collective-permute-start | bytes 1161224 | tf_op jit(solution)/shard_map/ppermute | solution.py:175
  80.7 8.9 %collective-permute-start.8 = (bf16[3,72,896]{2,1,0:T(8,128)(2,1)}, bf16[3,72,896]{2,1,0:T(8,128)(2,1)}, u32[]{:S(2)}, u32[]{:S(2)}) collective-permute-start(bf16[3,72,896]{2,1,0:T(8,128)(2,1)} %slice.178), channel_id=1, source_target_pairs={{0,2},{1,3},{2,0},{3,1},{4,6},{5,7},{6,4},{7,5},{8,10},{9,11},{10,... | collective-permute-start | bytes 1161224 | tf_op jit(solution)/shard_map/ppermute | solution.py:175
  95.9 39.1 %collective-permute-start.11 = (bf16[3,72,2816]{2,1,0:T(8,128)(2,1)S(1)}, bf16[3,72,2816]{2,1,0:T(8,128)(2,1)}, u32[]{:S(2)}, u32[]{:S(2)}) collective-permute-start(bf16[3,72,2816]{2,1,0:T(8,128)(2,1)S(1)} %pad_maximum_fusion.1.refs_1_), channel_id=1, source_target_pairs={{0,2},{1,3},{2,0},{3,1},{4,6},{5,7},{6,4},{7,5},{8,10},{9,11},{10,... | collective-permute-start | bytes 3649544 | tf_op jit(solution)/shard_map/ppermute | solution.py:175
  97.5 37.5 %collective-permute-start.10 = (bf16[3,72,2816]{2,1,0:T(8,128)(2,1)S(1)}, bf16[3,72,2816]{2,1,0:T(8,128)(2,1)}, u32[]{:S(2)}, u32[]{:S(2)}) collective-permute-start(bf16[3,72,2816]{2,1,0:T(8,128)(2,1)S(1)} %pad_maximum_fusion.1.refs_1_), channel_id=1, source_target_pairs={{0,1},{1,0},{2,3},{3,2},{4,5},{5,4},{6,7},{7,6},{8,9},{9,8},{10,11... | collective-permute-start | bytes 3649544 | tf_op jit(solution)/shard_map/ppermute | solution.py:175
  102.8 71.6 %all-to-all-start.2 = ((bf16[4,72,2176]{2,1,0:T(8,128)(2,1)}), bf16[4,72,2176]{2,1,0:T(8,128)(2,1)}, u32[]{:S(2)}, u32[]{:S(2)}) async-start(bf16[4,72,2176]{2,1,0:T(8,128)(2,1)} %broadcast_in_dim.68), calls=%async_computation.2 | async-start | bytes 2506752 | tf_op jit(solution)/shard_map/all_to_all | solution.py:193
  107.1 226.4 %reduce-scatter.2.cloned.1.call-start = ((), (), s32[]{:S(2)}) async-start(), calls=%async_computation.6 | async-start | bytes 6266880 | tf_op jit(solution)/shard_map/reduce_scatter | solution.py:863
  139.0 35.4 %collective-permute-start.12 = (bf16[3,72,1408]{2,1,0:T(8,128)(2,1)}, bf16[3,72,1408]{2,1,0:T(8,128)(2,1)S(1)}, u32[]{:S(2)}, u32[]{:S(2)}) collective-permute-start(bf16[3,72,1408]{2,1,0:T(8,128)(2,1)} %slice.187), channel_id=1, source_target_pairs={{0,1},{1,0},{2,3},{3,2},{4,5},{5,4},{6,7},{7,6},{8,9},{9,8},{10,11... | collective-permute-start | bytes 1824776 | tf_op jit(solution)/shard_map/ppermute | solution.py:175
  139.5 34.8 %collective-permute-start.13 = (bf16[3,72,1408]{2,1,0:T(8,128)(2,1)}, bf16[3,72,1408]{2,1,0:T(8,128)(2,1)}, u32[]{:S(2)}, u32[]{:S(2)}) collective-permute-start(bf16[3,72,1408]{2,1,0:T(8,128)(2,1)} %slice.188), channel_id=1, source_target_pairs={{0,2},{1,3},{2,0},{3,1},{4,6},{5,7},{6,4},{7,5},{8,10},{9,11},{10,... | collective-permute-start | bytes 1824776 | tf_op jit(solution)/shard_map/ppermute | solution.py:175
  141.2 33.2 %collective-permute-start.15 = (bf16[256,1152]{1,0:T(8,128)(2,1)}, bf16[256,1152]{1,0:T(8,128)(2,1)}, u32[]{:S(2)}, u32[]{:S(2)}) collective-permute-start(bf16[256,1152]{1,0:T(8,128)(2,1)} %get-tuple-element.419), channel_id=1, source_target_pairs={{0,1},{1,0},{2,5},{3,4},{4,3},{5,2},{6,7},{7,6},{8,9},{9,8},{10,13... | collective-permute-start | bytes 1769480 | tf_op jit(solution)/shard_map/ppermute | solution.py:175
  142.7 31.7 %collective-permute-start.14 = (bf16[256,1152]{1,0:T(8,128)(2,1)}, bf16[256,1152]{1,0:T(8,128)(2,1)}, u32[]{:S(2)}, u32[]{:S(2)}) collective-permute-start(bf16[256,1152]{1,0:T(8,128)(2,1)} %get-tuple-element.420), channel_id=1, source_target_pairs={{0,0},{1,1},{2,4},{3,5},{4,2},{5,3},{6,6},{7,7},{8,8},{9,9},{10,12... | collective-permute-start | bytes 1769480 | tf_op jit(solution)/shard_map/ppermute | solution.py:175
  177.4 12.2 %collective-permute-start.21 = (bf16[1152,640]{1,0:T(8,128)(2,1)}, bf16[1152,640]{1,0:T(8,128)(2,1)}, u32[]{:S(2)}, u32[]{:S(2)}) collective-permute-start(bf16[1152,640]{1,0:T(8,128)(2,1)} %bitcast.35.mine), channel_id=1, source_target_pairs={{0,4},{1,5},{2,6},{3,7},{4,0},{5,1},{6,2},{7,3},{8,12},{9,13},{10,... | collective-permute-start | bytes 4423688 | tf_op jit(solution)/shard_map/ppermute | solution.py:175
  177.6 9.7 %collective-permute-start.20 = (bf16[1024,640]{1,0:T(8,128)(2,1)}, bf16[1024,640]{1,0:T(8,128)(2,1)}, u32[]{:S(2)}, u32[]{:S(2)}) collective-permute-start(bf16[1024,640]{1,0:T(8,128)(2,1)} %get-tuple-element.229.mine.out_ref), channel_id=1, source_target_pairs={{0,4},{1,5},{2,6},{3,7},{4,0},{5,1},{6,2},{7,3},{8,12},{9,13},{10,... | collective-permute-start | bytes 3932168 | tf_op jit(solution)/shard_map/ppermute | solution.py:175
  181.1 23.0 %collective-permute-start.19 = (bf16[3,72,2176]{2,1,0:T(8,128)(2,1)S(1)}, bf16[3,72,2176]{2,1,0:T(8,128)(2,1)S(1)}, u32[]{:S(2)}, u32[]{:S(2)}) collective-permute-start(bf16[3,72,2176]{2,1,0:T(8,128)(2,1)S(1)} %pad_maximum_fusion.2.refs_1_), channel_id=1, source_target_pairs={{0,2},{1,3},{2,0},{3,1},{4,6},{5,7},{6,4},{7,5},{8,10},{9,11},{10,... | collective-permute-start | bytes 2820104 | tf_op jit(solution)/shard_map/ppermute | solution.py:175
  181.1 23.0 %collective-permute-start.18 = (bf16[3,72,2176]{2,1,0:T(8,128)(2,1)S(1)}, bf16[3,72,2176]{2,1,0:T(8,128)(2,1)S(1)}, u32[]{:S(2)}, u32[]{:S(2)}) collective-permute-start(bf16[3,72,2176]{2,1,0:T(8,128)(2,1)S(1)} %pad_maximum_fusion.2.refs_1_), channel_id=1, source_target_pairs={{0,1},{1,0},{2,3},{3,2},{4,5},{5,4},{6,7},{7,6},{8,9},{9,8},{10,11... | collective-permute-start | bytes 2820104 | tf_op jit(solution)/shard_map/ppermute | solution.py:175
  187.3 16.8 %collective-permute-start.17 = (bf16[512,1152]{1,0:T(8,128)(2,1)S(1)}, bf16[512,1152]{1,0:T(8,128)(2,1)S(1)}, u32[]{:S(2)}, u32[]{:S(2)}) collective-permute-start(bf16[512,1152]{1,0:T(8,128)(2,1)S(1)} %constant_dynamic-update-slice_fusion.2), channel_id=1, source_target_pairs={{0,4},{1,5},{2,6},{3,7},{4,0},{5,1},{6,2},{7,3},{8,12},{9,13},{10,... | collective-permute-start | bytes 3538952 | tf_op jit(solution)/shard_map/ppermute | solution.py:175
  204.1 13.7 %collective-permute-start.22 = (bf16[3,72,1024]{2,1,0:T(8,128)(2,1)S(1)}, bf16[3,72,1024]{2,1,0:T(8,128)(2,1)S(1)}, u32[]{:S(2)}, u32[]{:S(2)}) collective-permute-start(bf16[3,72,1024]{2,1,0:T(8,128)(2,1)S(1)} %slice.192), channel_id=1, source_target_pairs={{0,1},{1,0},{2,3},{3,2},{4,5},{5,4},{6,7},{7,6},{8,9},{9,8},{10,11... | collective-permute-start | bytes 1327112 | tf_op jit(solution)/shard_map/ppermute | solution.py:175
  204.8 14.0 %collective-permute-start.23 = (bf16[3,72,1152]{2,1,0:T(8,128)(2,1)S(1)}, bf16[3,72,1152]{2,1,0:T(8,128)(2,1)S(1)}, u32[]{:S(2)}, u32[]{:S(2)}) collective-permute-start(bf16[3,72,1152]{2,1,0:T(8,128)(2,1)S(1)} %slice.193), channel_id=1, source_target_pairs={{0,2},{1,3},{2,0},{3,1},{4,6},{5,7},{6,4},{7,5},{8,10},{9,11},{10,... | collective-permute-start | bytes 1493000 | tf_op jit(solution)/shard_map/ppermute | solution.py:175
  254.7 29.6 %collective-permute-start.24 = (bf16[1024,1152]{1,0:T(8,128)(2,1)}, bf16[1024,1152]{1,0:T(8,128)(2,1)}, u32[]{:S(2)}, u32[]{:S(2)}) collective-permute-start(bf16[1024,1152]{1,0:T(8,128)(2,1)} %convert_element_type.121), channel_id=1, source_target_pairs={{0,4},{1,5},{2,6},{3,7},{4,0},{5,1},{6,2},{7,3},{8,12},{9,13},{10,... | collective-permute-start | bytes 7077896 | tf_op jit(solution)/shard_map/ppermute | solution.py:175
  266.3 14.6 %collective-permute-start.25 = (bf16[512,1152]{1,0:T(8,128)(2,1)}, bf16[512,1152]{1,0:T(8,128)(2,1)}, u32[]{:S(2)}, u32[]{:S(2)}) collective-permute-start(bf16[512,1152]{1,0:T(8,128)(2,1)} %slice.286), channel_id=1, source_target_pairs={{0,4},{1,5},{2,6},{3,7},{4,0},{5,1},{6,2},{7,3},{8,12},{9,13},{10,... | collective-permute-start | bytes 3538952 | tf_op jit(solution)/shard_map/ppermute | solution.py:175
  284.3 49.2 %collective-permute-start.26 = (bf16[2,4,72,1024]{3,2,1,0:T(8,128)(2,1)}, bf16[2,4,72,1024]{3,2,1,0:T(8,128)(2,1)}, u32[]{:S(2)}, u32[]{:S(2)}) collective-permute-start(bf16[2,4,72,1024]{3,2,1,0:T(8,128)(2,1)} %get-tuple-element.257), channel_id=1, source_target_pairs={{0,1},{1,0},{2,3},{3,2},{4,5},{5,4},{6,7},{7,6},{8,9},{9,8},{10,11... | collective-permute-start | bytes 3538952 | tf_op jit(solution)/shard_map/ppermute | solution.py:175
  285.9 47.7 %collective-permute-start.27 = (bf16[2,4,72,1152]{3,2,1,0:T(8,128)(2,1)}, bf16[2,4,72,1152]{3,2,1,0:T(8,128)(2,1)}, u32[]{:S(2)}, u32[]{:S(2)}) collective-permute-start(bf16[2,4,72,1152]{3,2,1,0:T(8,128)(2,1)} %get-tuple-element.258), channel_id=1, source_target_pairs={{0,2},{1,3},{2,0},{3,1},{4,6},{5,7},{6,4},{7,5},{8,10},{9,11},{10,... | collective-permute-start | bytes 3981320 | tf_op jit(solution)/shard_map/ppermute | solution.py:175
  287.7 45.8 %collective-permute-start.29 = (bf16[256,1152]{1,0:T(8,128)(2,1)}, bf16[256,1152]{1,0:T(8,128)(2,1)}, u32[]{:S(2)}, u32[]{:S(2)}) collective-permute-start(bf16[256,1152]{1,0:T(8,128)(2,1)} %get-tuple-element.417), channel_id=1, source_target_pairs={{0,1},{1,0},{2,5},{3,4},{4,3},{5,2},{6,7},{7,6},{8,9},{9,8},{10,13... | collective-permute-start | bytes 1769480 | tf_op jit(solution)/shard_map/ppermute | solution.py:175
  288.2 45.3 %collective-permute-start.28 = (bf16[256,1152]{1,0:T(8,128)(2,1)}, bf16[256,1152]{1,0:T(8,128)(2,1)}, u32[]{:S(2)}, u32[]{:S(2)}) collective-permute-start(bf16[256,1152]{1,0:T(8,128)(2,1)} %get-tuple-element.418), channel_id=1, source_target_pairs={{0,0},{1,1},{2,4},{3,5},{4,2},{5,3},{6,6},{7,7},{8,8},{9,9},{10,12... | collective-permute-start | bytes 1769480 | tf_op jit(solution)/shard_map/ppermute | solution.py:175
  337.6 25.6 %collective-permute-start.32 = (bf16[288,1024]{1,0:T(8,128)(2,1)}, bf16[288,1024]{1,0:T(8,128)(2,1)}, u32[]{:S(2)}, u32[]{:S(2)}) collective-permute-start(bf16[288,1024]{1,0:T(8,128)(2,1)} %slice.202), channel_id=1, source_target_pairs={{0,1},{1,0},{2,3},{3,2},{4,5},{5,4},{6,7},{7,6},{8,9},{9,8},{10,11... | collective-permute-start | bytes 1769480 | tf_op jit(solution)/shard_map/ppermute | solution.py:175
  343.7 19.5 %collective-permute-start.30 = (bf16[4,72,1024]{2,1,0:T(8,128)(2,1)}, bf16[4,72,1024]{2,1,0:T(8,128)(2,1)S(1)}, u32[]{:S(2)}, u32[]{:S(2)}) collective-permute-start(bf16[4,72,1024]{2,1,0:T(8,128)(2,1)} %get-tuple-element.270), channel_id=1, source_target_pairs={{0,2},{1,3},{2,0},{3,1},{4,6},{5,7},{6,4},{7,5},{8,10},{9,11},{10,... | collective-permute-start | bytes 1769480 | tf_op jit(solution)/shard_map/ppermute | solution.py:175
  343.7 28.7 %collective-permute-start.33 = (bf16[288,1152]{1,0:T(8,128)(2,1)}, bf16[288,1152]{1,0:T(8,128)(2,1)S(1)}, u32[]{:S(2)}, u32[]{:S(2)}) collective-permute-start(bf16[288,1152]{1,0:T(8,128)(2,1)} %slice.203), channel_id=1, source_target_pairs={{0,2},{1,3},{2,0},{3,1},{4,6},{5,7},{6,4},{7,5},{8,10},{9,11},{10,... | collective-permute-start | bytes 1990664 | tf_op jit(solution)/shard_map/ppermute | solution.py:175
  345.7 26.7 %collective-permute-start.31 = (bf16[4,72,1152]{2,1,0:T(8,128)(2,1)}, bf16[4,72,1152]{2,1,0:T(8,128)(2,1)S(1)}, u32[]{:S(2)}, u32[]{:S(2)}) collective-permute-start(bf16[4,72,1152]{2,1,0:T(8,128)(2,1)} %get-tuple-element.271), channel_id=1, source_target_pairs={{0,1},{1,0},{2,3},{3,2},{4,5},{5,4},{6,7},{7,6},{8,9},{9,8},{10,11... | collective-permute-start | bytes 1990664 | tf_op jit(solution)/shard_map/ppermute | solution.py:175
  374.3 41.2 %all-to-all-start.3 = ((bf16[4,72,2176]{2,1,0:T(8,128)(2,1)}), bf16[4,72,2176]{2,1,0:T(8,128)(2,1)}, u32[]{:S(2)}, u32[]{:S(2)}) async-start(bf16[4,72,2176]{2,1,0:T(8,128)(2,1)} %shard_map.182), calls=%async_computation.4 | async-start | bytes 2506752 | tf_op jit(solution)/shard_map/all_to_all | solution.py:193
  379.2 30.2 %collective-permute-start.34 = (bf16[2,4,72,1152]{3,2,1,0:T(8,128)(2,1)}, bf16[2,4,72,1152]{3,2,1,0:T(8,128)(2,1)S(1)}, u32[]{:S(2)}, u32[]{:S(2)}) collective-permute-start(bf16[2,4,72,1152]{3,2,1,0:T(8,128)(2,1)} %get-tuple-element.287), channel_id=1, source_target_pairs={{0,1},{1,0},{2,3},{3,2},{4,5},{5,4},{6,7},{7,6},{8,9},{9,8},{10,11... | collective-permute-start | bytes 3981320 | tf_op jit(solution)/shard_map/ppermute | solution.py:175
  380.0 35.4 %collective-permute-start.35 = (bf16[2,4,72,1280]{3,2,1,0:T(8,128)(2,1)}, bf16[2,4,72,1280]{3,2,1,0:T(8,128)(2,1)S(1)}, u32[]{:S(2)}, u32[]{:S(2)}) collective-permute-start(bf16[2,4,72,1280]{3,2,1,0:T(8,128)(2,1)} %get-tuple-element.288), channel_id=1, source_target_pairs={{0,2},{1,3},{2,0},{3,1},{4,6},{5,7},{6,4},{7,5},{8,10},{9,11},{10,... | collective-permute-start | bytes 4423688 | tf_op jit(solution)/shard_map/ppermute | solution.py:175
  390.1 3.0 collective-permute-start.36
  392.6 35.5 %collective-permute-start.42 = (bf16[288,1024]{1,0:T(8,128)(2,1)}, bf16[288,1024]{1,0:T(8,128)(2,1)}, u32[]{:S(2)}, u32[]{:S(2)}) collective-permute-start(bf16[288,1024]{1,0:T(8,128)(2,1)} %add_convert_fusion.7), channel_id=1, source_target_pairs={{0,2},{1,3},{2,0},{3,1},{4,6},{5,7},{6,4},{7,5},{8,10},{9,11},{10,... | collective-permute-start | bytes 1769480 | tf_op jit(solution)/shard_map/ppermute | solution.py:175
  420.2 36.2 %collective-permute-start.40 = (bf16[4,72,1280]{2,1,0:T(8,128)(2,1)}, bf16[4,72,1280]{2,1,0:T(8,128)(2,1)S(1)}, u32[]{:S(2)}, u32[]{:S(2)}) collective-permute-start(bf16[4,72,1280]{2,1,0:T(8,128)(2,1)} %get-tuple-element.302), channel_id=1, source_target_pairs={{0,1},{1,0},{2,3},{3,2},{4,5},{5,4},{6,7},{7,6},{8,9},{9,8},{10,11... | collective-permute-start | bytes 2211848 | tf_op jit(solution)/shard_map/ppermute | solution.py:175
  422.8 30.4 %collective-permute-start.43 = (bf16[288,1152]{1,0:T(8,128)(2,1)S(1)}, bf16[288,1152]{1,0:T(8,128)(2,1)}, u32[]{:S(2)}, u32[]{:S(2)}) collective-permute-start(bf16[288,1152]{1,0:T(8,128)(2,1)S(1)} %add_convert_fusion.5), channel_id=1, source_target_pairs={{0,1},{1,0},{2,3},{3,2},{4,5},{5,4},{6,7},{7,6},{8,9},{9,8},{10,11... | collective-permute-start | bytes 1990664 | tf_op jit(solution)/shard_map/ppermute | solution.py:175
  423.6 32.8 %collective-permute-start.39 = (bf16[4,72,1152]{2,1,0:T(8,128)(2,1)}, bf16[4,72,1152]{2,1,0:T(8,128)(2,1)S(1)}, u32[]{:S(2)}, u32[]{:S(2)}) collective-permute-start(bf16[4,72,1152]{2,1,0:T(8,128)(2,1)} %get-tuple-element.301), channel_id=1, source_target_pairs={{0,2},{1,3},{2,0},{3,1},{4,6},{5,7},{6,4},{7,5},{8,10},{9,11},{10,... | collective-permute-start | bytes 1990664 | tf_op jit(solution)/shard_map/ppermute | solution.py:175
  426.9 27.5 %collective-permute-start.38 = (bf16[72,2176]{1,0:T(8,128)(2,1)S(1)}, bf16[72,2176]{1,0:T(8,128)(2,1)S(1)}, u32[]{:S(2)}, u32[]{:S(2)}) collective-permute-start(bf16[72,2176]{1,0:T(8,128)(2,1)S(1)} %reduce_sum.64.refs_0_), channel_id=1, source_target_pairs={{0,2},{1,3},{2,0},{3,1},{4,6},{5,7},{6,4},{7,5},{8,10},{9,11},{10,... | collective-permute-start | bytes 940040 | tf_op jit(solution)/shard_map/ppermute | solution.py:175
  428.2 28.2 %collective-permute-start.37 = (bf16[72,2176]{1,0:T(8,128)(2,1)S(1)}, bf16[72,2176]{1,0:T(8,128)(2,1)S(1)}, u32[]{:S(2)}, u32[]{:S(2)}) collective-permute-start(bf16[72,2176]{1,0:T(8,128)(2,1)S(1)} %reduce_sum.64.refs_0_), channel_id=1, source_target_pairs={{0,1},{1,0},{2,3},{3,2},{4,5},{5,4},{6,7},{7,6},{8,9},{9,8},{10,11... | collective-permute-start | bytes 940040 | tf_op jit(solution)/shard_map/ppermute | solution.py:175
  460.4 36.6 %all-to-all-start.4 = ((bf16[4,72,2432]{2,1,0:T(8,128)(2,1)}), bf16[4,72,2432]{2,1,0:T(8,128)(2,1)}, u32[]{:S(2)}, u32[]{:S(2)}) async-start(bf16[4,72,2432]{2,1,0:T(8,128)(2,1)} %shard_map.185), calls=%async_computation.5 | async-start | bytes 2801664 | tf_op jit(solution)/shard_map/all_to_all | solution.py:193
  468.3 22.3 %collective-permute-start.51 = (bf16[144,2176]{1,0:T(8,128)(2,1)S(1)}, bf16[144,2176]{1,0:T(8,128)(2,1)S(1)}, u32[]{:S(2)}, u32[]{:S(2)}) collective-permute-start(bf16[144,2176]{1,0:T(8,128)(2,1)S(1)} %get-tuple-element.404), channel_id=1, source_target_pairs={{0,4},{1,5},{2,6},{3,7},{4,0},{5,1},{6,2},{7,3},{8,12},{9,13},{10,... | collective-permute-start | bytes 1880072 | tf_op jit(solution)/shard_map/ppermute | solution.py:175
  469.5 15.7 %collective-permute-start.50 = (bf16[256,1152]{1,0:T(8,128)(2,1)S(1)}, bf16[256,1152]{1,0:T(8,128)(2,1)S(1)}, u32[]{:S(2)}, u32[]{:S(2)}) collective-permute-start(bf16[256,1152]{1,0:T(8,128)(2,1)S(1)} %get-tuple-element.415), channel_id=1, source_target_pairs={{0,1},{1,0},{2,5},{3,4},{4,3},{5,2},{6,7},{7,6},{8,9},{9,8},{10,13... | collective-permute-start | bytes 1769480 | tf_op jit(solution)/shard_map/ppermute | solution.py:175
  470.9 17.7 %collective-permute-start.49 = (bf16[256,1152]{1,0:T(8,128)(2,1)S(1)}, bf16[256,1152]{1,0:T(8,128)(2,1)S(1)}, u32[]{:S(2)}, u32[]{:S(2)}) collective-permute-start(bf16[256,1152]{1,0:T(8,128)(2,1)S(1)} %get-tuple-element.416), channel_id=1, source_target_pairs={{0,0},{1,1},{2,4},{3,5},{4,2},{5,3},{6,6},{7,7},{8,8},{9,9},{10,12... | collective-permute-start | bytes 1769480 | tf_op jit(solution)/shard_map/ppermute | solution.py:175
  471.6 22.7 %collective-permute-start.45 = (bf16[72,1152]{1,0:T(8,128)(2,1)S(1)}, bf16[72,1152]{1,0:T(8,128)(2,1)S(1)}, u32[]{:S(2)}, u32[]{:S(2)}) collective-permute-start(bf16[72,1152]{1,0:T(8,128)(2,1)S(1)} %slice.212), channel_id=1, source_target_pairs={{0,2},{1,3},{2,0},{3,1},{4,6},{5,7},{6,4},{7,5},{8,10},{9,11},{10,... | collective-permute-start | bytes 497672 | tf_op jit(solution)/shard_map/ppermute | solution.py:175
  475.8 18.5 %collective-permute-start.44 = (bf16[72,1024]{1,0:T(8,128)(2,1)S(1)}, bf16[72,1024]{1,0:T(8,128)(2,1)S(1)}, u32[]{:S(2)}, u32[]{:S(2)}) collective-permute-start(bf16[72,1024]{1,0:T(8,128)(2,1)S(1)} %slice.211), channel_id=1, source_target_pairs={{0,1},{1,0},{2,3},{3,2},{4,5},{5,4},{6,7},{7,6},{8,9},{9,8},{10,11... | collective-permute-start | bytes 442376 | tf_op jit(solution)/shard_map/ppermute | solution.py:175
  485.2 8.5 %collective-permute-start.48 = (f32[18,128]{1,0:T(8,128)S(1)}, f32[18,128]{1,0:T(8,128)S(1)}, u32[]{:S(2)}, u32[]{:S(2)}) collective-permute-start(f32[18,128]{1,0:T(8,128)S(1)} %add.289), channel_id=1, source_target_pairs={{0,3},{1,2},{2,1},{3,0},{4,7},{5,6},{6,5},{7,4},{8,11},{9,10},{10,... | collective-permute-start | bytes 27656 | tf_op jit(solution)/shard_map/ppermute | solution.py:175
  488.6 5.2 collective-permute-start.47
  490.6 3.8 collective-permute-start.46
  498.6 13.2 %collective-permute-start.54 = (bf16[72,2432]{1,0:T(8,128)(2,1)S(1)}, bf16[72,2432]{1,0:T(8,128)(2,1)S(1)}, u32[]{:S(2)}, u32[]{:S(2)}) collective-permute-start(bf16[72,2432]{1,0:T(8,128)(2,1)S(1)} %reduce_sum.65.refs_0_), channel_id=1, source_target_pairs={{0,2},{1,3},{2,0},{3,1},{4,6},{5,7},{6,4},{7,5},{8,10},{9,11},{10,... | collective-permute-start | bytes 1050632 | tf_op jit(solution)/shard_map/ppermute | solution.py:175
  500.4 11.4 %collective-permute-start.53 = (bf16[72,2432]{1,0:T(8,128)(2,1)S(1)}, bf16[72,2432]{1,0:T(8,128)(2,1)S(1)}, u32[]{:S(2)}, u32[]{:S(2)}) collective-permute-start(bf16[72,2432]{1,0:T(8,128)(2,1)S(1)} %reduce_sum.65.refs_0_), channel_id=1, source_target_pairs={{0,1},{1,0},{2,3},{3,2},{4,5},{5,4},{6,7},{7,6},{8,9},{9,8},{10,11... | collective-permute-start | bytes 1050632 | tf_op jit(solution)/shard_map/ppermute | solution.py:175
  502.4 9.4 %collective-permute-start.52 = (bf16[2,72,2176]{2,1,0:T(8,128)(2,1)S(1)}, bf16[2,72,2176]{2,1,0:T(8,128)(2,1)S(1)}, u32[]{:S(2)}, u32[]{:S(2)}) collective-permute-start(bf16[2,72,2176]{2,1,0:T(8,128)(2,1)S(1)} %shard_map.187), channel_id=1, source_target_pairs={{0,4},{1,5},{2,6},{3,7},{4,0},{5,1},{6,2},{7,3},{8,12},{9,13},{10,... | collective-permute-start | bytes 1880072 | tf_op jit(solution)/shard_map/ppermute | solution.py:175
  502.5 5.6 %collective-permute-start.57 = (f32[18,128]{1,0:T(8,128)S(1)}, f32[18,128]{1,0:T(8,128)S(1)}, u32[]{:S(2)}, u32[]{:S(2)}) collective-permute-start(f32[18,128]{1,0:T(8,128)S(1)} %add_add_fusion.2), channel_id=1, source_target_pairs={{0,24},{1,25},{2,26},{3,27},{4,28},{5,29},{6,30},{7,31},{8,16},{9,... | collective-permute-start | bytes 27656 | tf_op jit(solution)/shard_map/ppermute | solution.py:175
  506.9 4.6 collective-permute-start.56
  508.1 3.7 collective-permute-start.55
  511.8 5.8 %collective-permute-start.59 = (bf16[72,1280]{1,0:T(8,128)(2,1)S(1)}, bf16[72,1280]{1,0:T(8,128)(2,1)S(1)}, u32[]{:S(2)}, u32[]{:S(2)}) collective-permute-start(bf16[72,1280]{1,0:T(8,128)(2,1)S(1)} %slice.216), channel_id=1, source_target_pairs={{0,2},{1,3},{2,0},{3,1},{4,6},{5,7},{6,4},{7,5},{8,10},{9,11},{10,... | collective-permute-start | bytes 552968 | tf_op jit(solution)/shard_map/ppermute | solution.py:175
  512.2 5.4 %collective-permute-start.58 = (bf16[72,1152]{1,0:T(8,128)(2,1)S(1)}, bf16[72,1152]{1,0:T(8,128)(2,1)S(1)}, u32[]{:S(2)}, u32[]{:S(2)}) collective-permute-start(bf16[72,1152]{1,0:T(8,128)(2,1)S(1)} %slice.215), channel_id=1, source_target_pairs={{0,1},{1,0},{2,3},{3,2},{4,5},{5,4},{6,7},{7,6},{8,9},{9,8},{10,11... | collective-permute-start | bytes 497672 | tf_op jit(solution)/shard_map/ppermute | solution.py:175
  519.1 2.4 collective-permute-start.60
  (92 other events, 644.7 us)
Sparse Core Ops, SparseCore 0:
  228.3 90.4 reduce-scatter.1
